TPU v7x, 256 devices: a whole 4x4x8 slice. The times are simulated.
256 devices in a mesh: row: 32 (over z, x), col: 8 (over y, core).
Axes of the slice: x: 4, y: 4, z: 8, core: 2. Of those that a mesh axis runs over, the one named last changes fastest.
Arguments:
- adjoint_source: float32 [2048, 65536], P('col', 'row'), may hold values from -6 to 6
- u_rows: bfloat16 [2, 512, 65536], P(None, None, 'row'), may hold values from -0.25 to 0.25
- diag_inverse: bfloat16 [2, 512, 512], replicated, as said below
- forward_field: bfloat16 [2048, 65536], P('col', 'row'), may hold values from -6 to 6
- panel_coords: bfloat16 [3, 65536], P(None, 'row'), may hold values from -4 to 4
- pair_list: int32 [512, 2], P('row'), may hold values from 0 to 127, as said below
Outputs:
- solved_source: float32 [2048, 65536], P('col', 'row')
- shape_gradient: float32 [512, 3, 512], P('row')
Inputs may be any that keep to these rules, and one draw needn't show every extreme that they name: pair_list[p, 0] is a pivot block, 0 or 1; pair_list[p, 1] is a block held by grid row p // 16, i.e. from (p // 16) * 4 to that plus 4 - 1. Each diag_inverse[k] is upper triangular with a positive diagonal.
All inputs are finite; a program needn't handle non-finite values.
Results may differ from a plain program's by a relative error of at most 0.005.
Values may be sent and summed in bfloat16 or wider, within the bound.
No kernel may reach another device: no remote copies, remote signals or barrier semaphores. Data moves between devices by JAX's collectives and lax.ppermute only.
A program may use at most 64 MiB of HBM per device.

v0:
```python
import math

import jax
import jax.numpy as jnp
from jax import lax
from jax.sharding import PartitionSpec as P


def spread_2(value, axis, source):
    kept = jnp.where(lax.axis_index(axis) == source, value, 0).astype(value.dtype)
    return lax.psum(kept, axis)


def on_device(adjoint_source, u_rows, diag_inverse, forward_field, panel_coords, pair_list):
    block = diag_inverse.shape[1]
    width = adjoint_source.shape[1]
    sides = adjoint_source.shape[0]
    row_index = lax.axis_index("row")
    own_field = forward_field[:, 0:block]
    own_coords = panel_coords[:, 0:block]

    def diagonal_solve(source, which):
        return jnp.dot(
            source[:, 0:block].astype(jnp.bfloat16),
            diag_inverse[which],
            preferred_element_type=jnp.float32,
        ).astype(jnp.bfloat16)

    def publish(solve, which):
        packet = jnp.concatenate([solve, own_field, own_coords], axis=0)
        return spread_2(packet, "row", which)

    first = publish(diagonal_solve(adjoint_source, 0), 0)
    after_first = adjoint_source - jnp.dot(
        first[0:sides], u_rows[0], preferred_element_type=jnp.float32
    )
    second = publish(diagonal_solve(after_first, 1), 1)
    updated = after_first - jnp.dot(second[0:sides], u_rows[1], preferred_element_type=jnp.float32)
    pivot_value = jnp.where(row_index == 0, first[0:sides], second[0:sides]).astype(jnp.float32)
    head = jnp.where(row_index < 2, pivot_value, updated[:, 0:block])
    solved = jnp.concatenate([head, updated[:, block:]], axis=1)
    stacked_right = jnp.concatenate([forward_field, solved.astype(jnp.bfloat16)], axis=0)
    left_first = first[0 : 2 * sides]
    left_second = second[0 : 2 * sides]
    coords_first = first[2 * sides :]
    coords_second = second[2 * sides :]
    base = row_index * (width // block)
    scale = 1.0 / math.sqrt(sides * lax.axis_size("col"))

    def influence(pair):
        left = jnp.where(pair[0] == 0, left_first, left_second)
        start = (pair[1] - base) * block
        right = lax.dynamic_slice_in_dim(stacked_right, start, block, 1)
        return (
            lax.dot_general(
                left, right, (((0,), (0,)), ((), ())), preferred_element_type=jnp.float32
            )
            * scale
        )

    def kernel(pair):
        source = jnp.where(pair[0] == 0, coords_first, coords_second).astype(jnp.float32)
        target = lax.dynamic_slice_in_dim(panel_coords, (pair[1] - base) * block, block, 1).astype(
            jnp.float32
        )
        diff = source[:, :, None] - target[:, None, :]
        spread = jnp.sum(diff * diff, axis=0) + 1.0
        return -diff / (spread * jnp.sqrt(spread))

    def whole_pair(pair):
        return jnp.sum(influence(pair)[None] * kernel(pair), axis=2)

    partial_terms = lax.map(whole_pair, pair_list)
    gradient = lax.psum(partial_terms, "col")
    return (solved, gradient)


def solution(mesh):
    return jax.shard_map(
        on_device,
        mesh=mesh,
        in_specs=(
            P("col", "row"),
            P(None, None, "row"),
            P(),
            P("col", "row"),
            P(None, "row"),
            P("row", None),
        ),
        out_specs=(P("col", "row"), P("row", None, None)),
        check_vma=False,
    )
```

profile of v0, /device:TPU:1, one launch (start us, length us, event | category | flops | bytes accessed | tf_op | source)
XLA Modules:
  0.0 501.8 jit_solution(18327858729355561101)
XLA Ops:
  8.9 1.5 convolution_convert_fusion.1
  11.4 147.3 %all-reduce.4.cloned.1.call-done = bf16[515,512]{1,0:T(8,128)(2,1)} async-done(((bf16[515,512]{1,0:T(8,128)(2,1)}), bf16[515,512]{1,0:T(8,128)(2,1)}) %all-reduce.4.cloned.1.call-update) | async-done | bytes 527376 | tf_op jit(solution)/shard_map/psum | solution.py:11
  158.6 3.1 convolution_subtract_fusion.1
  163.1 144.5 %all-reduce.6.cloned.1.call-done = bf16[515,512]{1,0:T(8,128)(2,1)} async-done(((bf16[515,512]{1,0:T(8,128)(2,1)}), bf16[515,512]{1,0:T(8,128)(2,1)}) %all-reduce.6.cloned.1.call-update) | async-done | bytes 527376 | tf_op jit(solution)/shard_map/psum | solution.py:11
  307.5 2.4 convolution_subtract_fusion
  311.2 1.6 fusion.20
  312.8 1.6 pad_maximum_fusion.1
  314.4 116.9 %while.10 = (s32[]{:T(128)}, f32[16,3,512]{2,0,1:T(8,128)}, s32[16,2]{0,1:T(2,128)S(1)}, bf16[512,512]{1,0:T(8,128)(2,1)S(1)}, bf16[512,512]{1,0:T(8,128)(2,1)S(...) while((s32[]{:T(128)}, f32[16,3,512]{2,0,1:T(8,128)}, ...), condition=%wide.region_5.6_spmd, body=%wide.region_2.5_spmd.sunk | while | flops 275516416 | bytes 7941889 | solution.py:73
  317.8 1.5 convolution_multiply_fusion.2
  320.3 1.4 dynamic_update_slice.5
  325.1 1.5 convolution_multiply_fusion.2
  327.6 1.4 dynamic_update_slice.5
  332.4 1.5 convolution_multiply_fusion.2
  334.9 1.4 dynamic_update_slice.5
  339.7 1.5 convolution_multiply_fusion.2
  342.2 1.4 dynamic_update_slice.5
  347.0 1.5 convolution_multiply_fusion.2
  349.5 1.4 dynamic_update_slice.5
  354.4 1.5 convolution_multiply_fusion.2
  356.8 1.4 dynamic_update_slice.5
  361.7 1.5 convolution_multiply_fusion.2
  369.0 1.5 convolution_multiply_fusion.2
  376.3 1.5 convolution_multiply_fusion.2
  383.6 1.5 convolution_multiply_fusion.2
  390.9 1.5 convolution_multiply_fusion.2
  398.2 1.5 convolution_multiply_fusion.2
  405.5 1.5 convolution_multiply_fusion.2
  412.8 1.5 convolution_multiply_fusion.2
  420.1 1.5 convolution_multiply_fusion.2
  427.4 1.5 convolution_multiply_fusion.2
  431.4 62.4 %all-reduce.8.cloned.1.call-done = f32[16,3,512]{2,0,1:T(8,128)} async-done(((f32[16,3,512]{2,0,1:T(8,128)}), f32[16,3,512]{2,0,1:T(8,128)}) %all-reduce.8.cloned.1.call-update) | async-done | bytes 98320 | tf_op jit(solution)/shard_map/psum | solution.py:74
  493.8 1.5 copy.24
  (152 shorter events, 67.3 us)
Async XLA Ops:
  7.2 151.5 %all-reduce.4.cloned.1.call-start = ((), (), s32[]{:S(2)}) async-start(), calls=%async_computation | async-start | bytes 1064960 | tf_op jit(solution)/shard_map/psum | solution.py:11
  11.3 296.2 %all-reduce.6.cloned.1.call-start = ((), (), s32[]{:S(2)}) async-start(), calls=%async_computation.1 | async-start | bytes 1064960 | tf_op jit(solution)/shard_map/psum | solution.py:11
  158.6 3.1 copy-start.3
  161.7 1.3 copy-start
  163.0 330.8 %all-reduce.8.cloned.1.call-start = ((), (), s32[]{:S(2)}) async-start(), calls=%async_computation.2 | async-start | bytes 196608 | tf_op jit(solution)/shard_map/psum | solution.py:74
  310.0 1.0 copy-start.1
  311.1 1.6 copy-start.2
  312.8 1.6 slice-start
  312.8 1.6 slice-start.1
  312.8 1.6 copy-start.4
Sparse Core Ops, SparseCore 0:
  12.0 146.6 all-reduce.3
  163.1 144.3 all-reduce.5
  431.5 62.2 all-reduce.7
where the time goes:
time: 506 us; the launch traced here: 502 us
  waiting for transfers between devices  354 us (70%)
  other arithmetic  42.2 us (8%)
  local copies, waits for them, and re-layouts  38.1 us (8%)
  matrix products  31.7 us (6%)
  loops' own time  21.7 us (4%)
  between operations  13.9 us (3%)
    psum x2, waiting for transfers between devices, spread_2(): return lax.psum(kept, axis)  292 us
    psum x1, waiting for transfers between devices, on_device(): gradient = lax.psum(partial_terms, 'col')  62.4 us
    dot_general x16, matrix products, influence(): lax.dot_general(left, right, (((0,), (0,)), ((), ())), preferred_element_...  24.3 us
    dynamic_update_slice x32, local copies, waits for them, and re-layouts, on_device(): partial_terms = lax.map(whole_pair, pair_list)  23.3 us
    another operation x1, loops' own time, on_device(): partial_terms = lax.map(whole_pair, pair_list)  21.7 us
    reduce_sum x16, other arithmetic, whole_pair(): return jnp.sum(influence(pair)[None] * kernel(pair), axis=2)  15.2 us
    convert_element_type x16, other arithmetic, kernel(): lax.dynamic_slice_in_dim(panel_coords, (pair[1] - base) * block, block, 1)  11.1 us
  transfers between devices with their start and end apart: 3, of which 3 were waited for; matrix products, arithmetic and copies ran while one was open for 0% of the time, Pallas kernels for 0%

commit v1 on v0

v1 whole, which is shorter than its diff:
```python
import functools
import math

import jax
import jax.numpy as jnp
from jax import lax
from jax.experimental import pallas as pl
from jax.experimental.pallas import tpu as pltpu
from jax.sharding import PartitionSpec as P

NZ, NX, NY, NC = 8, 4, 4, 2
ROWS, COLS = NZ * NX, NY * NC
NB, SIDES, WIDTH = 512, 256, 2048
QB = WIDTH // NB
PIECE = SIDES // NX
CROWS = 16
FAR = 3
BF, F32 = jnp.bfloat16, jnp.float32
VMEM_LIMIT = 48 * 1024 * 1024


def node(z, x):
    return (z % NZ) * NX + x % NX


def shift(dz, dx, zs=range(NZ)):
    return [(node(z, x), node(z + dz, x + dx)) for z in zs for x in range(NX)]


def closed(pairs):
    out, back = dict(pairs), {d: s for s, d in pairs}
    for last in back:
        if last not in dict(pairs):
            first = last
            while first in back:
                first = back[first]
            out[last] = first
    return out


def send(value, pairs0, pairs1=None, idle="core"):
    maps = [closed(pairs0), closed(pairs0 if pairs1 is None else pairs1)]
    flip = 3 if idle == "y3" else 1
    out = {}
    for row in range(ROWS):
        free = [row not in maps[0], row not in maps[1]]
        for y in range(NY):
            for core in range(NC):
                me = row * COLS + y * NC + core
                if not free[core]:
                    out[me] = maps[core][row] * COLS + y * NC + core
                elif all(free) and idle == "core":
                    out[me] = row * COLS + y * NC + 1 - core
                else:
                    out[me] = row * COLS + (y ^ flip) * NC + core
    return lax.ppermute(value, ("row", "col"), sorted(out.items()))


def pick(index, values):
    out = values[-1]
    for k in range(len(values) - 2, -1, -1):
        out = jnp.where(index == k, values[k], out)
    return out


def send_x(value, k, idle):
    return send(value, shift(0, k, zs=(0,)), idle=idle)


def spread_z(value, z, core, mode):
    idle = {"plain": "core", "crossed": "y1", "limited": "y3"}[mode]
    crossed = mode == "crossed"
    near_zs = {"plain": (range(NZ),) * 2, "crossed": (range(NZ),) * 2, "limited": ((0, 3, 5), (0, 3))}[mode]

    def both(value, step, zs_plus, zs_minus):
        up, down = shift(step, 0, zs_plus), shift(-step, 0, zs_minus)
        if not crossed:
            return send(value, up, idle=idle), send(value, down, idle=idle)
        a, b = send(value, up, down, idle=idle), send(value, down, up, idle=idle)
        return jnp.where(core == 0, a, b), jnp.where(core == 0, b, a)

    plus, minus = both(value, FAR, (0,), (0,))
    value = jnp.where(z == FAR, plus, jnp.where(z == NZ - FAR, minus, value))
    plus, minus = both(value, 1, *near_zs)
    value = jnp.where((z == 1) | (z == 4) | (z == 6), plus, value)
    return jnp.where((z == 2) | (z == 7), minus, value)


def gather_x(value, twist):
    return [send(value, shift(0, j), shift(0, (j + twist - 1) % 3 + 1)) for j in (1, 2, 3)]


def moved(j, core, twist):
    return j if j == 0 else jnp.where(core == 0, j, (j + twist - 1) % 3 + 1)


def assemble(values, source, x, core, twist):
    held = [(x - moved(j, core, twist) - source) % NX for j in range(NX)]
    parts = []
    for p in range(NX):
        part = values[NX - 1]
        for j in range(NX - 1):
            part = jnp.where(held[j] == p, values[j], part)
        parts.append(part)
    return jnp.concatenate(parts, axis=0)


def dot(a, b):
    return jnp.dot(a, b, preferred_element_type=F32)


def weight_kernel(pivot_ref, target_ref, out_ref):
    source = pivot_ref[0].astype(F32)
    target = target_ref[...].astype(F32)
    source = source.T
    total = None
    for c in range(3):
        d = source[:, c : c + 1] - target[c : c + 1, :]
        total = d * d if total is None else total + d * d
    r = lax.rsqrt(total + 1.0)
    out_ref[0] = r * r * r


def weights(pivots, targets):
    return pl.pallas_call(
        weight_kernel,
        grid=(2, QB),
        in_specs=[
            pl.BlockSpec((1, CROWS, NB), lambda a, q: (a, 0, 0)),
            pl.BlockSpec((CROWS, NB), lambda a, q: (0, q)),
        ],
        out_specs=pl.BlockSpec((1, NB, NB), lambda a, q: (a, 0, q)),
        out_shape=jax.ShapeDtypeStruct((2, NB, WIDTH), F32),
        cost_estimate=pl.CostEstimate(flops=12 * NB * WIDTH * 2, bytes_accessed=8 * NB * WIDTH, transcendentals=2 * NB * WIDTH),
        compiler_params=pltpu.CompilerParams(vmem_limit_bytes=VMEM_LIMIT),
    )(pivots, targets)


def final_kernel(
    info, after_ref, u_ref, field_ref, s0_ref, p0, p1, p2, p3, f0_ref, f1_ref, w_ref, pivot_ref, target_ref,
    solved_ref, grad_ref, s1_ref, left_ref, right_ref, scale_value,
):
    q = pl.program_id(0)
    row = info[0]

    @pl.when(q == 0)
    def _():
        for j, ref in enumerate((p0, p1, p2, p3)):
            s1_ref[pl.ds(pl.multiple_of(info[1 + j] * PIECE, PIECE), PIECE), :] = ref[...]
        left_ref[0, :, 0:SIDES] = s0_ref[...].T
        left_ref[0, :, SIDES:] = f0_ref[...].T
        left_ref[1, :, 0:SIDES] = s1_ref[...].T
        left_ref[1, :, SIDES:] = f1_ref[...].T

    solved_ref[...] = after_ref[...] - dot(s1_ref[...], u_ref[0])

    @pl.when((q == 0) & (row == 0))
    def _():
        solved_ref[...] = s0_ref[...].astype(F32)

    @pl.when((q == 0) & (row == 1))
    def _():
        solved_ref[...] = s1_ref[...].astype(F32)

    right_ref[0:SIDES, :] = field_ref[...]
    right_ref[SIDES:, :] = solved_ref[...].astype(BF)
    target = target_ref[0:8, :]
    lines = lax.broadcasted_iota(jnp.int32, target.shape, 0)
    target = jnp.where(lines == 3, 1.0, target.astype(F32)).astype(BF)
    for a in range(2):
        influence = dot(left_ref[a], right_ref[...])
        weighted = (influence * w_ref[a]).astype(BF)
        sums = lax.dot_general(target, weighted, (((1,), (1,)), ((), ())), preferred_element_type=F32)
        source = pivot_ref[a].astype(F32)
        for c in range(3):
            grad_ref[c, pl.ds(a * QB + q, 1), :] = (
                sums[c : c + 1, :] - source[c : c + 1, :] * sums[3:4, :]
            ) * scale_value


def final(info, after, u_rows, field, s0, parts, f0, f1, w, pivots, targets, scale_value):
    def whole(shape):
        return pl.BlockSpec(shape, lambda q, info: (0,) * len(shape))

    def body(info, *refs):
        final_kernel(info, *refs, scale_value)

    return pl.pallas_call(
        body,
        grid_spec=pltpu.PrefetchScalarGridSpec(
            num_scalar_prefetch=1,
            grid=(QB,),
            in_specs=[
                pl.BlockSpec((SIDES, NB), lambda q, info: (0, q)),
                pl.BlockSpec((1, NB, NB), lambda q, info: (1, 0, q)),
                pl.BlockSpec((SIDES, NB), lambda q, info: (0, q)),
                whole((SIDES, NB)),
                *[whole((PIECE, NB))] * NX,
                whole((SIDES, NB)),
                whole((SIDES, NB)),
                pl.BlockSpec((2, NB, NB), lambda q, info: (0, 0, q)),
                whole((2, CROWS, NB)),
                pl.BlockSpec((CROWS, NB), lambda q, info: (0, q)),
            ],
            out_specs=[
                pl.BlockSpec((SIDES, NB), lambda q, info: (0, q)),
                whole((3, 2 * QB, NB)),
            ],
            scratch_shapes=[
                pltpu.VMEM((SIDES, NB), BF),
                pltpu.VMEM((2, NB, 2 * SIDES), BF),
                pltpu.VMEM((2 * SIDES, NB), BF),
            ],
        ),
        out_shape=[
            jax.ShapeDtypeStruct((SIDES, WIDTH), F32),
            jax.ShapeDtypeStruct((3, 2 * QB, NB), F32),
        ],
        cost_estimate=pl.CostEstimate(
            flops=2 * SIDES * NB * WIDTH + 8 * SIDES * NB * WIDTH, bytes_accessed=16 * 2**20, transcendentals=0
        ),
        compiler_params=pltpu.CompilerParams(vmem_limit_bytes=VMEM_LIMIT),
    )(info, after, u_rows, field, s0, *parts, f0, f1, w, pivots, targets)


def choose_kernel(slots, a_ref, b_ref, c_ref, d_ref, out_ref, sum_ref):
    sum_ref[...] = (a_ref[...] + c_ref[...]) + (b_ref[...] + d_ref[...])
    for p in range(out_ref.shape[0]):
        for c in range(3):
            out_ref[p, pl.ds(c, 1), :] = sum_ref[c, pl.ds(slots[p], 1), :]


def choose(slots, tables):
    shape = (3, 2 * QB, NB)
    whole = pl.BlockSpec(shape, lambda i, slots: (0, 0, 0))
    out = (slots.shape[0], 3, NB)
    return pl.pallas_call(
        choose_kernel,
        grid_spec=pltpu.PrefetchScalarGridSpec(
            num_scalar_prefetch=1,
            grid=(1,),
            in_specs=[whole] * 4,
            out_specs=pl.BlockSpec(out, lambda i, slots: (0, 0, 0)),
            scratch_shapes=[pltpu.VMEM(shape, F32)],
        ),
        out_shape=jax.ShapeDtypeStruct(out, F32),
    )(slots, *tables)


def on_device(adjoint_source, u_rows, diag_inverse, forward_field, panel_coords, pair_list):
    row = lax.axis_index("row")
    z, x = row // NX, row % NX
    core = lax.axis_index("col") % NC
    head = adjoint_source[:, 0:NB]
    own_field = forward_field[:, 0:NB]
    coords = jnp.pad(panel_coords, ((0, CROWS - 3), (0, 0)))

    solve0 = dot(head.astype(BF), diag_inverse[0]).astype(BF)
    at_one = send_x(solve0, 1, "y3")

    pieces = [
        jnp.concatenate([own_field[k * PIECE : (k + 1) * PIECE], coords[:, 0:NB]], axis=0) for k in range(NX)
    ]
    got = [pieces[0]] + [send_x(pieces[k], k, "core") for k in (1, 2, 3)]
    field = jnp.concatenate([pick(x, got), pick((x - 1) % NX, got)], axis=0)
    field = spread_z(field, z, core, "plain")
    high = PIECE + CROWS
    pivots = jnp.stack([field[PIECE:high], field[high + PIECE :]])
    field = jnp.concatenate([field[0:PIECE], field[high : high + PIECE]], axis=0)
    w = weights(pivots, coords)
    fields = [field] + gather_x(field, 1)
    f0 = assemble([v[0:PIECE] for v in fields], 0, x, core, 1)
    f1 = assemble([v[PIECE:] for v in fields], 1, x, core, 1)

    known0 = jnp.where(x == 0, solve0, at_one)
    block1 = (head - dot(known0, u_rows[0, :, 0:NB])).astype(BF)
    solve1 = dot(block1, diag_inverse[1]).astype(BF)
    quarters = [solve1[k * PIECE : (k + 1) * PIECE] for k in range(NX)]
    got = [quarters[0]] + [send_x(quarters[k], k, "y1") for k in (1, 2, 3)]
    part1 = spread_z(pick((x - 1) % NX, got), z, core, "crossed")
    parts1 = [part1] + gather_x(part1, 2)

    quarters = [solve0[k * PIECE : (k + 1) * PIECE] for k in range(NX)]
    got = [quarters[0], at_one[PIECE : 2 * PIECE]] + [send_x(quarters[k], k, "y3") for k in (2, 3)]
    part0 = spread_z(pick(x, got), z, core, "limited")
    parts0 = [part0] + gather_x(part0, 3)
    s0 = assemble(parts0, 0, x, core, 3)
    after = adjoint_source - dot(s0, u_rows[0])

    held = [(x - moved(j, core, 2) - 1) % NX for j in range(NX)]
    info = jnp.stack([row, *held]).astype(jnp.int32)
    scale_value = 1.0 / math.sqrt(SIDES * COLS)
    solved, table = final(info, after, u_rows, forward_field, s0, parts1, f0, f1, w, pivots, coords, scale_value)

    table = table + lax.ppermute(table, "col", [(c, c ^ 1) for c in range(COLS)])
    others = [lax.ppermute(table, "col", [(c, (c + NC * k) % COLS) for c in range(COLS)]) for k in (1, 2, 3)]
    slots = pair_list[:, 0] * QB + pair_list[:, 1] - row * QB
    gradient = choose(slots, [table, others[0], others[1], others[2]])
    return solved, gradient


def solution(mesh):
    return jax.shard_map(
        on_device,
        mesh=mesh,
        in_specs=(P("col", "row"), P(None, None, "row"), P(), P("col", "row"), P(None, "row"), P("row", None)),
        out_specs=(P("col", "row"), P("row", None, None)),
        check_vma=False,
    )
```

time: 506 us -> 99.3 us (0.20)
  waiting for transfers between devices: 354 us -> 18 us
  starting transfers between devices: 0.12 us -> 51 us
  other arithmetic: 42.2 us -> 1.91 us
  local copies, waits for them, and re-layouts: 38.1 us -> 4.7 us
  matrix products: 31.7 us -> 3.93 us
  loops' own time: 21.7 us -> 0 us
  Pallas kernels: 0 us -> 18.4 us
  between operations: 13.9 us -> 1 us
    psum x3 -> x0, waiting for transfers between devices: 354 us -> none  [the longest x2 292 us: spread_2(): return lax.psum(kept, axis)]
    ppermute x0 -> x34, starting transfers between devices: none -> 51 us  [the longest x30 36.5 us: send(): return lax.ppermute(value, ('row', 'col'), sorted(out.items()))]
    dot_general x20 -> x3, matrix products: 31.7 us -> 3.93 us  [dot(): return jnp.dot(a, b, preferred_element_type=F32)]
    dynamic_update_slice x32 -> x0, local copies, waits for them, and re-layouts: 23.3 us -> none  [on_device(): partial_terms = lax.map(whole_pair, pair_list)]
    another operation x1 -> x0, loops' own time: 21.7 us -> none  [on_device(): partial_terms = lax.map(whole_pair, pair_list)]
    reduce_sum x32 -> x0, other arithmetic: 21 us -> none  [the longest x16 15.2 us: whole_pair(): return jnp.sum(influence(pair)[None] * kernel(pair), axis=2)]
    pallas_call x0 -> x3, Pallas kernels: none -> 18.4 us  [the longest x1 8.85 us: final(): pl.pallas_call(body, grid_spec=pltpu.PrefetchScalarGridSpec(num_scalar_pr...]
    ppermute x0 -> x34, waiting for transfers between devices: none -> 18 us  [the longest x30 13 us: send(): return lax.ppermute(value, ('row', 'col'), sorted(out.items()))]
  transfers between devices with their start and end apart: 3 -> 34, of which waited for: 3 -> 15; matrix products, arithmetic and copies ran while one was open for 0% -> 7% of each run, Pallas kernels for 0% -> 7%
where the time goes in v1:
time: 99.3 us; the launch traced here: 98.8 us
  starting transfers between devices  51 us (51%)
  Pallas kernels  18.4 us (19%)
  waiting for transfers between devices  18 us (18%)
  local copies, waits for them, and re-layouts  4.7 us (5%)
  matrix products  3.93 us (4%)
  other arithmetic  1.91 us (2%)
  between operations  1 us (1%)
    ppermute x30, starting transfers between devices, send(): return lax.ppermute(value, ('row', 'col'), sorted(out.items()))  36.5 us
    ppermute x30, waiting for transfers between devices, send(): return lax.ppermute(value, ('row', 'col'), sorted(out.items()))  13 us
    ppermute x1, starting transfers between devices, on_device(): lax.ppermute(table, 'col', [(c, c ^ 1) for c in range(COLS)])  12.8 us
    pallas_call x1, Pallas kernels, final(): pl.pallas_call(body, grid_spec=pltpu.PrefetchScalarGridSpec(num_scalar_pr...  8.85 us
    pallas_call x1, Pallas kernels, weights(): pl.pallas_call(weight_kernel, grid=(2, QB), in_specs=[pl.BlockSpec((1, CR...  7.29 us
    ppermute x3, waiting for transfers between devices, on_device(): lax.ppermute(table, 'col', [(c, (c + NC * k) % COLS) for c in range(COLS)])  4.08 us
    dot_general x3, matrix products, dot(): return jnp.dot(a, b, preferred_element_type=F32)  3.93 us
    pallas_call x1, Pallas kernels, choose(): pl.pallas_call(choose_kernel, grid_spec=pltpu.PrefetchScalarGridSpec(num_...  2.23 us
  transfers between devices with their start and end apart: 34, of which 15 were waited for; matrix products, arithmetic and copies ran while one was open for 7% of the time, Pallas kernels for 7%

profile of v1, /device:TPU:1, one launch (start us, length us, event | category | flops | bytes accessed | tf_op | source)
XLA Modules:
  0.0 98.8 jit_solution(373902052477806650)
XLA Ops:
  1.4 1.0 fusion.17
  2.4 3.4 %collective-permute-start.22 = (bf16[80,512]{1,0:T(8,128)(2,1)S(1)}, bf16[80,512]{1,0:T(8,128)(2,1)S(1)}, u32[]{:S(2)}, u32[]{:S(2)}) collective-permute-start(bf16[80,512]{1,0:T(8,128)(2,1)S(1)} %get-tuple-element.35), channel_id=1, source_target_pairs={{0,24},{1,25},{2,26},{3,27},{4,28},{5,29},{6,30},{7,31},{8,0},{9,1... | collective-permute-start | bytes 245768 | tf_op jit(solution)/shard_map/ppermute | solution.py:56
  5.8 1.7 %collective-permute-start.21 = (bf16[80,512]{1,0:T(8,128)(2,1)S(1)}, bf16[80,512]{1,0:T(8,128)(2,1)S(1)}, u32[]{:S(2)}, u32[]{:S(2)}) collective-permute-start(bf16[80,512]{1,0:T(8,128)(2,1)S(1)} %get-tuple-element.37), channel_id=1, source_target_pairs={{0,16},{1,17},{2,18},{3,19},{4,20},{5,21},{6,22},{7,23},{8,24},{9,... | collective-permute-start | bytes 245768 | tf_op jit(solution)/shard_map/ppermute | solution.py:56
  7.5 1.5 %convolution_convert_fusion.1 = bf16[256,512]{1,0:T(8,128)(2,1)S(1)} fusion(bf16[2,512,512]{2,1,0:T(8,128)(2,1)} %param.8, f32[256,2048]{1,0:T(8,128)} %param.6), kind=kOutput, calls=%fused_computation.6 | convolution fusion | flops 134348800 | bytes 1048576 | tf_op jit(solution)/shard_map/dot_general | solution.py:109
  9.0 1.6 %collective-permute-start = (bf16[256,512]{1,0:T(8,128)(2,1)S(1)}, bf16[256,512]{1,0:T(8,128)(2,1)}, u32[]{:S(2)}, u32[]{:S(2)}) collective-permute-start(bf16[256,512]{1,0:T(8,128)(2,1)S(1)} %convolution_convert_fusion.1), channel_id=1, source_target_pairs={{0,8},{1,9},{2,10},{3,11},{4,12},{5,13},{6,14},{7,15},{8,16},{9,17... | collective-permute-start | bytes 786440 | tf_op jit(solution)/shard_map/ppermute | solution.py:56
  11.5 4.0 %collective-permute-start.24 = (bf16[160,512]{1,0:T(8,128)(2,1)S(1)}, bf16[160,512]{1,0:T(8,128)(2,1)S(1)}, u32[]{:S(2)}, u32[]{:S(2)}) collective-permute-start(bf16[160,512]{1,0:T(8,128)(2,1)S(1)} %pad_maximum_fusion.3), channel_id=1, source_target_pairs={{0,160},{1,161},{2,162},{3,163},{4,164},{5,165},{6,166},{7,167},{8... | collective-permute-start | bytes 491528 | tf_op jit(solution)/shard_map/ppermute | solution.py:56
  16.1 2.5 %collective-permute-start.2 = (bf16[64,512]{1,0:T(8,128)(2,1)}, bf16[64,512]{1,0:T(8,128)(2,1)S(1)}, u32[]{:S(2)}, u32[]{:S(2)}) collective-permute-start(bf16[64,512]{1,0:T(8,128)(2,1)} %get-tuple-element.29), channel_id=1, source_target_pairs={{0,24},{1,25},{2,26},{3,27},{4,28},{5,29},{6,30},{7,31},{8,0},{9,1... | collective-permute-start | bytes 196616 | tf_op jit(solution)/shard_map/ppermute | solution.py:56
  19.3 3.1 %collective-permute-done.23 = bf16[160,512]{1,0:T(8,128)(2,1)S(1)} collective-permute-done((bf16[160,512]{1,0:T(8,128)(2,1)S(1)}, bf16[160,512]{1,0:T(8,128)(2,1)S(1)}, u32[]{:S(2)}, u32[]{:S(2)}) %collective-permute-start.23) | collective-permute-done | bytes 163872 | tf_op jit(solution)/shard_map/ppermute | solution.py:56
  22.6 2.7 %collective-permute-start.25 = (bf16[160,512]{1,0:T(8,128)(2,1)S(1)}, bf16[160,512]{1,0:T(8,128)(2,1)S(1)}, u32[]{:S(2)}, u32[]{:S(2)}) collective-permute-start(bf16[160,512]{1,0:T(8,128)(2,1)S(1)} %select_select_fusion.1), channel_id=1, source_target_pairs={{0,224},{1,225},{2,226},{3,227},{4,228},{5,229},{6,230},{7,231},{8... | collective-permute-start | bytes 491528 | tf_op jit(solution)/shard_map/ppermute | solution.py:56
  26.1 1.2 %collective-permute-start.4 = (bf16[64,512]{1,0:T(8,128)(2,1)S(1)}, bf16[64,512]{1,0:T(8,128)(2,1)S(1)}, u32[]{:S(2)}, u32[]{:S(2)}) collective-permute-start(bf16[64,512]{1,0:T(8,128)(2,1)S(1)} %fusion.16), channel_id=1, source_target_pairs={{0,160},{1,161},{2,162},{3,163},{4,164},{5,165},{6,166},{7,167},{8... | collective-permute-start | bytes 196616 | tf_op jit(solution)/shard_map/ppermute | solution.py:56
  27.6 1.7 %convolution_convert_fusion = bf16[256,512]{1,0:T(8,128)(2,1)S(1)} fusion(bf16[2,512,512]{2,1,0:T(8,128)(2,1)} %param.8, bf16[2,512,2048]{2,1,0:T(8,128)(2,1)} %refs_1_.1, f32[256,2048]{1,0:T(8,128)S(1)} %copy-done.2, bf16[256,512]{1,0:T(8,128)(2,1)S(1)} %convolution_convert_fusion.1, bf16[256,512]{1,0:T(8,128)(2,1)} %collective-permute-done, pred[]{:T(512)S(6)} %eq.184), kind=kOutput, calls=%fused_computation.5 | convolution fusion | flops 268959744 | bytes 2359297 | tf_op jit(solution)/shard_map/dot_general | solution.py:109
  29.3 2.4 %collective-permute-start.12 = (bf16[64,512]{1,0:T(8,128)(2,1)S(1)}, bf16[64,512]{1,0:T(8,128)(2,1)S(1)}, u32[]{:S(2)}, u32[]{:S(2)}) collective-permute-start(bf16[64,512]{1,0:T(8,128)(2,1)S(1)} %get-tuple-element.22), channel_id=1, source_target_pairs={{0,24},{1,25},{2,26},{3,27},{4,28},{5,29},{6,30},{7,31},{8,0},{9,1... | collective-permute-start | bytes 196616 | tf_op jit(solution)/shard_map/ppermute | solution.py:56
  32.3 2.7 %collective-permute-start.11 = (bf16[64,512]{1,0:T(8,128)(2,1)S(1)}, bf16[64,512]{1,0:T(8,128)(2,1)S(1)}, u32[]{:S(2)}, u32[]{:S(2)}) collective-permute-start(bf16[64,512]{1,0:T(8,128)(2,1)S(1)} %get-tuple-element.23), channel_id=1, source_target_pairs={{0,16},{1,17},{2,18},{3,19},{4,20},{5,21},{6,22},{7,23},{8,24},{9,... | collective-permute-start | bytes 196616 | tf_op jit(solution)/shard_map/ppermute | solution.py:56
  35.5 1.4 %collective-permute-done.11 = bf16[64,512]{1,0:T(8,128)(2,1)S(1)} collective-permute-done((bf16[64,512]{1,0:T(8,128)(2,1)S(1)}, bf16[64,512]{1,0:T(8,128)(2,1)S(1)}, u32[]{:S(2)}, u32[]{:S(2)}) %collective-permute-start.11) | collective-permute-done | bytes 65568 | tf_op jit(solution)/shard_map/ppermute | solution.py:56
  36.9 2.5 %collective-permute-done.10 = bf16[64,512]{1,0:T(8,128)(2,1)S(1)} collective-permute-done((bf16[64,512]{1,0:T(8,128)(2,1)S(1)}, bf16[64,512]{1,0:T(8,128)(2,1)S(1)}, u32[]{:S(2)}, u32[]{:S(2)}) %collective-permute-start.10) | collective-permute-done | bytes 65568 | tf_op jit(solution)/shard_map/ppermute | solution.py:56
  39.9 1.4 %collective-permute-done.5 = bf16[64,512]{1,0:T(8,128)(2,1)S(1)} collective-permute-done((bf16[64,512]{1,0:T(8,128)(2,1)S(1)}, bf16[64,512]{1,0:T(8,128)(2,1)S(1)}, u32[]{:S(2)}, u32[]{:S(2)}) %collective-permute-start.5) | collective-permute-done | bytes 65568 | tf_op jit(solution)/shard_map/ppermute | solution.py:56
  41.3 2.6 %collective-permute-start.9 = (bf16[64,512]{1,0:T(8,128)(2,1)S(1)}, bf16[64,512]{1,0:T(8,128)(2,1)S(1)}, u32[]{:S(2)}, u32[]{:S(2)}) collective-permute-start(bf16[64,512]{1,0:T(8,128)(2,1)S(1)} %select_select_fusion.18), channel_id=1, source_target_pairs={{0,24},{1,25},{2,26},{3,27},{4,28},{5,29},{6,30},{7,31},{8,0},{9,1... | collective-permute-start | bytes 196616 | tf_op jit(solution)/shard_map/ppermute | solution.py:56
  44.4 1.6 %collective-permute-done.13 = bf16[64,512]{1,0:T(8,128)(2,1)S(1)} collective-permute-done((bf16[64,512]{1,0:T(8,128)(2,1)S(1)}, bf16[64,512]{1,0:T(8,128)(2,1)S(1)}, u32[]{:S(2)}, u32[]{:S(2)}) %collective-permute-start.13) | collective-permute-done | bytes 65568 | tf_op jit(solution)/shard_map/ppermute | solution.py:56
  46.7 1.4 %collective-permute-start.15 = (bf16[64,512]{1,0:T(8,128)(2,1)S(1)}, bf16[64,512]{1,0:T(8,128)(2,1)S(1)}, u32[]{:S(2)}, u32[]{:S(2)}) collective-permute-start(bf16[64,512]{1,0:T(8,128)(2,1)S(1)} %select_select_fusion.13), channel_id=1, source_target_pairs={{0,224},{1,33},{2,226},{3,35},{4,228},{5,37},{6,230},{7,39},{8,232... | collective-permute-start | bytes 196616 | tf_op jit(solution)/shard_map/ppermute | solution.py:56
  48.1 7.3 %shard_map.77.refs_10_ = f32[2,512,2048]{2,1,0:T(8,128)} custom-call(bf16[2,16,512]{2,1,0:T(8,128)(2,1)S(1)} %pad_maximum_fusion.9.pivot_ref.refs_11_, bf16[16,2048]{1,0:T(8,128)(2,1)S(1)} %pad.4.target_ref.refs_12_), custom_call_target="tpu_custom_call" | custom-call | flops 25165824 | bytes 8388608 | tf_op jit(solution)/shard_map/pallas_call | solution.py:125
  55.4 1.3 %collective-permute-start.29 = (bf16[128,512]{1,0:T(8,128)(2,1)S(1)}, bf16[128,512]{1,0:T(8,128)(2,1)S(1)}, u32[]{:S(2)}, u32[]{:S(2)}) collective-permute-start(bf16[128,512]{1,0:T(8,128)(2,1)S(1)} %pad_maximum_fusion.8), channel_id=1, source_target_pairs={{0,24},{1,9},{2,26},{3,11},{4,28},{5,13},{6,30},{7,15},{8,0},{9,17... | collective-permute-start | bytes 393224 | tf_op jit(solution)/shard_map/ppermute | solution.py:56
  56.7 1.4 %collective-permute-start.28 = (bf16[128,512]{1,0:T(8,128)(2,1)S(1)}, bf16[128,512]{1,0:T(8,128)(2,1)S(1)}, u32[]{:S(2)}, u32[]{:S(2)}) collective-permute-start(bf16[128,512]{1,0:T(8,128)(2,1)S(1)} %pad_maximum_fusion.8), channel_id=1, source_target_pairs={{0,8},{1,17},{2,10},{3,19},{4,12},{5,21},{6,14},{7,23},{8,16},{9,2... | collective-permute-start | bytes 393224 | tf_op jit(solution)/shard_map/ppermute | solution.py:56
  58.1 2.0 %collective-permute-start.27 = (bf16[128,512]{1,0:T(8,128)(2,1)S(1)}, bf16[128,512]{1,0:T(8,128)(2,1)S(1)}, u32[]{:S(2)}, u32[]{:S(2)}) collective-permute-start(bf16[128,512]{1,0:T(8,128)(2,1)S(1)} %pad_maximum_fusion.8), channel_id=1, source_target_pairs={{0,16},{1,25},{2,18},{3,27},{4,20},{5,29},{6,22},{7,31},{8,24},{9,... | collective-permute-start | bytes 393224 | tf_op jit(solution)/shard_map/ppermute | solution.py:56
  61.7 2.6 %collective-permute-start.17 = (bf16[64,512]{1,0:T(8,128)(2,1)S(1)}, bf16[64,512]{1,0:T(8,128)(2,1)S(1)}, u32[]{:S(2)}, u32[]{:S(2)}) collective-permute-start(bf16[64,512]{1,0:T(8,128)(2,1)S(1)} %select_select_fusion.12.refs_4_), channel_id=1, source_target_pairs={{0,8},{1,25},{2,10},{3,27},{4,12},{5,29},{6,14},{7,31},{8,16},{9,1... | collective-permute-start | bytes 196616 | tf_op jit(solution)/shard_map/ppermute | solution.py:56
  65.6 8.8 %shard_map.78 = (f32[256,2048]{1,0:T(8,128)}, f32[3,8,512]{2,1,0:T(8,128)S(1)}) custom-call(s32[5]{0:T(128)S(1)} %stack.32.info, f32[256,2048]{1,0:T(8,128)S(1)} %convolution_subtract_fusion.refs_0_, bf16[2,512,2048]{2,1,0:T(8,128)(2,1)} %refs_1_.1, bf16[256,2048]{1,0:T(8,128)(2,1)S(1)} %copy-done, bf16[256,512]{1,0:T(8,128)(2,1)S(1)} %pad_maximum_fusion.refs_3_, ...), custom_call_target="tpu_custom_call" | custom-call | flops 2684354560 | bytes 16777216 | tf_op jit(solution)/shard_map/pallas_call | solution.py:188
  74.4 12.8 %collective-permute-start.30 = (f32[3,8,512]{2,1,0:T(8,128)S(1)}, f32[3,8,512]{2,1,0:T(8,128)S(1)}, u32[]{:S(2)}, u32[]{:S(2)}) collective-permute-start(f32[3,8,512]{2,1,0:T(8,128)S(1)} %get-tuple-element.5), channel_id=1, source_target_pairs={{0,1},{1,0},{2,3},{3,2},{4,5},{5,4},{6,7},{7,6},{8,9},{9,8},{10,11... | collective-permute-start | bytes 147464 | tf_op jit(solution)/shard_map/ppermute | solution.py:295
  87.2 0.9 collective-permute-done.30
  88.5 1.2 %collective-permute-start.32 = (f32[3,8,512]{2,1,0:T(8,128)S(1)}, f32[3,8,512]{2,1,0:T(8,128)S(1)}, u32[]{:S(2)}, u32[]{:S(2)}) collective-permute-start(f32[3,8,512]{2,1,0:T(8,128)S(1)} %add.73.a_ref), channel_id=1, source_target_pairs={{0,4},{1,5},{2,6},{3,7},{4,0},{5,1},{6,2},{7,3},{8,12},{9,13},{10,... | collective-permute-start | bytes 147464 | tf_op jit(solution)/shard_map/ppermute | solution.py:296
  91.2 1.8 %collective-permute-done.32.c_ref = f32[3,8,512]{2,1,0:T(8,128)S(1)} collective-permute-done((f32[3,8,512]{2,1,0:T(8,128)S(1)}, f32[3,8,512]{2,1,0:T(8,128)S(1)}, u32[]{:S(2)}, u32[]{:S(2)}) %collective-permute-start.32) | collective-permute-done | bytes 49184 | tf_op jit(solution)/shard_map/ppermute | solution.py:296
  93.0 1.4 %collective-permute-done.31.b_ref = f32[3,8,512]{2,1,0:T(8,128)S(1)} collective-permute-done((f32[3,8,512]{2,1,0:T(8,128)S(1)}, f32[3,8,512]{2,1,0:T(8,128)S(1)}, u32[]{:S(2)}, u32[]{:S(2)}) %collective-permute-start.31) | collective-permute-done | bytes 49184 | tf_op jit(solution)/shard_map/ppermute | solution.py:296
  95.0 2.2 %shard_map.79 = f32[16,3,512]{2,1,0:T(4,128)} custom-call(s32[16]{0:T(128)} %subtract_bitcast_fusion.slots, f32[3,8,512]{2,1,0:T(8,128)} %copy-done.3, f32[3,8,512]{2,1,0:T(8,128)} %copy-done.7, f32[3,8,512]{2,1,0:T(8,128)} %copy-done.6, f32[3,8,512]{2,1,0:T(8,128)} %copy-done.5), custom_call_target="tpu_custom_call" | custom-call | tf_op jit(solution)/shard_map/pallas_call | solution.py:237
  97.3 1.6 %copy.8 = f32[16,3,512]{2,0,1:T(8,128)} copy(f32[16,3,512]{2,1,0:T(4,128)} %shard_map.79) | data formatting | bytes 196608
  (91 shorter events, 12.2 us)
Async XLA Ops:
  2.4 8.2 %collective-permute-start.22 = (bf16[80,512]{1,0:T(8,128)(2,1)S(1)}, bf16[80,512]{1,0:T(8,128)(2,1)S(1)}, u32[]{:S(2)}, u32[]{:S(2)}) collective-permute-start(bf16[80,512]{1,0:T(8,128)(2,1)S(1)} %get-tuple-element.35), channel_id=1, source_target_pairs={{0,24},{1,25},{2,26},{3,27},{4,28},{5,29},{6,30},{7,31},{8,0},{9,1... | collective-permute-start | bytes 245768 | tf_op jit(solution)/shard_map/ppermute | solution.py:56
  5.8 5.6 %collective-permute-start.20 = (bf16[80,512]{1,0:T(8,128)(2,1)S(1)}, bf16[80,512]{1,0:T(8,128)(2,1)S(1)}, u32[]{:S(2)}, u32[]{:S(2)}) collective-permute-start(bf16[80,512]{1,0:T(8,128)(2,1)S(1)} %get-tuple-element.36), channel_id=1, source_target_pairs={{0,8},{1,9},{2,10},{3,11},{4,12},{5,13},{6,14},{7,15},{8,16},{9,17... | collective-permute-start | bytes 245768 | tf_op jit(solution)/shard_map/ppermute | solution.py:56
  5.8 5.6 %collective-permute-start.21 = (bf16[80,512]{1,0:T(8,128)(2,1)S(1)}, bf16[80,512]{1,0:T(8,128)(2,1)S(1)}, u32[]{:S(2)}, u32[]{:S(2)}) collective-permute-start(bf16[80,512]{1,0:T(8,128)(2,1)S(1)} %get-tuple-element.37), channel_id=1, source_target_pairs={{0,16},{1,17},{2,18},{3,19},{4,20},{5,21},{6,22},{7,23},{8,24},{9,... | collective-permute-start | bytes 245768 | tf_op jit(solution)/shard_map/ppermute | solution.py:56
  9.0 16.2 %collective-permute-start = (bf16[256,512]{1,0:T(8,128)(2,1)S(1)}, bf16[256,512]{1,0:T(8,128)(2,1)}, u32[]{:S(2)}, u32[]{:S(2)}) collective-permute-start(bf16[256,512]{1,0:T(8,128)(2,1)S(1)} %convolution_convert_fusion.1), channel_id=1, source_target_pairs={{0,8},{1,9},{2,10},{3,11},{4,12},{5,13},{6,14},{7,15},{8,16},{9,17... | collective-permute-start | bytes 786440 | tf_op jit(solution)/shard_map/ppermute | solution.py:56
  11.5 7.8 %collective-permute-start.24 = (bf16[160,512]{1,0:T(8,128)(2,1)S(1)}, bf16[160,512]{1,0:T(8,128)(2,1)S(1)}, u32[]{:S(2)}, u32[]{:S(2)}) collective-permute-start(bf16[160,512]{1,0:T(8,128)(2,1)S(1)} %pad_maximum_fusion.3), channel_id=1, source_target_pairs={{0,160},{1,161},{2,162},{3,163},{4,164},{5,165},{6,166},{7,167},{8... | collective-permute-start | bytes 491528 | tf_op jit(solution)/shard_map/ppermute | solution.py:56
  15.5 6.9 %collective-permute-start.23 = (bf16[160,512]{1,0:T(8,128)(2,1)S(1)}, bf16[160,512]{1,0:T(8,128)(2,1)S(1)}, u32[]{:S(2)}, u32[]{:S(2)}) collective-permute-start(bf16[160,512]{1,0:T(8,128)(2,1)S(1)} %pad_maximum_fusion.3), channel_id=1, source_target_pairs={{0,96},{1,97},{2,98},{3,99},{4,100},{5,101},{6,102},{7,103},{8,104... | collective-permute-start | bytes 491528 | tf_op jit(solution)/shard_map/ppermute | solution.py:56
  16.1 9.1 %collective-permute-start.2 = (bf16[64,512]{1,0:T(8,128)(2,1)}, bf16[64,512]{1,0:T(8,128)(2,1)S(1)}, u32[]{:S(2)}, u32[]{:S(2)}) collective-permute-start(bf16[64,512]{1,0:T(8,128)(2,1)} %get-tuple-element.29), channel_id=1, source_target_pairs={{0,24},{1,25},{2,26},{3,27},{4,28},{5,29},{6,30},{7,31},{8,0},{9,1... | collective-permute-start | bytes 196616 | tf_op jit(solution)/shard_map/ppermute | solution.py:56
  18.6 6.6 %collective-permute-start.1 = (bf16[64,512]{1,0:T(8,128)(2,1)S(1)}, bf16[64,512]{1,0:T(8,128)(2,1)S(1)}, u32[]{:S(2)}, u32[]{:S(2)}) collective-permute-start(bf16[64,512]{1,0:T(8,128)(2,1)S(1)} %get-tuple-element.30), channel_id=1, source_target_pairs={{0,16},{1,17},{2,18},{3,19},{4,20},{5,21},{6,22},{7,23},{8,24},{9,... | collective-permute-start | bytes 196616 | tf_op jit(solution)/shard_map/ppermute | solution.py:56
  22.5 24.0 %collective-permute-start.26 = (bf16[160,512]{1,0:T(8,128)(2,1)S(1)}, bf16[160,512]{1,0:T(8,128)(2,1)S(1)}, u32[]{:S(2)}, u32[]{:S(2)}) collective-permute-start(bf16[160,512]{1,0:T(8,128)(2,1)S(1)} %select_select_fusion.1), channel_id=1, source_target_pairs={{0,32},{1,33},{2,34},{3,35},{4,36},{5,37},{6,38},{7,39},{8,40},{9,... | collective-permute-start | bytes 491528 | tf_op jit(solution)/shard_map/ppermute | solution.py:56
  22.6 24.1 %collective-permute-start.25 = (bf16[160,512]{1,0:T(8,128)(2,1)S(1)}, bf16[160,512]{1,0:T(8,128)(2,1)S(1)}, u32[]{:S(2)}, u32[]{:S(2)}) collective-permute-start(bf16[160,512]{1,0:T(8,128)(2,1)S(1)} %select_select_fusion.1), channel_id=1, source_target_pairs={{0,224},{1,225},{2,226},{3,227},{4,228},{5,229},{6,230},{7,231},{8... | collective-permute-start | bytes 491528 | tf_op jit(solution)/shard_map/ppermute | solution.py:56
  26.1 6.2 %collective-permute-start.4 = (bf16[64,512]{1,0:T(8,128)(2,1)S(1)}, bf16[64,512]{1,0:T(8,128)(2,1)S(1)}, u32[]{:S(2)}, u32[]{:S(2)}) collective-permute-start(bf16[64,512]{1,0:T(8,128)(2,1)S(1)} %fusion.16), channel_id=1, source_target_pairs={{0,160},{1,161},{2,162},{3,163},{4,164},{5,165},{6,166},{7,167},{8... | collective-permute-start | bytes 196616 | tf_op jit(solution)/shard_map/ppermute | solution.py:56
  27.3 7.7 %collective-permute-start.3 = (bf16[64,512]{1,0:T(8,128)(2,1)S(1)}, bf16[64,512]{1,0:T(8,128)(2,1)S(1)}, u32[]{:S(2)}, u32[]{:S(2)}) collective-permute-start(bf16[64,512]{1,0:T(8,128)(2,1)S(1)} %fusion.16), channel_id=1, source_target_pairs={{0,96},{1,97},{2,98},{3,99},{4,100},{5,101},{6,102},{7,103},{8,104... | collective-permute-start | bytes 196616 | tf_op jit(solution)/shard_map/ppermute | solution.py:56
  29.3 6.1 %collective-permute-start.12 = (bf16[64,512]{1,0:T(8,128)(2,1)S(1)}, bf16[64,512]{1,0:T(8,128)(2,1)S(1)}, u32[]{:S(2)}, u32[]{:S(2)}) collective-permute-start(bf16[64,512]{1,0:T(8,128)(2,1)S(1)} %get-tuple-element.22), channel_id=1, source_target_pairs={{0,24},{1,25},{2,26},{3,27},{4,28},{5,29},{6,30},{7,31},{8,0},{9,1... | collective-permute-start | bytes 196616 | tf_op jit(solution)/shard_map/ppermute | solution.py:56
  32.3 4.6 %collective-permute-start.11 = (bf16[64,512]{1,0:T(8,128)(2,1)S(1)}, bf16[64,512]{1,0:T(8,128)(2,1)S(1)}, u32[]{:S(2)}, u32[]{:S(2)}) collective-permute-start(bf16[64,512]{1,0:T(8,128)(2,1)S(1)} %get-tuple-element.23), channel_id=1, source_target_pairs={{0,16},{1,17},{2,18},{3,19},{4,20},{5,21},{6,22},{7,23},{8,24},{9,... | collective-permute-start | bytes 196616 | tf_op jit(solution)/shard_map/ppermute | solution.py:56
  35.1 4.3 %collective-permute-start.10 = (bf16[64,512]{1,0:T(8,128)(2,1)S(1)}, bf16[64,512]{1,0:T(8,128)(2,1)S(1)}, u32[]{:S(2)}, u32[]{:S(2)}) collective-permute-start(bf16[64,512]{1,0:T(8,128)(2,1)S(1)} %get-tuple-element.24), channel_id=1, source_target_pairs={{0,8},{1,9},{2,10},{3,11},{4,12},{5,13},{6,14},{7,15},{8,16},{9,17... | collective-permute-start | bytes 196616 | tf_op jit(solution)/shard_map/ppermute | solution.py:56
  35.4 4.1 %collective-permute-start.6 = (bf16[64,512]{1,0:T(8,128)(2,1)S(1)}, bf16[64,512]{1,0:T(8,128)(2,1)S(1)}, u32[]{:S(2)}, u32[]{:S(2)}) collective-permute-start(bf16[64,512]{1,0:T(8,128)(2,1)S(1)} %select_select_fusion.19), channel_id=1, source_target_pairs={{0,32},{1,33},{2,34},{3,35},{4,36},{5,37},{6,38},{7,39},{8,40},{9,... | collective-permute-start | bytes 196616 | tf_op jit(solution)/shard_map/ppermute | solution.py:56
  36.9 4.3 %collective-permute-start.5 = (bf16[64,512]{1,0:T(8,128)(2,1)S(1)}, bf16[64,512]{1,0:T(8,128)(2,1)S(1)}, u32[]{:S(2)}, u32[]{:S(2)}) collective-permute-start(bf16[64,512]{1,0:T(8,128)(2,1)S(1)} %select_select_fusion.19), channel_id=1, source_target_pairs={{0,224},{1,225},{2,226},{3,227},{4,228},{5,229},{6,230},{7,231},{8... | collective-permute-start | bytes 196616 | tf_op jit(solution)/shard_map/ppermute | solution.py:56
  39.4 5.0 %collective-permute-start.14 = (bf16[64,512]{1,0:T(8,128)(2,1)S(1)}, bf16[64,512]{1,0:T(8,128)(2,1)S(1)}, u32[]{:S(2)}, u32[]{:S(2)}) collective-permute-start(bf16[64,512]{1,0:T(8,128)(2,1)S(1)} %slice_select_fusion), channel_id=1, source_target_pairs={{0,160},{1,97},{2,162},{3,99},{4,164},{5,101},{6,166},{7,103},{8,1... | collective-permute-start | bytes 196616 | tf_op jit(solution)/shard_map/ppermute | solution.py:56
  39.5 6.4 %collective-permute-start.13 = (bf16[64,512]{1,0:T(8,128)(2,1)S(1)}, bf16[64,512]{1,0:T(8,128)(2,1)S(1)}, u32[]{:S(2)}, u32[]{:S(2)}) collective-permute-start(bf16[64,512]{1,0:T(8,128)(2,1)S(1)} %slice_select_fusion), channel_id=1, source_target_pairs={{0,96},{1,161},{2,98},{3,163},{4,100},{5,165},{6,102},{7,167},{8,1... | collective-permute-start | bytes 196616 | tf_op jit(solution)/shard_map/ppermute | solution.py:56
  41.3 16.8 %collective-permute-start.9 = (bf16[64,512]{1,0:T(8,128)(2,1)S(1)}, bf16[64,512]{1,0:T(8,128)(2,1)S(1)}, u32[]{:S(2)}, u32[]{:S(2)}) collective-permute-start(bf16[64,512]{1,0:T(8,128)(2,1)S(1)} %select_select_fusion.18), channel_id=1, source_target_pairs={{0,24},{1,25},{2,26},{3,27},{4,28},{5,29},{6,30},{7,31},{8,0},{9,1... | collective-permute-start | bytes 196616 | tf_op jit(solution)/shard_map/ppermute | solution.py:56
  44.4 15.8 %collective-permute-start.8 = (bf16[64,512]{1,0:T(8,128)(2,1)S(1)}, bf16[64,512]{1,0:T(8,128)(2,1)S(1)}, u32[]{:S(2)}, u32[]{:S(2)}) collective-permute-start(bf16[64,512]{1,0:T(8,128)(2,1)S(1)} %select_select_fusion.18), channel_id=1, source_target_pairs={{0,8},{1,9},{2,10},{3,11},{4,12},{5,13},{6,14},{7,15},{8,16},{9,17... | collective-permute-start | bytes 196616 | tf_op jit(solution)/shard_map/ppermute | solution.py:56
  46.0 14.7 %collective-permute-start.7 = (bf16[64,512]{1,0:T(8,128)(2,1)S(1)}, bf16[64,512]{1,0:T(8,128)(2,1)S(1)}, u32[]{:S(2)}, u32[]{:S(2)}) collective-permute-start(bf16[64,512]{1,0:T(8,128)(2,1)S(1)} %select_select_fusion.18), channel_id=1, source_target_pairs={{0,16},{1,17},{2,18},{3,19},{4,20},{5,21},{6,22},{7,23},{8,24},{9,... | collective-permute-start | bytes 196616 | tf_op jit(solution)/shard_map/ppermute | solution.py:56
  46.5 8.9 %collective-permute-start.16 = (bf16[64,512]{1,0:T(8,128)(2,1)S(1)}, bf16[64,512]{1,0:T(8,128)(2,1)S(1)}, u32[]{:S(2)}, u32[]{:S(2)}) collective-permute-start(bf16[64,512]{1,0:T(8,128)(2,1)S(1)} %select_select_fusion.13), channel_id=1, source_target_pairs={{0,32},{1,225},{2,34},{3,227},{4,36},{5,229},{6,38},{7,231},{8,40}... | collective-permute-start | bytes 196616 | tf_op jit(solution)/shard_map/ppermute | solution.py:56
  46.7 10.0 %collective-permute-start.15 = (bf16[64,512]{1,0:T(8,128)(2,1)S(1)}, bf16[64,512]{1,0:T(8,128)(2,1)S(1)}, u32[]{:S(2)}, u32[]{:S(2)}) collective-permute-start(bf16[64,512]{1,0:T(8,128)(2,1)S(1)} %select_select_fusion.13), channel_id=1, source_target_pairs={{0,224},{1,33},{2,226},{3,35},{4,228},{5,37},{6,230},{7,39},{8,232... | collective-permute-start | bytes 196616 | tf_op jit(solution)/shard_map/ppermute | solution.py:56
  55.4 6.2 %collective-permute-start.29 = (bf16[128,512]{1,0:T(8,128)(2,1)S(1)}, bf16[128,512]{1,0:T(8,128)(2,1)S(1)}, u32[]{:S(2)}, u32[]{:S(2)}) collective-permute-start(bf16[128,512]{1,0:T(8,128)(2,1)S(1)} %pad_maximum_fusion.8), channel_id=1, source_target_pairs={{0,24},{1,9},{2,26},{3,11},{4,28},{5,13},{6,30},{7,15},{8,0},{9,17... | collective-permute-start | bytes 393224 | tf_op jit(solution)/shard_map/ppermute | solution.py:56
  56.7 7.5 %collective-permute-start.28 = (bf16[128,512]{1,0:T(8,128)(2,1)S(1)}, bf16[128,512]{1,0:T(8,128)(2,1)S(1)}, u32[]{:S(2)}, u32[]{:S(2)}) collective-permute-start(bf16[128,512]{1,0:T(8,128)(2,1)S(1)} %pad_maximum_fusion.8), channel_id=1, source_target_pairs={{0,8},{1,17},{2,10},{3,19},{4,12},{5,21},{6,14},{7,23},{8,16},{9,2... | collective-permute-start | bytes 393224 | tf_op jit(solution)/shard_map/ppermute | solution.py:56
  58.1 6.1 %collective-permute-start.27 = (bf16[128,512]{1,0:T(8,128)(2,1)S(1)}, bf16[128,512]{1,0:T(8,128)(2,1)S(1)}, u32[]{:S(2)}, u32[]{:S(2)}) collective-permute-start(bf16[128,512]{1,0:T(8,128)(2,1)S(1)} %pad_maximum_fusion.8), channel_id=1, source_target_pairs={{0,16},{1,25},{2,18},{3,27},{4,20},{5,29},{6,22},{7,31},{8,24},{9,... | collective-permute-start | bytes 393224 | tf_op jit(solution)/shard_map/ppermute | solution.py:56
  60.2 4.7 %collective-permute-start.19 = (bf16[64,512]{1,0:T(8,128)(2,1)S(1)}, bf16[64,512]{1,0:T(8,128)(2,1)S(1)}, u32[]{:S(2)}, u32[]{:S(2)}) collective-permute-start(bf16[64,512]{1,0:T(8,128)(2,1)S(1)} %select_select_fusion.12.refs_4_), channel_id=1, source_target_pairs={{0,24},{1,17},{2,26},{3,19},{4,28},{5,21},{6,30},{7,23},{8,0},{9,2... | collective-permute-start | bytes 196616 | tf_op jit(solution)/shard_map/ppermute | solution.py:56
  60.7 4.8 %collective-permute-start.18 = (bf16[64,512]{1,0:T(8,128)(2,1)S(1)}, bf16[64,512]{1,0:T(8,128)(2,1)S(1)}, u32[]{:S(2)}, u32[]{:S(2)}) collective-permute-start(bf16[64,512]{1,0:T(8,128)(2,1)S(1)} %select_select_fusion.12.refs_4_), channel_id=1, source_target_pairs={{0,16},{1,9},{2,18},{3,11},{4,20},{5,13},{6,22},{7,15},{8,24},{9,1... | collective-permute-start | bytes 196616 | tf_op jit(solution)/shard_map/ppermute | solution.py:56
  74.4 13.7 %collective-permute-start.30 = (f32[3,8,512]{2,1,0:T(8,128)S(1)}, f32[3,8,512]{2,1,0:T(8,128)S(1)}, u32[]{:S(2)}, u32[]{:S(2)}) collective-permute-start(f32[3,8,512]{2,1,0:T(8,128)S(1)} %get-tuple-element.5), channel_id=1, source_target_pairs={{0,1},{1,0},{2,3},{3,2},{4,5},{5,4},{6,7},{7,6},{8,9},{9,8},{10,11... | collective-permute-start | bytes 147464 | tf_op jit(solution)/shard_map/ppermute | solution.py:295
  88.5 4.4 %collective-permute-start.32 = (f32[3,8,512]{2,1,0:T(8,128)S(1)}, f32[3,8,512]{2,1,0:T(8,128)S(1)}, u32[]{:S(2)}, u32[]{:S(2)}) collective-permute-start(f32[3,8,512]{2,1,0:T(8,128)S(1)} %add.73.a_ref), channel_id=1, source_target_pairs={{0,4},{1,5},{2,6},{3,7},{4,0},{5,1},{6,2},{7,3},{8,12},{9,13},{10,... | collective-permute-start | bytes 147464 | tf_op jit(solution)/shard_map/ppermute | solution.py:296
  89.7 4.7 %collective-permute-start.31 = (f32[3,8,512]{2,1,0:T(8,128)S(1)}, f32[3,8,512]{2,1,0:T(8,128)S(1)}, u32[]{:S(2)}, u32[]{:S(2)}) collective-permute-start(f32[3,8,512]{2,1,0:T(8,128)S(1)} %add.73.a_ref), channel_id=1, source_target_pairs={{0,2},{1,3},{2,4},{3,5},{4,6},{5,7},{6,0},{7,1},{8,10},{9,11},{10,... | collective-permute-start | bytes 147464 | tf_op jit(solution)/shard_map/ppermute | solution.py:296
  (11 other events, 103.1 us)

commit v2 on v1

v2 whole, which is shorter than its diff:
```python
import math

import jax
import jax.numpy as jnp
from jax import lax
from jax.experimental import pallas as pl
from jax.experimental.pallas import tpu as pltpu
from jax.sharding import PartitionSpec as P

NZ, NX, NY, NC = 8, 4, 4, 2
ROWS, COLS = NZ * NX, NY * NC
NB, SIDES, WIDTH = 512, 256, 2048
QB = WIDTH // NB
HALF = SIDES // 2
CROWS = 16
FAR = 3
BF, F32 = jnp.bfloat16, jnp.float32
VMEM_LIMIT = 15 * 1024 * 1024


def node(z, x):
    return (z % NZ) * NX + x % NX


def shift(dz, dx, zs=range(NZ)):
    return [(node(z, x), node(z + dz, x + dx)) for z in zs for x in range(NX)]


def closed(pairs):
    out, back = dict(pairs), {d: s for s, d in pairs}
    for last in back:
        if last not in dict(pairs):
            first = last
            while first in back:
                first = back[first]
            out[last] = first
    return out


def send(value, pairs0, pairs1=None, idle="core"):
    maps = [closed(pairs0), closed(pairs0 if pairs1 is None else pairs1)]
    flip = 3 if idle == "y3" else 1
    out = {}
    for row in range(ROWS):
        free = [row not in maps[0], row not in maps[1]]
        for y in range(NY):
            for core in range(NC):
                me = row * COLS + y * NC + core
                if not free[core]:
                    out[me] = maps[core][row] * COLS + y * NC + core
                elif all(free) and idle == "core":
                    out[me] = row * COLS + y * NC + 1 - core
                else:
                    out[me] = row * COLS + (y ^ flip) * NC + core
    return lax.ppermute(value, ("row", "col"), sorted(out.items()))


def choose(condition, a, b):
    return lax.select(condition, a, b)


def swap_x(value, partner, zs=range(NZ)):
    return send(value, [(node(z, x), node(z, partner[x])) for z in zs for x in range(NX)])


def spread_far(value, z):
    plus = send(value, [(node(a, x), node(b, x)) for a, b in ((0, 3), (3, 2), (2, 1), (1, 0)) for x in range(NX)])
    minus = send(value, [(node(a, x), node(b, x)) for a, b in ((0, 5), (5, 6), (6, 7), (7, 0)) for x in range(NX)])
    return choose(z == 3, plus, choose(z == 5, minus, value))


def spread_near(value, z):
    plus, minus = send(value, shift(1, 0)), send(value, shift(-1, 0))
    value = choose((z == 1) | (z == 4) | (z == 6), plus, value)
    return choose((z == 2) | (z == 7), minus, value)


def gather_x(value, twist):
    return [send(value, shift(0, j), shift(0, (j + twist - 1) % 3 + 1)) for j in (1, 2, 3)]


def moved(j, core, twist):
    return j if j == 0 else jnp.where(core == 0, j, (j + twist - 1) % 3 + 1)


def held(x, core, twist):
    return [(x - moved(j, core, twist)) % NX for j in range(NX)]


def dot(a, b):
    return jnp.dot(a, b, preferred_element_type=F32)


def weight_kernel(pivot_ref, target_ref, out_ref):
    source = pivot_ref[0].astype(F32)
    target = target_ref[...].astype(F32)
    source = source.T
    total = None
    for c in range(3):
        d = source[:, c : c + 1] - target[c : c + 1, :]
        total = d * d if total is None else total + d * d
    r = lax.rsqrt(total + 1.0)
    out_ref[0] = (r * r * r).astype(BF)


def weights(pivots, targets):
    return pl.pallas_call(
        weight_kernel,
        grid=(2, QB),
        in_specs=[
            pl.BlockSpec((1, CROWS, NB), lambda a, q: (a, 0, 0)),
            pl.BlockSpec((CROWS, NB), lambda a, q: (0, q)),
        ],
        out_specs=pl.BlockSpec((1, NB, NB), lambda a, q: (a, 0, q)),
        out_shape=jax.ShapeDtypeStruct((2, NB, WIDTH), BF),
        cost_estimate=pl.CostEstimate(
            flops=12 * NB * WIDTH * 2, bytes_accessed=8 * NB * WIDTH, transcendentals=2 * NB * WIDTH
        ),
        compiler_params=pltpu.CompilerParams(vmem_limit_bytes=VMEM_LIMIT),
    )(pivots, targets)


def final_kernel(
    info, source_ref, u_ref, field_ref, p0, p1, p2, p3, own_ref, other_ref, w_ref, pivot_ref, target_ref,
    solved_ref, grad_ref, s_ref, both_ref, left_ref, right_ref, scale_value,
):
    q = pl.program_id(0)
    row = info[0]

    @pl.when(q == 0)
    def _():
        for j, ref in enumerate((p0, p1, p2, p3)):
            column = info[2 + j]
            a = (column ^ (column >> 1)) & 1
            start = pl.multiple_of((column >> 1) * HALF, HALF)
            s_ref[a, pl.ds(start, HALF), :] = ref[...]
        for a in range(2):
            both_ref[:, a * NB : (a + 1) * NB] = s_ref[a]
            left_ref[a, :, 0:SIDES] = s_ref[a].T
        left_ref[info[1], :, SIDES:] = own_ref[...].T
        left_ref[1 - info[1], :, SIDES:] = other_ref[...].T

    solved_ref[...] = source_ref[...] - dot(both_ref[...], u_ref[...])

    @pl.when((q == 0) & (row < 2))
    def _():
        solved_ref[...] = s_ref[row].astype(F32)

    right_ref[0:SIDES, :] = field_ref[...]
    right_ref[SIDES:, :] = solved_ref[...].astype(BF)
    target = target_ref[0:8, :]
    lines = lax.broadcasted_iota(jnp.int32, target.shape, 0)
    target = jnp.where(lines == 3, 1.0, target.astype(F32)).astype(BF)
    for a in range(2):
        influence = dot(left_ref[a], right_ref[...])
        weighted = (influence * w_ref[a].astype(F32)).astype(BF)
        sums = lax.dot_general(target, weighted, (((1,), (1,)), ((), ())), preferred_element_type=F32)
        source = pivot_ref[a].astype(F32)
        for c in range(3):
            grad_ref[c, pl.ds(a * QB + q, 1), :] = (
                sums[c : c + 1, :] - source[c : c + 1, :] * sums[3:4, :]
            ) * scale_value


def final(info, source, u_rows, field, parts, fields, w, pivots, targets, scale_value):
    def whole(shape):
        return pl.BlockSpec(shape, lambda q, info: (0,) * len(shape))

    def body(info, *refs):
        final_kernel(info, *refs, scale_value)

    return pl.pallas_call(
        body,
        grid_spec=pltpu.PrefetchScalarGridSpec(
            num_scalar_prefetch=1,
            grid=(QB,),
            in_specs=[
                pl.BlockSpec((SIDES, NB), lambda q, info: (0, q)),
                pl.BlockSpec((2 * NB, NB), lambda q, info: (0, q)),
                pl.BlockSpec((SIDES, NB), lambda q, info: (0, q)),
                *[whole((HALF, NB))] * NX,
                *[whole((SIDES, NB))] * 2,
                pl.BlockSpec((2, NB, NB), lambda q, info: (0, 0, q)),
                whole((2, CROWS, NB)),
                pl.BlockSpec((CROWS, NB), lambda q, info: (0, q)),
            ],
            out_specs=[
                pl.BlockSpec((SIDES, NB), lambda q, info: (0, q)),
                whole((3, 2 * QB, NB)),
            ],
            scratch_shapes=[
                pltpu.VMEM((2, SIDES, NB), BF),
                pltpu.VMEM((SIDES, 2 * NB), BF),
                pltpu.VMEM((2, NB, 2 * SIDES), BF),
                pltpu.VMEM((2 * SIDES, NB), BF),
            ],
        ),
        out_shape=[
            jax.ShapeDtypeStruct((SIDES, WIDTH), F32),
            jax.ShapeDtypeStruct((3, 2 * QB, NB), F32),
        ],
        cost_estimate=pl.CostEstimate(
            flops=4 * SIDES * NB * WIDTH + 8 * SIDES * NB * WIDTH, bytes_accessed=14 * 2**20, transcendentals=0
        ),
        compiler_params=pltpu.CompilerParams(vmem_limit_bytes=VMEM_LIMIT),
    )(info, source, u_rows.reshape(2 * NB, WIDTH), field, *parts, *fields, w, pivots, targets)


def spread_fields(value, z, x, core):
    along_x = ((0, 3), (1, 2))
    steps0 = [
        [(node(0, a), node(0, b)) for a, b in along_x],
        [(node(a, x), node(b, x)) for a, b in ((0, 3),) for x in range(NX)],
        [(node(a, x), node(b, x)) for a, b in ((0, 6), (3, 5)) for x in range(NX)],
        [(node(a, x), node(b, x)) for a, b in ((0, 1), (3, 2), (6, 7), (5, 4)) for x in range(NX)],
    ]
    steps1 = [
        [(node(a, x), node(b, x)) for a, b in ((0, 5),) for x in (0, 1)],
        [(node(a, x), node(b, x)) for a, b in ((0, 2), (5, 3)) for x in (0, 1)],
        [(node(a, x), node(b, x)) for a, b in ((0, 7), (5, 6), (2, 1), (3, 4)) for x in (0, 1)],
        [(node(z, a), node(z, b)) for a, b in along_x for z in range(NZ)],
    ]
    near = (z == 1) | (z == 4) | (z == 7)
    here0 = [(z == 0) & (x >= 2), z == 3, (z == 6) | (z == 5), near | (z == 2)]
    here1 = [z == 5, (z == 2) | (z == 3), near | (z == 6), x >= 2]
    for k in range(4):
        got = send(value, steps0[k], steps1[k])
        value = jnp.where(jnp.where(core == 0, here0[k], here1[k]), got, value)
        yield value
    yield send(value, [(node(z, x), node(z, x ^ 1)) for z in range(NZ) for x in range(NX)])


def on_device(adjoint_source, u_rows, diag_inverse, forward_field, panel_coords, pair_list):
    row = lax.axis_index("row")
    z, x = row // NX, row % NX
    core = lax.axis_index("col") % NC
    head = adjoint_source[:, 0:NB]
    coords = jnp.pad(panel_coords, ((0, CROWS - 3), (0, 0)))

    solve0 = dot(head.astype(BF), diag_inverse[0]).astype(BF)
    at_one = send(solve0, [(node(0, 0), node(0, 1))])

    own_field, _ = lax.optimization_barrier((forward_field[:, 0:NB], solve0))
    field_steps = list(spread_fields(own_field, z, x, core))

    known0 = choose(x == 0, solve0, at_one)
    block1 = (head - dot(known0, u_rows[0, :, 0:NB])).astype(BF)
    solve1 = dot(block1, diag_inverse[1]).astype(BF)

    mine = choose(x == 0, solve0, solve1)
    own_coords = coords[:, 0:NB]
    first = jnp.concatenate([mine[0:HALF], own_coords], axis=0)
    second = jnp.concatenate([mine[HALF:], own_coords], axis=0)
    solves = choose(x >= 2, swap_x(second, (3, 2, 1, 0), zs=(0,)), first)
    solves = spread_near(spread_far(solves, z), z)
    coords_own = solves[HALF:]
    coords_other = swap_x(coords_own, (1, 0, 3, 2))
    odd = (x == 1) | (x == 2)
    pivots = jnp.stack([choose(odd, coords_other, coords_own), choose(odd, coords_own, coords_other)])
    solves = solves[0:HALF]
    w = weights(pivots, coords)
    parts = [solves] + gather_x(solves, 2)

    swapped = odd.astype(jnp.int32)
    info = jnp.stack([row, swapped, *held(x, core, 2)]).astype(jnp.int32)
    scale_value = 1.0 / math.sqrt(SIDES * COLS)
    solved, table = final(
        info, adjoint_source, u_rows, forward_field, parts, field_steps[3:], w, pivots, coords, scale_value
    )

    table = table + lax.ppermute(table, "col", [(c, c ^ 1) for c in range(COLS)])
    others = [lax.ppermute(table, "col", [(c, (c + NC * k) % COLS) for c in range(COLS)]) for k in (1, 2, 3)]
    table = (table + others[1]) + (others[0] + others[2])
    slots = (pair_list[:, 0] * QB + pair_list[:, 1] - row * QB)[:, None, None]
    gradient = jnp.broadcast_to(table[:, 0, :][None], (pair_list.shape[0], 3, NB))
    for k in range(1, 2 * QB):
        gradient = jnp.where(slots == k, table[:, k, :][None], gradient)
    return solved, gradient


def solution(mesh):
    return jax.shard_map(
        on_device,
        mesh=mesh,
        in_specs=(P("col", "row"), P(None, None, "row"), P(), P("col", "row"), P(None, "row"), P("row", None)),
        out_specs=(P("col", "row"), P("row", None, None)),
        check_vma=False,
    )
```

time: 99.3 us -> 74.6 us (0.75)
  starting transfers between devices: 51 us -> 28.9 us
  Pallas kernels: 18.4 us -> 13.5 us
  waiting for transfers between devices: 18 us -> 21.4 us
  local copies, waits for them, and re-layouts: 4.7 us -> 1.88 us
  other arithmetic: 1.91 us -> 3.69 us
    ppermute x30 -> x15, starting transfers between devices: 36.5 us -> 17.8 us  [send(): return lax.ppermute(value, ('row', 'col'), sorted(out.items()))]
    ppermute x1, starting transfers between devices: 12.8 us -> 5.25 us  [on_device(): lax.ppermute(table, 'col', [(c, c ^ 1) for c in range(COLS)])]
    ppermute x30 -> x15, waiting for transfers between devices: 13 us -> 19 us  [send(): return lax.ppermute(value, ('row', 'col'), sorted(out.items()))]
    ppermute x3, starting transfers between devices: 1.63 us -> 5.79 us  [on_device(): lax.ppermute(table, 'col', [(c, (c + NC * k) % COLS) for c in range(COLS)])]
    ppermute x3, waiting for transfers between devices: 4.08 us -> 1.47 us  [on_device(): lax.ppermute(table, 'col', [(c, (c + NC * k) % COLS) for c in range(COLS)])]
    select_n x14 -> x8, other arithmetic: 1.25 us -> 3.62 us  [the longest x3 1.66 us: choose(): return lax.select(condition, a, b)]
    pallas_call x1 -> x0, Pallas kernels: 2.23 us -> none  [choose(): pl.pallas_call(choose_kernel, grid_spec=pltpu.PrefetchScalarGridSpec(num_...]
    unnamed x19 -> x16, local copies, waits for them, and re-layouts: 2.22 us -> 0.05 us
  transfers between devices with their start and end apart: 34 -> 19, of which waited for: 15 -> 10; matrix products, arithmetic and copies ran while one was open for 7% -> 9% of each run, Pallas kernels for 7% -> 7%
where the time goes in v2:
time: 74.6 us; the launch traced here: 73.8 us
  starting transfers between devices  28.9 us (39%)
  waiting for transfers between devices  21.4 us (29%)
  Pallas kernels  13.5 us (18%)
  other arithmetic  3.69 us (5%)
  matrix products  3.39 us (5%)
  local copies, waits for them, and re-layouts  1.88 us (3%)
  between operations  1.08 us (1%)
    ppermute x15, waiting for transfers between devices, send(): return lax.ppermute(value, ('row', 'col'), sorted(out.items()))  19 us
    ppermute x15, starting transfers between devices, send(): return lax.ppermute(value, ('row', 'col'), sorted(out.items()))  17.8 us
    pallas_call x1, Pallas kernels, final(): pl.pallas_call(body, grid_spec=pltpu.PrefetchScalarGridSpec(num_scalar_pr...  8.19 us
    ppermute x3, starting transfers between devices, on_device(): lax.ppermute(table, 'col', [(c, (c + NC * k) % COLS) for c in range(COLS)])  5.79 us
    pallas_call x1, Pallas kernels, weights(): pl.pallas_call(weight_kernel, grid=(2, QB), in_specs=[pl.BlockSpec((1, CR...  5.31 us
    ppermute x1, starting transfers between devices, on_device(): lax.ppermute(table, 'col', [(c, c ^ 1) for c in range(COLS)])  5.25 us
    dot_general x2, matrix products, dot(): return jnp.dot(a, b, preferred_element_type=F32)  3.39 us
    select_n x3, other arithmetic, choose(): return lax.select(condition, a, b)  1.66 us
  transfers between devices with their start and end apart: 19, of which 10 were waited for; matrix products, arithmetic and copies ran while one was open for 9% of the time, Pallas kernels for 7%

profile of v2, /device:TPU:1, one launch (start us, length us, event | category | flops | bytes accessed | tf_op | source)
XLA Modules:
  0.0 73.8 jit_solution(10034616918690559038)
XLA Ops:
  0.6 1.5 %convolution_convert_fusion.1 = bf16[256,512]{1,0:T(8,128)(2,1)S(1)} fusion(bf16[2,512,512]{2,1,0:T(8,128)(2,1)} %param.8, f32[256,2048]{1,0:T(8,128)} %refs_0_.1), kind=kOutput, calls=%fused_computation.3 | convolution fusion | flops 134348800 | bytes 1048576 | tf_op jit(solution)/shard_map/dot_general | solution.py:91
  2.1 2.1 %collective-permute-start = (bf16[256,512]{1,0:T(8,128)(2,1)S(1)}, bf16[256,512]{1,0:T(8,128)(2,1)S(1)}, u32[]{:S(2)}, u32[]{:S(2)}) collective-permute-start(bf16[256,512]{1,0:T(8,128)(2,1)S(1)} %convolution_convert_fusion.1), channel_id=1, source_target_pairs={{0,8},{1,9},{2,10},{3,11},{4,12},{5,13},{6,14},{7,15},{8,0},{9,1},... | collective-permute-start | bytes 786440 | tf_op jit(solution)/shard_map/ppermute | solution.py:55
  4.3 1.0 %slice.68 = bf16[256,512]{1,0:T(8,128)(2,1)S(1)} slice(bf16[256,2048]{1,0:T(8,128)(2,1)} %refs_2_.1), slice={[0:256], [0:512]} | slice | bytes 524288 | tf_op jit(solution)/shard_map/slice | solution.py:243
  5.2 6.0 %collective-permute-start.9 = (bf16[256,512]{1,0:T(8,128)(2,1)S(1)}, bf16[256,512]{1,0:T(8,128)(2,1)S(1)}, u32[]{:S(2)}, u32[]{:S(2)}) collective-permute-start(bf16[256,512]{1,0:T(8,128)(2,1)S(1)} %slice.68), channel_id=1, source_target_pairs={{0,24},{1,161},{2,26},{3,163},{4,28},{5,165},{6,30},{7,167},{8,16}... | collective-permute-start | bytes 786440 | tf_op jit(solution)/shard_map/ppermute | solution.py:55
  11.3 0.7 pad_slice_fusion
  11.9 1.9 %fusion.1 = bf16[256,512]{1,0:T(8,128)(2,1)S(1)} fusion(bf16[256,512]{1,0:T(8,128)(2,1)S(1)} %convolution_convert_fusion.1, bf16[2,512,512]{2,1,0:T(8,128)(2,1)} %param.8, bf16[2,512,2048]{2,1,0:T(8,128)(2,1)} %param.7, f32[256,2048]{1,0:T(8,128)} %refs_0_.1, bf16[256,512]{1,0:T(8,128)(2,1)S(1)} %collective-permute-done, pred[]{:T(512)S(6)} %eq.144), kind=kOutput, calls=%fused_computation.4 | convolution fusion | flops 269090816 | bytes 2622464 | tf_op jit(solution)/shard_map/dot_general | solution.py:91
  14.0 1.0 %collective-permute-done.9 = bf16[256,512]{1,0:T(8,128)(2,1)S(1)} collective-permute-done((bf16[256,512]{1,0:T(8,128)(2,1)S(1)}, bf16[256,512]{1,0:T(8,128)(2,1)S(1)}, u32[]{:S(2)}, u32[]{:S(2)}) %collective-permute-start.9) | collective-permute-done | bytes 262176 | tf_op jit(solution)/shard_map/ppermute | solution.py:55
  15.2 5.6 %collective-permute-done.1 = bf16[144,512]{1,0:T(8,128)(2,1)S(1)} collective-permute-done((bf16[144,512]{1,0:T(8,128)(2,1)S(1)}, bf16[144,512]{1,0:T(8,128)(2,1)S(1)}, u32[]{:S(2)}, u32[]{:S(2)}) %collective-permute-start.1) | collective-permute-done | bytes 147488 | tf_op jit(solution)/shard_map/ppermute | solution.py:55
  21.0 3.1 %collective-permute-done.10 = bf16[256,512]{1,0:T(8,128)(2,1)S(1)} collective-permute-done((bf16[256,512]{1,0:T(8,128)(2,1)S(1)}, bf16[256,512]{1,0:T(8,128)(2,1)S(1)}, u32[]{:S(2)}, u32[]{:S(2)}) %collective-permute-start.10) | collective-permute-done | bytes 262176 | tf_op jit(solution)/shard_map/ppermute | solution.py:55
  24.2 0.1 collective-permute-start.11
  24.3 2.8 %collective-permute-done.2 = bf16[144,512]{1,0:T(8,128)(2,1)S(1)} collective-permute-done((bf16[144,512]{1,0:T(8,128)(2,1)S(1)}, bf16[144,512]{1,0:T(8,128)(2,1)S(1)}, u32[]{:S(2)}, u32[]{:S(2)}) %collective-permute-start.2) | collective-permute-done | bytes 147488 | tf_op jit(solution)/shard_map/ppermute | solution.py:55
  27.1 0.7 select_select_fusion.1
  27.8 1.5 %collective-permute-start.5 = (bf16[144,512]{1,0:T(8,128)(2,1)}, bf16[144,512]{1,0:T(8,128)(2,1)}, u32[]{:S(2)}, u32[]{:S(2)}) collective-permute-start(bf16[144,512]{1,0:T(8,128)(2,1)} %select_select_fusion.1), channel_id=1, source_target_pairs={{0,32},{1,33},{2,34},{3,35},{4,36},{5,37},{6,38},{7,39},{8,40},{9,... | collective-permute-start | bytes 442376 | tf_op jit(solution)/shard_map/ppermute | solution.py:55
  29.3 4.2 %collective-permute-done.11 = bf16[256,512]{1,0:T(8,128)(2,1)} collective-permute-done((bf16[256,512]{1,0:T(8,128)(2,1)S(1)}, bf16[256,512]{1,0:T(8,128)(2,1)}, u32[]{:S(2)}, u32[]{:S(2)}) %collective-permute-start.11) | collective-permute-done | bytes 262176 | tf_op jit(solution)/shard_map/ppermute | solution.py:55
  33.5 1.1 %broadcast_select_fusion.2 = bf16[256,512]{1,0:T(8,128)(2,1)S(1)} fusion(bf16[256,512]{1,0:T(8,128)(2,1)} %collective-permute-done.11, bf16[256,512]{1,0:T(8,128)(2,1)} %copy-done.3, pred[]{:T(512)S(6)} %select_n.177), kind=kLoop, calls=%fused_computation.16 | loop fusion | flops 131072 | bytes 786433 | tf_op jit(solution)/shard_map/jit(_where)/select_n | solution.py:228
  34.7 0.1 collective-permute-start.12
  35.1 0.9 %select_select_fusion = bf16[144,512]{1,0:T(8,128)(2,1)S(1)} fusion(bf16[144,512]{1,0:T(8,128)(2,1)} %collective-permute-done.4, bf16[144,512]{1,0:T(8,128)(2,1)} %collective-permute-done.5, bf16[144,512]{1,0:T(8,128)(2,1)} %select_select_fusion.1, pred[]{:T(512)S(6)} %or.31, pred[]{:T(512)S(6)} %or.29), kind=kLoop, calls=%fused_computation.22 | loop fusion | flops 147456 | bytes 589826 | tf_op jit(solution)/shard_map/select_n | solution.py:59
  36.1 2.6 %collective-permute-start.6 = (bf16[128,512]{1,0:T(8,128)(2,1)S(1)}, bf16[128,512]{1,0:T(8,128)(2,1)S(1)}, u32[]{:S(2)}, u32[]{:S(2)}) collective-permute-start(bf16[128,512]{1,0:T(8,128)(2,1)S(1)} %slice.82.refs_3_), channel_id=1, source_target_pairs={{0,8},{1,25},{2,10},{3,27},{4,12},{5,29},{6,14},{7,31},{8,16},{9,1... | collective-permute-start | bytes 393224 | tf_op jit(solution)/shard_map/ppermute | solution.py:55
  38.6 1.7 %collective-permute-start.7 = (bf16[128,512]{1,0:T(8,128)(2,1)S(1)}, bf16[128,512]{1,0:T(8,128)(2,1)S(1)}, u32[]{:S(2)}, u32[]{:S(2)}) collective-permute-start(bf16[128,512]{1,0:T(8,128)(2,1)S(1)} %slice.82.refs_3_), channel_id=1, source_target_pairs={{0,16},{1,9},{2,18},{3,11},{4,20},{5,13},{6,22},{7,15},{8,24},{9,1... | collective-permute-start | bytes 393224 | tf_op jit(solution)/shard_map/ppermute | solution.py:55
  40.3 1.7 %collective-permute-start.8 = (bf16[128,512]{1,0:T(8,128)(2,1)S(1)}, bf16[128,512]{1,0:T(8,128)(2,1)S(1)}, u32[]{:S(2)}, u32[]{:S(2)}) collective-permute-start(bf16[128,512]{1,0:T(8,128)(2,1)S(1)} %slice.82.refs_3_), channel_id=1, source_target_pairs={{0,24},{1,17},{2,26},{3,19},{4,28},{5,21},{6,30},{7,23},{8,0},{9,2... | collective-permute-start | bytes 393224 | tf_op jit(solution)/shard_map/ppermute | solution.py:55
  42.1 1.7 %collective-permute-start.13 = (bf16[256,512]{1,0:T(8,128)(2,1)S(1)}, bf16[256,512]{1,0:T(8,128)(2,1)S(1)}, u32[]{:S(2)}, u32[]{:S(2)}) collective-permute-start(bf16[256,512]{1,0:T(8,128)(2,1)S(1)} %broadcast_select_fusion.3.refs_7_), channel_id=1, source_target_pairs={{0,8},{1,9},{2,10},{3,11},{4,12},{5,13},{6,14},{7,15},{8,0},{9,1},... | collective-permute-start | bytes 786440 | tf_op jit(solution)/shard_map/ppermute | solution.py:55
  43.8 1.9 %collective-permute-done.14 = bf16[16,512]{1,0:T(8,128)(2,1)S(1)} collective-permute-done((bf16[16,512]{1,0:T(8,128)(2,1)S(1)}, bf16[16,512]{1,0:T(8,128)(2,1)S(1)}, u32[]{:S(2)}, u32[]{:S(2)}) %collective-permute-start.14) | collective-permute-done | bytes 16416 | tf_op jit(solution)/shard_map/ppermute | solution.py:55
  45.7 5.3 %shard_map.77.refs_9_ = bf16[2,512,2048]{2,1,0:T(8,128)(2,1)S(1)} custom-call(bf16[2,16,512]{2,1,0:T(8,128)(2,1)S(1)} %pad_maximum_fusion.2.pivot_ref.refs_10_, bf16[16,2048]{1,0:T(8,128)(2,1)S(1)} %pad.4.target_ref.refs_11_), custom_call_target="tpu_custom_call" | custom-call | flops 25165824 | bytes 8388608 | tf_op jit(solution)/shard_map/pallas_call | solution.py:107
  51.1 0.2 collective-permute-done.13.refs_8_
  51.3 8.2 %shard_map.78 = (f32[256,2048]{1,0:T(8,128)}, f32[3,8,512]{2,1,0:T(8,128)S(1)}) custom-call(s32[6]{0:T(128)S(1)} %stack.40.info, f32[256,2048]{1,0:T(8,128)S(1)} %copy-done.1, bf16[1024,2048]{1,0:T(8,128)(2,1)S(1)} %bitcast.51, bf16[256,2048]{1,0:T(8,128)(2,1)S(1)} %copy-done.2, bf16[128,512]{1,0:T(8,128)(2,1)S(1)} %slice.82.refs_3_, ...), custom_call_target="tpu_custom_call" | custom-call | flops 3221225472 | bytes 14680064 | tf_op jit(solution)/shard_map/pallas_call | solution.py:172
  59.5 5.3 %collective-permute-start.15 = (f32[3,8,512]{2,1,0:T(8,128)S(1)}, f32[3,8,512]{2,1,0:T(8,128)S(1)}, u32[]{:S(2)}, u32[]{:S(2)}) collective-permute-start(f32[3,8,512]{2,1,0:T(8,128)S(1)} %get-tuple-element.7), channel_id=1, source_target_pairs={{0,1},{1,0},{2,3},{3,2},{4,5},{5,4},{6,7},{7,6},{8,9},{9,8},{10,11... | collective-permute-start | bytes 147464 | tf_op jit(solution)/shard_map/ppermute | solution.py:271
  64.8 0.9 %collective-permute-done.15 = f32[3,8,512]{2,1,0:T(8,128)S(1)} collective-permute-done((f32[3,8,512]{2,1,0:T(8,128)S(1)}, f32[3,8,512]{2,1,0:T(8,128)S(1)}, u32[]{:S(2)}, u32[]{:S(2)}) %collective-permute-start.15) | collective-permute-done | bytes 49184 | tf_op jit(solution)/shard_map/ppermute | solution.py:271
  65.7 3.1 %collective-permute-start.16 = (f32[3,8,512]{2,1,0:T(8,128)S(1)}, f32[3,8,512]{2,1,0:T(8,128)S(1)}, u32[]{:S(2)}, u32[]{:S(2)}) collective-permute-start(f32[3,8,512]{2,1,0:T(8,128)S(1)} %add.67), channel_id=1, source_target_pairs={{0,4},{1,5},{2,6},{3,7},{4,0},{5,1},{6,2},{7,3},{8,12},{9,13},{10,... | collective-permute-start | bytes 147464 | tf_op jit(solution)/shard_map/ppermute | solution.py:272
  68.8 0.4 collective-permute-start.17
  69.2 2.3 %collective-permute-start.18 = (f32[3,8,512]{2,1,0:T(8,128)S(1)}, f32[3,8,512]{2,1,0:T(8,128)S(1)}, u32[]{:S(2)}, u32[]{:S(2)}) collective-permute-start(f32[3,8,512]{2,1,0:T(8,128)S(1)} %add.67), channel_id=1, source_target_pairs={{0,6},{1,7},{2,0},{3,1},{4,2},{5,3},{6,4},{7,5},{8,14},{9,15},{10,... | collective-permute-start | bytes 147464 | tf_op jit(solution)/shard_map/ppermute | solution.py:272
  71.5 1.5 %collective-permute-done.17 = f32[3,8,512]{2,1,0:T(8,128)S(1)} collective-permute-done((f32[3,8,512]{2,1,0:T(8,128)S(1)}, f32[3,8,512]{2,1,0:T(8,128)S(1)}, u32[]{:S(2)}, u32[]{:S(2)}) %collective-permute-start.17) | collective-permute-done | bytes 49184 | tf_op jit(solution)/shard_map/ppermute | solution.py:272
  73.1 0.7 %select_select_fusion.2 = f32[16,3,512]{2,0,1:T(8,128)} fusion(f32[3,512]{1,0:T(4,128)S(1)} %get-tuple-element.28, f32[3,512]{1,0:T(4,128)S(1)} %get-tuple-element.29, f32[3,512]{1,0:T(4,128)S(1)} %get-tuple-element.30, f32[3,512]{1,0:T(4,128)S(1)} %get-tuple-element.31, f32[3,512]{1,0:T(4,128)S(1)} %get-tuple-element.32, ...), kind=kLoop, calls=%fused_computation.24 | loop fusion | flops 172032 | bytes 147568 | tf_op jit(solution)/shard_map/jit(_where)/select_n | solution.py:277
  (49 shorter events, 0.9 us)
Async XLA Ops:
  2.1 9.8 %collective-permute-start = (bf16[256,512]{1,0:T(8,128)(2,1)S(1)}, bf16[256,512]{1,0:T(8,128)(2,1)S(1)}, u32[]{:S(2)}, u32[]{:S(2)}) collective-permute-start(bf16[256,512]{1,0:T(8,128)(2,1)S(1)} %convolution_convert_fusion.1), channel_id=1, source_target_pairs={{0,8},{1,9},{2,10},{3,11},{4,12},{5,13},{6,14},{7,15},{8,0},{9,1},... | collective-permute-start | bytes 786440 | tf_op jit(solution)/shard_map/ppermute | solution.py:55
  5.2 9.8 %collective-permute-start.9 = (bf16[256,512]{1,0:T(8,128)(2,1)S(1)}, bf16[256,512]{1,0:T(8,128)(2,1)S(1)}, u32[]{:S(2)}, u32[]{:S(2)}) collective-permute-start(bf16[256,512]{1,0:T(8,128)(2,1)S(1)} %slice.68), channel_id=1, source_target_pairs={{0,24},{1,161},{2,26},{3,163},{4,28},{5,165},{6,30},{7,167},{8,16}... | collective-permute-start | bytes 786440 | tf_op jit(solution)/shard_map/ppermute | solution.py:55
  13.8 21.0 %copy-start.4 = (bf16[3,2048]{1,0:T(4,128)(2,1)S(1)}, bf16[3,2048]{1,0:T(4,128)(2,1)}, u32[]{:S(2)}) copy-start(bf16[3,2048]{1,0:T(4,128)(2,1)} %param.10) | copy-start | bytes 36868
  13.9 6.9 %collective-permute-start.1 = (bf16[144,512]{1,0:T(8,128)(2,1)S(1)}, bf16[144,512]{1,0:T(8,128)(2,1)S(1)}, u32[]{:S(2)}, u32[]{:S(2)}) collective-permute-start(bf16[144,512]{1,0:T(8,128)(2,1)S(1)} %pad_maximum_fusion.1), channel_id=1, source_target_pairs={{0,24},{1,25},{2,26},{3,27},{4,28},{5,29},{6,30},{7,31},{8,16},{9,... | collective-permute-start | bytes 442376 | tf_op jit(solution)/shard_map/ppermute | solution.py:55
  15.0 9.1 %collective-permute-start.10 = (bf16[256,512]{1,0:T(8,128)(2,1)S(1)}, bf16[256,512]{1,0:T(8,128)(2,1)S(1)}, u32[]{:S(2)}, u32[]{:S(2)}) collective-permute-start(bf16[256,512]{1,0:T(8,128)(2,1)S(1)} %broadcast_select_fusion), channel_id=1, source_target_pairs={{0,96},{1,65},{2,98},{3,67},{4,100},{5,69},{6,102},{7,71},{8,104},... | collective-permute-start | bytes 786440 | tf_op jit(solution)/shard_map/ppermute | solution.py:55
  20.8 6.3 %collective-permute-start.2 = (bf16[144,512]{1,0:T(8,128)(2,1)S(1)}, bf16[144,512]{1,0:T(8,128)(2,1)S(1)}, u32[]{:S(2)}, u32[]{:S(2)}) collective-permute-start(bf16[144,512]{1,0:T(8,128)(2,1)S(1)} %fusion.15), channel_id=1, source_target_pairs={{0,96},{1,97},{2,98},{3,99},{4,100},{5,101},{6,102},{7,103},{8,104... | collective-permute-start | bytes 442376 | tf_op jit(solution)/shard_map/ppermute | solution.py:55
  20.9 6.2 %collective-permute-start.3 = (bf16[144,512]{1,0:T(8,128)(2,1)S(1)}, bf16[144,512]{1,0:T(8,128)(2,1)S(1)}, u32[]{:S(2)}, u32[]{:S(2)}) collective-permute-start(bf16[144,512]{1,0:T(8,128)(2,1)S(1)} %fusion.15), channel_id=1, source_target_pairs={{0,160},{1,161},{2,162},{3,163},{4,164},{5,165},{6,166},{7,167},{8... | collective-permute-start | bytes 442376 | tf_op jit(solution)/shard_map/ppermute | solution.py:55
  24.2 5.1 %copy-start.3 = (bf16[256,512]{1,0:T(8,128)(2,1)}, bf16[256,512]{1,0:T(8,128)(2,1)S(1)}, u32[]{:S(2)}) copy-start(bf16[256,512]{1,0:T(8,128)(2,1)S(1)} %broadcast_select_fusion.1) | copy-start | bytes 786436
  24.2 9.3 %collective-permute-start.11 = (bf16[256,512]{1,0:T(8,128)(2,1)S(1)}, bf16[256,512]{1,0:T(8,128)(2,1)}, u32[]{:S(2)}, u32[]{:S(2)}) collective-permute-start(bf16[256,512]{1,0:T(8,128)(2,1)S(1)} %broadcast_select_fusion.1), channel_id=1, source_target_pairs={{0,192},{1,225},{2,194},{3,227},{4,196},{5,229},{6,198},{7,231},{8... | collective-permute-start | bytes 786440 | tf_op jit(solution)/shard_map/ppermute | solution.py:55
  27.1 24.2 %copy-start.2 = (bf16[256,2048]{1,0:T(8,128)(2,1)S(1)}, bf16[256,2048]{1,0:T(8,128)(2,1)}, u32[]{:S(2)}) copy-start(bf16[256,2048]{1,0:T(8,128)(2,1)} %refs_2_.1) | copy-start | bytes 3145732
  27.8 7.2 %collective-permute-start.4 = (bf16[144,512]{1,0:T(8,128)(2,1)}, bf16[144,512]{1,0:T(8,128)(2,1)}, u32[]{:S(2)}, u32[]{:S(2)}) collective-permute-start(bf16[144,512]{1,0:T(8,128)(2,1)} %select_select_fusion.1), channel_id=1, source_target_pairs={{0,224},{1,225},{2,226},{3,227},{4,228},{5,229},{6,230},{7,231},{8... | collective-permute-start | bytes 442376 | tf_op jit(solution)/shard_map/ppermute | solution.py:55
  27.8 7.3 %collective-permute-start.5 = (bf16[144,512]{1,0:T(8,128)(2,1)}, bf16[144,512]{1,0:T(8,128)(2,1)}, u32[]{:S(2)}, u32[]{:S(2)}) collective-permute-start(bf16[144,512]{1,0:T(8,128)(2,1)} %select_select_fusion.1), channel_id=1, source_target_pairs={{0,32},{1,33},{2,34},{3,35},{4,36},{5,37},{6,38},{7,39},{8,40},{9,... | collective-permute-start | bytes 442376 | tf_op jit(solution)/shard_map/ppermute | solution.py:55
  33.5 17.8 %copy-start.1 = (f32[256,2048]{1,0:T(8,128)S(1)}, f32[256,2048]{1,0:T(8,128)}, u32[]{:S(2)}) copy-start(f32[256,2048]{1,0:T(8,128)} %refs_0_.1) | copy-start | bytes 6291460
  34.7 7.4 %collective-permute-start.12 = (bf16[256,512]{1,0:T(8,128)(2,1)S(1)}, bf16[256,512]{1,0:T(8,128)(2,1)}, u32[]{:S(2)}, u32[]{:S(2)}) collective-permute-start(bf16[256,512]{1,0:T(8,128)(2,1)S(1)} %broadcast_select_fusion.2), channel_id=1, source_target_pairs={{0,32},{1,25},{2,34},{3,27},{4,36},{5,29},{6,38},{7,31},{8,40},{9,... | collective-permute-start | bytes 786440 | tf_op jit(solution)/shard_map/ppermute | solution.py:55
  36.1 15.0 %collective-permute-start.6 = (bf16[128,512]{1,0:T(8,128)(2,1)S(1)}, bf16[128,512]{1,0:T(8,128)(2,1)S(1)}, u32[]{:S(2)}, u32[]{:S(2)}) collective-permute-start(bf16[128,512]{1,0:T(8,128)(2,1)S(1)} %slice.82.refs_3_), channel_id=1, source_target_pairs={{0,8},{1,25},{2,10},{3,27},{4,12},{5,29},{6,14},{7,31},{8,16},{9,1... | collective-permute-start | bytes 393224 | tf_op jit(solution)/shard_map/ppermute | solution.py:55
  38.6 12.4 %collective-permute-start.7 = (bf16[128,512]{1,0:T(8,128)(2,1)S(1)}, bf16[128,512]{1,0:T(8,128)(2,1)S(1)}, u32[]{:S(2)}, u32[]{:S(2)}) collective-permute-start(bf16[128,512]{1,0:T(8,128)(2,1)S(1)} %slice.82.refs_3_), channel_id=1, source_target_pairs={{0,16},{1,9},{2,18},{3,11},{4,20},{5,13},{6,22},{7,15},{8,24},{9,1... | collective-permute-start | bytes 393224 | tf_op jit(solution)/shard_map/ppermute | solution.py:55
  40.3 10.7 %collective-permute-start.8 = (bf16[128,512]{1,0:T(8,128)(2,1)S(1)}, bf16[128,512]{1,0:T(8,128)(2,1)S(1)}, u32[]{:S(2)}, u32[]{:S(2)}) collective-permute-start(bf16[128,512]{1,0:T(8,128)(2,1)S(1)} %slice.82.refs_3_), channel_id=1, source_target_pairs={{0,24},{1,17},{2,26},{3,19},{4,28},{5,21},{6,30},{7,23},{8,0},{9,2... | collective-permute-start | bytes 393224 | tf_op jit(solution)/shard_map/ppermute | solution.py:55
  42.0 3.7 %collective-permute-start.14 = (bf16[16,512]{1,0:T(8,128)(2,1)S(1)}, bf16[16,512]{1,0:T(8,128)(2,1)S(1)}, u32[]{:S(2)}, u32[]{:S(2)}) collective-permute-start(bf16[16,512]{1,0:T(8,128)(2,1)S(1)} %slice.83), channel_id=1, source_target_pairs={{0,8},{1,9},{2,10},{3,11},{4,12},{5,13},{6,14},{7,15},{8,0},{9,1},... | collective-permute-start | bytes 49160 | tf_op jit(solution)/shard_map/ppermute | solution.py:55
  42.1 9.2 %collective-permute-start.13 = (bf16[256,512]{1,0:T(8,128)(2,1)S(1)}, bf16[256,512]{1,0:T(8,128)(2,1)S(1)}, u32[]{:S(2)}, u32[]{:S(2)}) collective-permute-start(bf16[256,512]{1,0:T(8,128)(2,1)S(1)} %broadcast_select_fusion.3.refs_7_), channel_id=1, source_target_pairs={{0,8},{1,9},{2,10},{3,11},{4,12},{5,13},{6,14},{7,15},{8,0},{9,1},... | collective-permute-start | bytes 786440 | tf_op jit(solution)/shard_map/ppermute | solution.py:55
  45.7 5.6 %copy-start = (bf16[2,512,2048]{2,1,0:T(8,128)(2,1)S(1)}, bf16[2,512,2048]{2,1,0:T(8,128)(2,1)}, u32[]{:S(2)}) copy-start(bf16[2,512,2048]{2,1,0:T(8,128)(2,1)} %param.7) | copy-start | bytes 12582916
  51.3 13.5 %copy-start.5 = (s32[16,2]{0,1:T(2,128)S(1)}, s32[16,2]{0,1:T(2,128)}, u32[]{:S(2)}) copy-start(s32[16,2]{0,1:T(2,128)} %param.11) | copy-start | bytes 388
  59.5 6.1 %collective-permute-start.15 = (f32[3,8,512]{2,1,0:T(8,128)S(1)}, f32[3,8,512]{2,1,0:T(8,128)S(1)}, u32[]{:S(2)}, u32[]{:S(2)}) collective-permute-start(f32[3,8,512]{2,1,0:T(8,128)S(1)} %get-tuple-element.7), channel_id=1, source_target_pairs={{0,1},{1,0},{2,3},{3,2},{4,5},{5,4},{6,7},{7,6},{8,9},{9,8},{10,11... | collective-permute-start | bytes 147464 | tf_op jit(solution)/shard_map/ppermute | solution.py:271
  65.7 5.8 %collective-permute-start.16 = (f32[3,8,512]{2,1,0:T(8,128)S(1)}, f32[3,8,512]{2,1,0:T(8,128)S(1)}, u32[]{:S(2)}, u32[]{:S(2)}) collective-permute-start(f32[3,8,512]{2,1,0:T(8,128)S(1)} %add.67), channel_id=1, source_target_pairs={{0,4},{1,5},{2,6},{3,7},{4,0},{5,1},{6,2},{7,3},{8,12},{9,13},{10,... | collective-permute-start | bytes 147464 | tf_op jit(solution)/shard_map/ppermute | solution.py:272
  68.8 4.2 %collective-permute-start.17 = (f32[3,8,512]{2,1,0:T(8,128)S(1)}, f32[3,8,512]{2,1,0:T(8,128)S(1)}, u32[]{:S(2)}, u32[]{:S(2)}) collective-permute-start(f32[3,8,512]{2,1,0:T(8,128)S(1)} %add.67), channel_id=1, source_target_pairs={{0,2},{1,3},{2,4},{3,5},{4,6},{5,7},{6,0},{7,1},{8,10},{9,11},{10,... | collective-permute-start | bytes 147464 | tf_op jit(solution)/shard_map/ppermute | solution.py:272
  69.2 3.8 %collective-permute-start.18 = (f32[3,8,512]{2,1,0:T(8,128)S(1)}, f32[3,8,512]{2,1,0:T(8,128)S(1)}, u32[]{:S(2)}, u32[]{:S(2)}) collective-permute-start(f32[3,8,512]{2,1,0:T(8,128)S(1)} %add.67), channel_id=1, source_target_pairs={{0,6},{1,7},{2,0},{3,1},{4,2},{5,3},{6,4},{7,5},{8,14},{9,15},{10,... | collective-permute-start | bytes 147464 | tf_op jit(solution)/shard_map/ppermute | solution.py:272

commit v3 on v2

v3 whole, which is shorter than its diff:
```python
import math

import jax
import jax.numpy as jnp
from jax import lax
from jax.experimental import pallas as pl
from jax.experimental.pallas import tpu as pltpu
from jax.sharding import PartitionSpec as P

NZ, NX, NY, NC = 8, 4, 4, 2
ROWS, COLS = NZ * NX, NY * NC
NB, SIDES, WIDTH = 512, 256, 2048
QB = WIDTH // NB
HALF = SIDES // 2
CROWS = 16
FAR = 3
BF, F32 = jnp.bfloat16, jnp.float32
VMEM_LIMIT = 15 * 1024 * 1024


def node(z, x):
    return (z % NZ) * NX + x % NX


def shift(dz, dx, zs=range(NZ)):
    return [(node(z, x), node(z + dz, x + dx)) for z in zs for x in range(NX)]


def closed(pairs):
    out, back = dict(pairs), {d: s for s, d in pairs}
    for last in back:
        if last not in dict(pairs):
            first = last
            while first in back:
                first = back[first]
            out[last] = first
    return out


def send(value, pairs0, pairs1=None, idle="core"):
    maps = [closed(pairs0), closed(pairs0 if pairs1 is None else pairs1)]
    flip = 3 if idle == "y3" else 1
    out = {}
    for row in range(ROWS):
        free = [row not in maps[0], row not in maps[1]]
        for y in range(NY):
            for core in range(NC):
                me = row * COLS + y * NC + core
                if not free[core]:
                    out[me] = maps[core][row] * COLS + y * NC + core
                elif all(free) and idle == "core":
                    out[me] = row * COLS + y * NC + 1 - core
                else:
                    out[me] = row * COLS + (y ^ flip) * NC + core
    return lax.ppermute(value, ("row", "col"), sorted(out.items()))


def choose(condition, a, b):
    return lax.select(condition, a, b)


def swap_x(value, partner, zs=range(NZ)):
    return send(value, [(node(z, x), node(z, partner[x])) for z in zs for x in range(NX)])


def along_z(pairs):
    return [(node(a, x), node(b, x)) for a, b in pairs for x in range(NX)]


def spread_z(value, z):
    far = [send(value, along_z(((0, 3),))), send(value, along_z(((0, 5),)))]
    near = [send(value, along_z(((0, 1),))), send(value, along_z(((0, 7),)))]
    relays = choose(z == 3, far[0], choose(z == 5, far[1], value))
    near += [send(relays, along_z(((3, 4), (5, 6)))), send(relays, along_z(((3, 2),)))]
    held = choose(z == 1, near[0], choose(z == 7, near[1], relays))
    return choose((z == 4) | (z == 6), near[2], choose(z == 2, near[3], held))


def gather_x(value, twist):
    return [send(value, shift(0, j), shift(0, (j + twist - 1) % 3 + 1)) for j in (1, 2, 3)]


def moved(j, core, twist):
    return j if j == 0 else jnp.where(core == 0, j, (j + twist - 1) % 3 + 1)


def held(x, core, twist):
    return [(x - moved(j, core, twist)) % NX for j in range(NX)]


def dot(a, b):
    return jnp.dot(a, b, preferred_element_type=F32)


def in_hbm(array):
    return pltpu.with_memory_space_constraint(array, pltpu.HBM)


def halves_kernel(field, coords, first, second):
    for k, out in enumerate((first, second)):
        out[0:HALF, :] = field[k * HALF : (k + 1) * HALF, :]
        out[HALF:, :] = jnp.zeros((CROWS, NB), BF)
        out[HALF : HALF + 3, :] = coords[...]


def halves(field, coords):
    shape = (HALF + CROWS, NB)
    return pl.pallas_call(
        halves_kernel,
        grid=(1,),
        in_specs=[pl.BlockSpec((SIDES, NB), lambda i: (0, 0)), pl.BlockSpec((3, NB), lambda i: (0, 0))],
        out_specs=[pl.BlockSpec(shape, lambda i: (0, 0))] * 2,
        out_shape=[jax.ShapeDtypeStruct(shape, BF)] * 2,
    )(in_hbm(field), in_hbm(coords))


def exact_parts(value):
    high = value.astype(BF).astype(F32)
    middle = (value - high).astype(BF).astype(F32)
    return high, middle, value - high - middle


def lines_of(shape):
    return lax.broadcasted_iota(jnp.int32, shape, 0)


def final_kernel(
    info, source_ref, u_ref, field_ref, p0, p1, p2, p3, target_ref,
    solved_ref, grad_ref, s_ref, f_ref, both_ref, left_ref, right_ref, pivot_ref, near_ref, scale_value,
):
    q = pl.program_id(0)
    row = info[0]

    @pl.when(q == 0)
    def _():
        for j, ref in enumerate((p0, p1, p2, p3)):
            column = info[1 + j]
            a = (column ^ (column >> 1)) & 1
            start = pl.multiple_of((column >> 1) * HALF, HALF)
            s_ref[a, pl.ds(start, HALF), :] = ref[0:HALF, :]
            f_ref[a, pl.ds(start, HALF), :] = ref[HALF:SIDES, :]
            pivot_ref[a] = ref[SIDES:, :].astype(F32)
        for a in range(2):
            both_ref[:, a * NB : (a + 1) * NB] = s_ref[a]
            left_ref[a, :, 0:SIDES] = s_ref[a].T
            left_ref[a, :, SIDES:] = f_ref[a].T
            x = pivot_ref[a]
            line = lines_of(x.shape)
            near = jnp.where(line < 3, x, jnp.where(line < 9, 1.0, 0.0))
            for k, part in enumerate(exact_parts(jnp.sum(x * x, axis=0, keepdims=True))):
                near = jnp.where(line == 3 + k, part, near)
            near_ref[a] = near.T.astype(BF)

    solved_ref[...] = source_ref[...] - dot(both_ref[...], u_ref[...])

    @pl.when((q == 0) & (row < 2))
    def _():
        solved_ref[...] = s_ref[row].astype(F32)

    right_ref[0:SIDES, :] = field_ref[...]
    right_ref[SIDES:, :] = solved_ref[...].astype(BF)
    y = target_ref[...].astype(F32)
    line = lines_of(y.shape)
    far = jnp.where(line < 3, -2.0 * y, jnp.where(line < 6, 1.0, 0.0))
    for k, part in enumerate(exact_parts(jnp.sum(y * y, axis=0, keepdims=True) + 1.0)):
        far = jnp.where(line == 6 + k, part, far)
    far = far.astype(BF)
    target = jnp.where(line == 3, 1.0, y).astype(BF)
    for a in range(2):
        influence = dot(left_ref[a], right_ref[...])
        r = lax.rsqrt(dot(near_ref[a], far))
        weighted = (influence * (r * r * r)).astype(BF)
        sums = lax.dot_general(target, weighted, (((1,), (1,)), ((), ())), preferred_element_type=F32)
        source = pivot_ref[a]
        for c in range(3):
            grad_ref[c, pl.ds(a * QB + q, 1), :] = (
                sums[c : c + 1, :] - source[c : c + 1, :] * sums[3:4, :]
            ) * scale_value


def final(info, source, u_rows, field, parts, targets, scale_value):
    def whole(shape):
        return pl.BlockSpec(shape, lambda q, info: (0,) * len(shape))

    def body(info, *refs):
        final_kernel(info, *refs, scale_value)

    return pl.pallas_call(
        body,
        grid_spec=pltpu.PrefetchScalarGridSpec(
            num_scalar_prefetch=1,
            grid=(QB,),
            in_specs=[
                pl.BlockSpec((SIDES, NB), lambda q, info: (0, q)),
                pl.BlockSpec((2 * NB, NB), lambda q, info: (0, q)),
                pl.BlockSpec((SIDES, NB), lambda q, info: (0, q)),
                *[whole((SIDES + CROWS, NB))] * NX,
                pl.BlockSpec((CROWS, NB), lambda q, info: (0, q)),
            ],
            out_specs=[
                pl.BlockSpec((SIDES, NB), lambda q, info: (0, q)),
                whole((3, 2 * QB, NB)),
            ],
            scratch_shapes=[
                pltpu.VMEM((2, SIDES, NB), BF),
                pltpu.VMEM((2, SIDES, NB), BF),
                pltpu.VMEM((SIDES, 2 * NB), BF),
                pltpu.VMEM((2, NB, 2 * SIDES), BF),
                pltpu.VMEM((2 * SIDES, NB), BF),
                pltpu.VMEM((2, CROWS, NB), F32),
                pltpu.VMEM((2, NB, CROWS), BF),
            ],
        ),
        out_shape=[
            jax.ShapeDtypeStruct((SIDES, WIDTH), F32),
            jax.ShapeDtypeStruct((3, 2 * QB, NB), F32),
        ],
        cost_estimate=pl.CostEstimate(
            flops=4 * SIDES * NB * WIDTH + 8 * SIDES * NB * WIDTH, bytes_accessed=14 * 2**20, transcendentals=0
        ),
        compiler_params=pltpu.CompilerParams(vmem_limit_bytes=VMEM_LIMIT),
    )(info, in_hbm(source), in_hbm(u_rows.reshape(2 * NB, WIDTH)), in_hbm(field), *parts, targets)


def on_device(adjoint_source, u_rows, diag_inverse, forward_field, panel_coords, pair_list):
    row = lax.axis_index("row")
    z, x = row // NX, row % NX
    core = lax.axis_index("col") % NC
    head = adjoint_source[:, 0:NB]

    solve0 = dot(head.astype(BF), diag_inverse[0]).astype(BF)
    at_one = send(solve0, [(node(0, 0), node(0, 1))])

    later_field, later_coords, _ = lax.optimization_barrier((forward_field, panel_coords, solve0))
    first, second = halves(later_field, later_coords)
    fields = choose(x >= 2, swap_x(second, (3, 2, 1, 0), zs=(0,)), first)

    known0 = choose(x == 0, solve0, at_one)
    block1 = (head - dot(known0, u_rows[0, :, 0:NB])).astype(BF)
    solve1 = dot(block1, diag_inverse[1]).astype(BF)

    mine = choose(x == 0, solve0, solve1)
    solves = choose(x >= 2, swap_x(mine[HALF:], (3, 2, 1, 0), zs=(0,)), mine[0:HALF])
    value = jnp.concatenate([solves, fields], axis=0)
    value = spread_z(value, z)
    parts = [value] + gather_x(value, 2)

    coords = jnp.pad(panel_coords, ((0, CROWS - 3), (0, 0)))
    info = jnp.stack([row, *held(x, core, 2), ]).astype(jnp.int32)
    scale_value = 1.0 / math.sqrt(SIDES * COLS)
    solved, table = final(
        info, adjoint_source, u_rows, forward_field, parts, coords, scale_value
    )

    table = table + lax.ppermute(table, "col", [(c, c ^ 1) for c in range(COLS)])
    others = [lax.ppermute(table, "col", [(c, (c + NC * k) % COLS) for c in range(COLS)]) for k in (1, 2, 3)]
    table = (table + others[1]) + (others[0] + others[2])
    slots = (pair_list[:, 0] * QB + pair_list[:, 1] - row * QB)[:, None, None]
    gradient = jnp.broadcast_to(table[:, 0, :][None], (pair_list.shape[0], 3, NB))
    for k in range(1, 2 * QB):
        gradient = jnp.where(slots == k, table[:, k, :][None], gradient)
    return solved, gradient


def solution(mesh):
    return jax.shard_map(
        on_device,
        mesh=mesh,
        in_specs=(P("col", "row"), P(None, None, "row"), P(), P("col", "row"), P(None, "row"), P("row", None)),
        out_specs=(P("col", "row"), P("row", None, None)),
        check_vma=False,
    )
```

time: 74.6 us -> 68.9 us (0.924)
  waiting for transfers between devices: 21.4 us -> 30.4 us
  starting transfers between devices: 28.9 us -> 21.4 us
  other arithmetic: 3.69 us -> 1.01 us
  Pallas kernels: 13.5 us -> 11.4 us
  local copies, waits for them, and re-layouts: 1.88 us -> 0.18 us
    ppermute x15 -> x12, waiting for transfers between devices: 19 us -> 27.7 us  [send(): return lax.ppermute(value, ('row', 'col'), sorted(out.items()))]
    ppermute x1, starting transfers between devices: 5.25 us -> 1.59 us  [on_device(): lax.ppermute(table, 'col', [(c, c ^ 1) for c in range(COLS)])]
    pallas_call x1, Pallas kernels: 5.31 us -> 1.68 us  [halves(): pl.pallas_call(halves_kernel, grid=(1,), in_specs=[pl.BlockSpec((SIDES, N...]
    ppermute x15 -> x12, starting transfers between devices: 17.8 us -> 15.5 us  [send(): return lax.ppermute(value, ('row', 'col'), sorted(out.items()))]
    slice x5 -> x1, local copies, waits for them, and re-layouts: 1.69 us -> 0.01 us  [on_device(): mine[HALF:]]
    pallas_call x1, Pallas kernels: 8.19 us -> 9.75 us  [final(): pl.pallas_call(body, grid_spec=pltpu.PrefetchScalarGridSpec(num_scalar_pr...]
    ppermute x3, starting transfers between devices: 5.79 us -> 4.31 us  [on_device(): lax.ppermute(table, 'col', [(c, (c + NC * k) % COLS) for c in range(COLS)])]
    select_n x3 -> x4, other arithmetic: 1.66 us -> 0.2 us  [choose(): return lax.select(condition, a, b)]
  transfers between devices with their start and end apart: 19 -> 16, of which waited for: 10 -> 11; matrix products, arithmetic and copies ran while one was open for 9% -> 3% of each run, Pallas kernels for 7% -> 2%
where the time goes in v3:
time: 68.9 us; the launch traced here: 68.5 us
  waiting for transfers between devices  30.4 us (44%)
  starting transfers between devices  21.4 us (31%)
  Pallas kernels  11.4 us (17%)
  matrix products  3.32 us (5%)
  other arithmetic  1.01 us (1%)
  between operations  0.86 us (1%)
    ppermute x12, waiting for transfers between devices, send(): return lax.ppermute(value, ('row', 'col'), sorted(out.items()))  27.7 us
    ppermute x12, starting transfers between devices, send(): return lax.ppermute(value, ('row', 'col'), sorted(out.items()))  15.5 us
    pallas_call x1, Pallas kernels, final(): pl.pallas_call(body, grid_spec=pltpu.PrefetchScalarGridSpec(num_scalar_pr...  9.75 us
    ppermute x3, starting transfers between devices, on_device(): lax.ppermute(table, 'col', [(c, (c + NC * k) % COLS) for c in range(COLS)])  4.31 us
    dot_general x2, matrix products, dot(): return jnp.dot(a, b, preferred_element_type=F32)  3.32 us
    ppermute x3, waiting for transfers between devices, on_device(): lax.ppermute(table, 'col', [(c, (c + NC * k) % COLS) for c in range(COLS)])  1.76 us
    pallas_call x1, Pallas kernels, halves(): pl.pallas_call(halves_kernel, grid=(1,), in_specs=[pl.BlockSpec((SIDES, N...  1.68 us
    ppermute x1, starting transfers between devices, on_device(): lax.ppermute(table, 'col', [(c, c ^ 1) for c in range(COLS)])  1.59 us
  transfers between devices with their start and end apart: 16, of which 11 were waited for; matrix products, arithmetic and copies ran while one was open for 3% of the time, Pallas kernels for 2%

profile of v3, /device:TPU:1, one launch (start us, length us, event | category | flops | bytes accessed | tf_op | source)
XLA Modules:
  0.0 68.5 jit_solution(8825660453784247712)
XLA Ops:
  0.6 1.6 %convolution_convert_fusion.1 = bf16[256,512]{1,0:T(8,128)(2,1)S(1)} fusion(bf16[2,512,512]{2,1,0:T(8,128)(2,1)} %param.8, f32[256,2048]{1,0:T(8,128)} %refs_0_.1), kind=kOutput, calls=%fused_computation.3 | convolution fusion | flops 134348800 | bytes 1048576 | tf_op jit(solution)/shard_map/dot_general | solution.py:92
  2.2 2.1 %collective-permute-start = (bf16[256,512]{1,0:T(8,128)(2,1)S(1)}, bf16[256,512]{1,0:T(8,128)(2,1)S(1)}, u32[]{:S(2)}, u32[]{:S(2)}) collective-permute-start(bf16[256,512]{1,0:T(8,128)(2,1)S(1)} %convolution_convert_fusion.1), channel_id=1, source_target_pairs={{0,8},{1,9},{2,10},{3,11},{4,12},{5,13},{6,14},{7,15},{8,0},{9,1},... | collective-permute-start | bytes 786440 | tf_op jit(solution)/shard_map/ppermute | solution.py:55
  4.4 1.7 %shard_map.77 = (bf16[144,512]{1,0:T(8,128)(2,1)}, bf16[144,512]{1,0:T(8,128)(2,1)}) custom-call(bf16[256,2048]{1,0:T(8,128)(2,1)} %refs_2_.1, bf16[3,2048]{1,0:T(4,128)(2,1)} %coords), custom_call_target="tpu_custom_call" | custom-call | tf_op jit(solution)/shard_map/pallas_call | solution.py:108
  6.0 1.9 %collective-permute-start.2 = (bf16[144,512]{1,0:T(8,128)(2,1)}, bf16[144,512]{1,0:T(8,128)(2,1)S(1)}, u32[]{:S(2)}, u32[]{:S(2)}) collective-permute-start(bf16[144,512]{1,0:T(8,128)(2,1)} %get-tuple-element.10), channel_id=1, source_target_pairs={{0,24},{1,25},{2,26},{3,27},{4,28},{5,29},{6,30},{7,31},{8,16},{9,... | collective-permute-start | bytes 442376 | tf_op jit(solution)/shard_map/ppermute | solution.py:55
  8.0 1.1 %collective-permute-done = bf16[256,512]{1,0:T(8,128)(2,1)S(1)} collective-permute-done((bf16[256,512]{1,0:T(8,128)(2,1)S(1)}, bf16[256,512]{1,0:T(8,128)(2,1)S(1)}, u32[]{:S(2)}, u32[]{:S(2)}) %collective-permute-start) | collective-permute-done | bytes 262176 | tf_op jit(solution)/shard_map/ppermute | solution.py:55
  9.1 1.7 %fusion.1 = bf16[256,512]{1,0:T(8,128)(2,1)S(1)} fusion(bf16[256,512]{1,0:T(8,128)(2,1)S(1)} %convolution_convert_fusion.1, bf16[2,512,512]{2,1,0:T(8,128)(2,1)S(1)} %copy-done, bf16[2,512,2048]{2,1,0:T(8,128)(2,1)} %param.7, f32[256,2048]{1,0:T(8,128)} %refs_0_.1, bf16[256,512]{1,0:T(8,128)(2,1)S(1)} %collective-permute-done, pred[]{:T(512)S(6)} %eq.118), kind=kOutput, calls=%fused_computation.4 | convolution fusion | flops 269090816 | bytes 2622464 | tf_op jit(solution)/shard_map/dot_general | solution.py:92
  10.8 0.1 collective-permute-start.1
  10.9 0.7 collective-permute-done.2
  11.6 4.3 %collective-permute-done.1 = bf16[128,512]{1,0:T(8,128)(2,1)S(1)} collective-permute-done((bf16[128,512]{1,0:T(8,128)(2,1)S(1)}, bf16[128,512]{1,0:T(8,128)(2,1)S(1)}, u32[]{:S(2)}, u32[]{:S(2)}) %collective-permute-start.1) | collective-permute-done | bytes 131104 | tf_op jit(solution)/shard_map/ppermute | solution.py:55
  16.0 0.1 collective-permute-start.3
  16.1 0.1 collective-permute-start.4
  16.2 0.1 collective-permute-start.7
  16.3 0.1 collective-permute-start.8
  16.4 7.0 %collective-permute-done.3 = bf16[272,512]{1,0:T(8,128)(2,1)S(1)} collective-permute-done((bf16[272,512]{1,0:T(8,128)(2,1)S(1)}, bf16[272,512]{1,0:T(8,128)(2,1)S(1)}, u32[]{:S(2)}, u32[]{:S(2)}) %collective-permute-start.3) | collective-permute-done | bytes 278560 | tf_op jit(solution)/shard_map/ppermute | solution.py:55
  23.4 1.3 %collective-permute-done.4 = bf16[272,512]{1,0:T(8,128)(2,1)S(1)} collective-permute-done((bf16[272,512]{1,0:T(8,128)(2,1)S(1)}, bf16[272,512]{1,0:T(8,128)(2,1)S(1)}, u32[]{:S(2)}, u32[]{:S(2)}) %collective-permute-start.4) | collective-permute-done | bytes 278560 | tf_op jit(solution)/shard_map/ppermute | solution.py:55
  24.7 0.1 select_select_fusion.1
  24.8 8.1 %collective-permute-start.5 = (bf16[272,512]{1,0:T(8,128)(2,1)S(1)}, bf16[272,512]{1,0:T(8,128)(2,1)S(1)}, u32[]{:S(2)}, u32[]{:S(2)}) collective-permute-start(bf16[272,512]{1,0:T(8,128)(2,1)S(1)} %select_select_fusion.1), channel_id=1, source_target_pairs={{0,1},{1,0},{2,3},{3,2},{4,5},{5,4},{6,7},{7,6},{8,9},{9,8},{10,11... | collective-permute-start | bytes 835592 | tf_op jit(solution)/shard_map/ppermute | solution.py:55
  32.9 0.1 collective-permute-start.6
  33.0 1.1 %collective-permute-done.5 = bf16[272,512]{1,0:T(8,128)(2,1)S(1)} collective-permute-done((bf16[272,512]{1,0:T(8,128)(2,1)S(1)}, bf16[272,512]{1,0:T(8,128)(2,1)S(1)}, u32[]{:S(2)}, u32[]{:S(2)}) %collective-permute-start.5) | collective-permute-done | bytes 278560 | tf_op jit(solution)/shard_map/ppermute | solution.py:55
  34.1 0.4 collective-permute-done.6
  34.6 0.6 collective-permute-start.11
  35.3 2.0 %collective-permute-start.9 = (bf16[272,512]{1,0:T(8,128)(2,1)S(1)}, bf16[272,512]{1,0:T(8,128)(2,1)S(1)}, u32[]{:S(2)}, u32[]{:S(2)}) collective-permute-start(bf16[272,512]{1,0:T(8,128)(2,1)S(1)} %select_select_fusion.refs_3_), channel_id=1, source_target_pairs={{0,8},{1,25},{2,10},{3,27},{4,12},{5,29},{6,14},{7,31},{8,16},{9,1... | collective-permute-start | bytes 835592 | tf_op jit(solution)/shard_map/ppermute | solution.py:55
  37.4 11.9 %collective-permute-done.10.refs_5_ = bf16[272,512]{1,0:T(8,128)(2,1)S(1)} collective-permute-done((bf16[272,512]{1,0:T(8,128)(2,1)S(1)}, bf16[272,512]{1,0:T(8,128)(2,1)S(1)}, u32[]{:S(2)}, u32[]{:S(2)}) %collective-permute-start.10) | collective-permute-done | bytes 278560 | tf_op jit(solution)/shard_map/ppermute | solution.py:55
  49.4 9.8 %shard_map.78 = (f32[256,2048]{1,0:T(8,128)}, f32[3,8,512]{2,1,0:T(8,128)S(1)}) custom-call(s32[5]{0:T(128)S(1)} %stack.23.info, f32[256,2048]{1,0:T(8,128)} %refs_0_.1, bf16[1024,2048]{1,0:T(8,128)(2,1)} %bitcast.46, bf16[256,2048]{1,0:T(8,128)(2,1)} %refs_2_.1, bf16[272,512]{1,0:T(8,128)(2,1)S(1)} %select_select_fusion.refs_3_, ...), custom_call_target="tpu_custom_call" | custom-call | flops 3221225472 | bytes 14680064 | tf_op jit(solution)/shard_map/pallas_call | solution.py:188
  59.1 1.6 %collective-permute-start.12 = (f32[3,8,512]{2,1,0:T(8,128)S(1)}, f32[3,8,512]{2,1,0:T(8,128)S(1)}, u32[]{:S(2)}, u32[]{:S(2)}) collective-permute-start(f32[3,8,512]{2,1,0:T(8,128)S(1)} %get-tuple-element.13), channel_id=1, source_target_pairs={{0,1},{1,0},{2,3},{3,2},{4,5},{5,4},{6,7},{7,6},{8,9},{9,8},{10,11... | collective-permute-start | bytes 147464 | tf_op jit(solution)/shard_map/ppermute | solution.py:255
  60.7 0.9 %collective-permute-done.12 = f32[3,8,512]{2,1,0:T(8,128)S(1)} collective-permute-done((f32[3,8,512]{2,1,0:T(8,128)S(1)}, f32[3,8,512]{2,1,0:T(8,128)S(1)}, u32[]{:S(2)}, u32[]{:S(2)}) %collective-permute-start.12) | collective-permute-done | bytes 49184 | tf_op jit(solution)/shard_map/ppermute | solution.py:255
  61.6 1.6 %collective-permute-start.13 = (f32[3,8,512]{2,1,0:T(8,128)S(1)}, f32[3,8,512]{2,1,0:T(8,128)S(1)}, u32[]{:S(2)}, u32[]{:S(2)}) collective-permute-start(f32[3,8,512]{2,1,0:T(8,128)S(1)} %add.67), channel_id=1, source_target_pairs={{0,4},{1,5},{2,6},{3,7},{4,0},{5,1},{6,2},{7,3},{8,12},{9,13},{10,... | collective-permute-start | bytes 147464 | tf_op jit(solution)/shard_map/ppermute | solution.py:256
  63.2 0.4 collective-permute-start.14
  63.6 2.3 %collective-permute-start.15 = (f32[3,8,512]{2,1,0:T(8,128)S(1)}, f32[3,8,512]{2,1,0:T(8,128)S(1)}, u32[]{:S(2)}, u32[]{:S(2)}) collective-permute-start(f32[3,8,512]{2,1,0:T(8,128)S(1)} %add.67), channel_id=1, source_target_pairs={{0,6},{1,7},{2,0},{3,1},{4,2},{5,3},{6,4},{7,5},{8,14},{9,15},{10,... | collective-permute-start | bytes 147464 | tf_op jit(solution)/shard_map/ppermute | solution.py:256
  65.9 0.2 collective-permute-done.13
  66.1 1.6 %collective-permute-done.14 = f32[3,8,512]{2,1,0:T(8,128)S(1)} collective-permute-done((f32[3,8,512]{2,1,0:T(8,128)S(1)}, f32[3,8,512]{2,1,0:T(8,128)S(1)}, u32[]{:S(2)}, u32[]{:S(2)}) %collective-permute-start.14) | collective-permute-done | bytes 49184 | tf_op jit(solution)/shard_map/ppermute | solution.py:256
  67.8 0.7 %select_select_fusion.2 = f32[16,3,512]{2,0,1:T(8,128)} fusion(f32[3,512]{1,0:T(4,128)S(1)} %get-tuple-element.30, f32[3,512]{1,0:T(4,128)S(1)} %get-tuple-element.31, f32[3,512]{1,0:T(4,128)S(1)} %get-tuple-element.32, f32[3,512]{1,0:T(4,128)S(1)} %get-tuple-element.33, f32[3,512]{1,0:T(4,128)S(1)} %get-tuple-element.34, ...), kind=kLoop, calls=%fused_computation.20 | loop fusion | flops 172032 | bytes 147568 | tf_op jit(solution)/shard_map/jit(_where)/select_n | solution.py:261
  (30 shorter events, 0.4 us)
Async XLA Ops:
  0.6 8.4 %copy-start = (bf16[2,512,512]{2,1,0:T(8,128)(2,1)S(1)}, bf16[2,512,512]{2,1,0:T(8,128)(2,1)}, u32[]{:S(2)}) copy-start(bf16[2,512,512]{2,1,0:T(8,128)(2,1)} %param.8) | copy-start | bytes 3145732
  2.2 6.8 %collective-permute-start = (bf16[256,512]{1,0:T(8,128)(2,1)S(1)}, bf16[256,512]{1,0:T(8,128)(2,1)S(1)}, u32[]{:S(2)}, u32[]{:S(2)}) collective-permute-start(bf16[256,512]{1,0:T(8,128)(2,1)S(1)} %convolution_convert_fusion.1), channel_id=1, source_target_pairs={{0,8},{1,9},{2,10},{3,11},{4,12},{5,13},{6,14},{7,15},{8,0},{9,1},... | collective-permute-start | bytes 786440 | tf_op jit(solution)/shard_map/ppermute | solution.py:55
  6.0 5.5 %copy-start.1 = (bf16[144,512]{1,0:T(8,128)(2,1)S(1)}, bf16[144,512]{1,0:T(8,128)(2,1)}, u32[]{:S(2)}) copy-start(bf16[144,512]{1,0:T(8,128)(2,1)} %get-tuple-element.11) | copy-start | bytes 442372
  6.0 5.5 %collective-permute-start.2 = (bf16[144,512]{1,0:T(8,128)(2,1)}, bf16[144,512]{1,0:T(8,128)(2,1)S(1)}, u32[]{:S(2)}, u32[]{:S(2)}) collective-permute-start(bf16[144,512]{1,0:T(8,128)(2,1)} %get-tuple-element.10), channel_id=1, source_target_pairs={{0,24},{1,25},{2,26},{3,27},{4,28},{5,29},{6,30},{7,31},{8,16},{9,... | collective-permute-start | bytes 442376 | tf_op jit(solution)/shard_map/ppermute | solution.py:55
  10.8 5.1 %collective-permute-start.1 = (bf16[128,512]{1,0:T(8,128)(2,1)S(1)}, bf16[128,512]{1,0:T(8,128)(2,1)S(1)}, u32[]{:S(2)}, u32[]{:S(2)}) collective-permute-start(bf16[128,512]{1,0:T(8,128)(2,1)S(1)} %slice.64), channel_id=1, source_target_pairs={{0,24},{1,25},{2,26},{3,27},{4,28},{5,29},{6,30},{7,31},{8,16},{9,... | collective-permute-start | bytes 393224 | tf_op jit(solution)/shard_map/ppermute | solution.py:55
  11.6 25.7 %copy-start.2 = (bf16[3,2048]{1,0:T(4,128)(2,1)S(1)}, bf16[3,2048]{1,0:T(4,128)(2,1)}, u32[]{:S(2)}) copy-start(bf16[3,2048]{1,0:T(4,128)(2,1)} %coords) | copy-start | bytes 36868
  16.0 7.4 %collective-permute-start.3 = (bf16[272,512]{1,0:T(8,128)(2,1)S(1)}, bf16[272,512]{1,0:T(8,128)(2,1)S(1)}, u32[]{:S(2)}, u32[]{:S(2)}) collective-permute-start(bf16[272,512]{1,0:T(8,128)(2,1)S(1)} %pad_maximum_fusion), channel_id=1, source_target_pairs={{0,96},{1,97},{2,98},{3,99},{4,100},{5,101},{6,102},{7,103},{8,104... | collective-permute-start | bytes 835592 | tf_op jit(solution)/shard_map/ppermute | solution.py:55
  16.1 8.6 %collective-permute-start.4 = (bf16[272,512]{1,0:T(8,128)(2,1)S(1)}, bf16[272,512]{1,0:T(8,128)(2,1)S(1)}, u32[]{:S(2)}, u32[]{:S(2)}) collective-permute-start(bf16[272,512]{1,0:T(8,128)(2,1)S(1)} %pad_maximum_fusion), channel_id=1, source_target_pairs={{0,160},{1,161},{2,162},{3,163},{4,164},{5,165},{6,166},{7,167},{8... | collective-permute-start | bytes 835592 | tf_op jit(solution)/shard_map/ppermute | solution.py:55
  16.2 16.8 %collective-permute-start.7 = (bf16[272,512]{1,0:T(8,128)(2,1)S(1)}, bf16[272,512]{1,0:T(8,128)(2,1)S(1)}, u32[]{:S(2)}, u32[]{:S(2)}) collective-permute-start(bf16[272,512]{1,0:T(8,128)(2,1)S(1)} %pad_maximum_fusion), channel_id=1, source_target_pairs={{0,32},{1,33},{2,34},{3,35},{4,36},{5,37},{6,38},{7,39},{8,40},{9,... | collective-permute-start | bytes 835592 | tf_op jit(solution)/shard_map/ppermute | solution.py:55
  16.3 16.7 %collective-permute-start.8 = (bf16[272,512]{1,0:T(8,128)(2,1)S(1)}, bf16[272,512]{1,0:T(8,128)(2,1)S(1)}, u32[]{:S(2)}, u32[]{:S(2)}) collective-permute-start(bf16[272,512]{1,0:T(8,128)(2,1)S(1)} %pad_maximum_fusion), channel_id=1, source_target_pairs={{0,224},{1,225},{2,226},{3,227},{4,228},{5,229},{6,230},{7,231},{8... | collective-permute-start | bytes 835592 | tf_op jit(solution)/shard_map/ppermute | solution.py:55
  24.8 9.3 %collective-permute-start.5 = (bf16[272,512]{1,0:T(8,128)(2,1)S(1)}, bf16[272,512]{1,0:T(8,128)(2,1)S(1)}, u32[]{:S(2)}, u32[]{:S(2)}) collective-permute-start(bf16[272,512]{1,0:T(8,128)(2,1)S(1)} %select_select_fusion.1), channel_id=1, source_target_pairs={{0,1},{1,0},{2,3},{3,2},{4,5},{5,4},{6,7},{7,6},{8,9},{9,8},{10,11... | collective-permute-start | bytes 835592 | tf_op jit(solution)/shard_map/ppermute | solution.py:55
  32.9 1.6 %collective-permute-start.6 = (bf16[272,512]{1,0:T(8,128)(2,1)S(1)}, bf16[272,512]{1,0:T(8,128)(2,1)S(1)}, u32[]{:S(2)}, u32[]{:S(2)}) collective-permute-start(bf16[272,512]{1,0:T(8,128)(2,1)S(1)} %select_select_fusion.1), channel_id=1, source_target_pairs={{0,1},{1,0},{2,3},{3,2},{4,5},{5,4},{6,7},{7,6},{8,9},{9,8},{10,11... | collective-permute-start | bytes 835592 | tf_op jit(solution)/shard_map/ppermute | solution.py:55
  34.5 14.8 %collective-permute-start.10 = (bf16[272,512]{1,0:T(8,128)(2,1)S(1)}, bf16[272,512]{1,0:T(8,128)(2,1)S(1)}, u32[]{:S(2)}, u32[]{:S(2)}) collective-permute-start(bf16[272,512]{1,0:T(8,128)(2,1)S(1)} %select_select_fusion.refs_3_), channel_id=1, source_target_pairs={{0,16},{1,9},{2,18},{3,11},{4,20},{5,13},{6,22},{7,15},{8,24},{9,1... | collective-permute-start | bytes 835592 | tf_op jit(solution)/shard_map/ppermute | solution.py:55
  34.6 14.7 %collective-permute-start.11 = (bf16[272,512]{1,0:T(8,128)(2,1)S(1)}, bf16[272,512]{1,0:T(8,128)(2,1)S(1)}, u32[]{:S(2)}, u32[]{:S(2)}) collective-permute-start(bf16[272,512]{1,0:T(8,128)(2,1)S(1)} %select_select_fusion.refs_3_), channel_id=1, source_target_pairs={{0,24},{1,17},{2,26},{3,19},{4,28},{5,21},{6,30},{7,23},{8,0},{9,2... | collective-permute-start | bytes 835592 | tf_op jit(solution)/shard_map/ppermute | solution.py:55
  35.3 14.1 %collective-permute-start.9 = (bf16[272,512]{1,0:T(8,128)(2,1)S(1)}, bf16[272,512]{1,0:T(8,128)(2,1)S(1)}, u32[]{:S(2)}, u32[]{:S(2)}) collective-permute-start(bf16[272,512]{1,0:T(8,128)(2,1)S(1)} %select_select_fusion.refs_3_), channel_id=1, source_target_pairs={{0,8},{1,25},{2,10},{3,27},{4,12},{5,29},{6,14},{7,31},{8,16},{9,1... | collective-permute-start | bytes 835592 | tf_op jit(solution)/shard_map/ppermute | solution.py:55
  49.3 11.4 %copy-start.3 = (s32[16,2]{0,1:T(2,128)S(1)}, s32[16,2]{0,1:T(2,128)}, u32[]{:S(2)}) copy-start(s32[16,2]{0,1:T(2,128)} %param.11) | copy-start | bytes 388
  59.1 2.5 %collective-permute-start.12 = (f32[3,8,512]{2,1,0:T(8,128)S(1)}, f32[3,8,512]{2,1,0:T(8,128)S(1)}, u32[]{:S(2)}, u32[]{:S(2)}) collective-permute-start(f32[3,8,512]{2,1,0:T(8,128)S(1)} %get-tuple-element.13), channel_id=1, source_target_pairs={{0,1},{1,0},{2,3},{3,2},{4,5},{5,4},{6,7},{7,6},{8,9},{9,8},{10,11... | collective-permute-start | bytes 147464 | tf_op jit(solution)/shard_map/ppermute | solution.py:255
  61.6 4.5 %collective-permute-start.13 = (f32[3,8,512]{2,1,0:T(8,128)S(1)}, f32[3,8,512]{2,1,0:T(8,128)S(1)}, u32[]{:S(2)}, u32[]{:S(2)}) collective-permute-start(f32[3,8,512]{2,1,0:T(8,128)S(1)} %add.67), channel_id=1, source_target_pairs={{0,4},{1,5},{2,6},{3,7},{4,0},{5,1},{6,2},{7,3},{8,12},{9,13},{10,... | collective-permute-start | bytes 147464 | tf_op jit(solution)/shard_map/ppermute | solution.py:256
  63.2 4.4 %collective-permute-start.14 = (f32[3,8,512]{2,1,0:T(8,128)S(1)}, f32[3,8,512]{2,1,0:T(8,128)S(1)}, u32[]{:S(2)}, u32[]{:S(2)}) collective-permute-start(f32[3,8,512]{2,1,0:T(8,128)S(1)} %add.67), channel_id=1, source_target_pairs={{0,2},{1,3},{2,4},{3,5},{4,6},{5,7},{6,0},{7,1},{8,10},{9,11},{10,... | collective-permute-start | bytes 147464 | tf_op jit(solution)/shard_map/ppermute | solution.py:256
  63.6 4.0 %collective-permute-start.15 = (f32[3,8,512]{2,1,0:T(8,128)S(1)}, f32[3,8,512]{2,1,0:T(8,128)S(1)}, u32[]{:S(2)}, u32[]{:S(2)}) collective-permute-start(f32[3,8,512]{2,1,0:T(8,128)S(1)} %add.67), channel_id=1, source_target_pairs={{0,6},{1,7},{2,0},{3,1},{4,2},{5,3},{6,4},{7,5},{8,14},{9,15},{10,... | collective-permute-start | bytes 147464 | tf_op jit(solution)/shard_map/ppermute | solution.py:256

commit v4 on v3

--- a/solution.py
+++ b/solution.py
@@ -15,7 +15,8 @@
 CROWS = 16
 FAR = 3
 BF, F32 = jnp.bfloat16, jnp.float32
-VMEM_LIMIT = 15 * 1024 * 1024
+UNROLL = 4
+VMEM_LIMIT = 28 * 1024 * 1024
 
 
 def node(z, x):
@@ -128,10 +129,10 @@
     info, source_ref, u_ref, field_ref, p0, p1, p2, p3, target_ref,
     solved_ref, grad_ref, s_ref, f_ref, both_ref, left_ref, right_ref, pivot_ref, near_ref, scale_value,
 ):
-    q = pl.program_id(0)
+    step = pl.program_id(0)
     row = info[0]
 
-    @pl.when(q == 0)
+    @pl.when(step == 0)
     def _():
         for j, ref in enumerate((p0, p1, p2, p3)):
             column = info[1 + j]
@@ -151,31 +152,57 @@
                 near = jnp.where(line == 3 + k, part, near)
             near_ref[a] = near.T.astype(BF)
 
-    solved_ref[...] = source_ref[...] - dot(both_ref[...], u_ref[...])
-
-    @pl.when((q == 0) & (row < 2))
+    for sub in range(UNROLL):
+        here = slice(sub * NB, (sub + 1) * NB)
+        block = pl.ds(pl.multiple_of(step * UNROLL * NB + sub * NB, NB), NB)
+        solved_ref[:, here] = source_ref[:, block] - dot(both_ref[...], u_ref[:, block])
+
+    @pl.when((step == 0) & (row < 2))
     def _():
-        solved_ref[...] = s_ref[row].astype(F32)
-
-    right_ref[0:SIDES, :] = field_ref[...]
-    right_ref[SIDES:, :] = solved_ref[...].astype(BF)
-    y = target_ref[...].astype(F32)
+        solved_ref[:, 0:NB] = s_ref[row].astype(F32)
+
+    for sub in range(UNROLL):
+        final_block(step * UNROLL + sub, sub, solved_ref, field_ref, target_ref, grad_ref, left_ref, right_ref.at[sub], pivot_ref, near_ref, scale_value)
+
+
+def final_block(q, sub, solved_ref, field_ref, target_ref, grad_ref, left_ref, right_ref, pivot_ref, near_ref, scale_value):
+    block = pl.ds(pl.multiple_of(q * NB, NB), NB)
+    right_ref[0:SIDES, :] = field_ref[:, block]
+    right_ref[SIDES:, :] = solved_ref[:, sub * NB : (sub + 1) * NB].astype(BF)
+    y = target_ref[:, block].astype(F32)
     line = lines_of(y.shape)
     far = jnp.where(line < 3, -2.0 * y, jnp.where(line < 6, 1.0, 0.0))
     for k, part in enumerate(exact_parts(jnp.sum(y * y, axis=0, keepdims=True) + 1.0)):
         far = jnp.where(line == 6 + k, part, far)
     far = far.astype(BF)
     target = jnp.where(line == 3, 1.0, y).astype(BF)
+    influence = dot(left_ref[...].reshape(2 * NB, 2 * SIDES), right_ref[...])
+    r = lax.rsqrt(dot(near_ref[...].reshape(2 * NB, CROWS), far))
+    weighted = (influence * (r * r * r)).astype(BF)
+    sums = lax.dot_general(target, weighted, (((1,), (1,)), ((), ())), preferred_element_type=F32) * scale_value
     for a in range(2):
-        influence = dot(left_ref[a], right_ref[...])
-        r = lax.rsqrt(dot(near_ref[a], far))
-        weighted = (influence * (r * r * r)).astype(BF)
-        sums = lax.dot_general(target, weighted, (((1,), (1,)), ((), ())), preferred_element_type=F32)
+        here = sums[:, a * NB : (a + 1) * NB]
         source = pivot_ref[a]
         for c in range(3):
-            grad_ref[c, pl.ds(a * QB + q, 1), :] = (
-                sums[c : c + 1, :] - source[c : c + 1, :] * sums[3:4, :]
-            ) * scale_value
+            grad_ref[c, pl.ds(a * QB + q, 1), :] = here[c : c + 1, :] - source[c : c + 1, :] * here[3:4, :]
+
+
+def load_kernel(*refs):
+    for k in range(len(refs) // 2):
+        refs[len(refs) // 2 + k][...] = refs[k][...]
+
+
+def load(*arrays):
+    blocks = [pl.BlockSpec((array.shape[0], NB), lambda q: (0, q)) for array in arrays]
+    return pl.pallas_call(
+        load_kernel,
+        grid=(QB,),
+        in_specs=blocks,
+        out_specs=blocks,
+        out_shape=[jax.ShapeDtypeStruct(array.shape, array.dtype) for array in arrays],
+        cost_estimate=pl.CostEstimate(flops=0, bytes_accessed=14 * 2**20, transcendentals=0),
+        compiler_params=pltpu.CompilerParams(vmem_limit_bytes=VMEM_LIMIT),
+    )(*[in_hbm(array) for array in arrays])
 
 
 def final(info, source, u_rows, field, parts, targets, scale_value):
@@ -189,16 +216,10 @@
         body,
         grid_spec=pltpu.PrefetchScalarGridSpec(
             num_scalar_prefetch=1,
-            grid=(QB,),
-            in_specs=[
-                pl.BlockSpec((SIDES, NB), lambda q, info: (0, q)),
-                pl.BlockSpec((2 * NB, NB), lambda q, info: (0, q)),
-                pl.BlockSpec((SIDES, NB), lambda q, info: (0, q)),
-                *[whole((SIDES + CROWS, NB))] * NX,
-                pl.BlockSpec((CROWS, NB), lambda q, info: (0, q)),
-            ],
+            grid=(QB // UNROLL,),
+            in_specs=[pl.BlockSpec(memory_space=pltpu.VMEM)] * (4 + NX),
             out_specs=[
-                pl.BlockSpec((SIDES, NB), lambda q, info: (0, q)),
+                pl.BlockSpec((SIDES, UNROLL * NB), lambda q, info: (0, q)),
                 whole((3, 2 * QB, NB)),
             ],
             scratch_shapes=[
@@ -206,7 +227,7 @@
                 pltpu.VMEM((2, SIDES, NB), BF),
                 pltpu.VMEM((SIDES, 2 * NB), BF),
                 pltpu.VMEM((2, NB, 2 * SIDES), BF),
-                pltpu.VMEM((2 * SIDES, NB), BF),
+                pltpu.VMEM((UNROLL, 2 * SIDES, NB), BF),
                 pltpu.VMEM((2, CROWS, NB), F32),
                 pltpu.VMEM((2, NB, CROWS), BF),
             ],
@@ -219,7 +240,7 @@
             flops=4 * SIDES * NB * WIDTH + 8 * SIDES * NB * WIDTH, bytes_accessed=14 * 2**20, transcendentals=0
         ),
         compiler_params=pltpu.CompilerParams(vmem_limit_bytes=VMEM_LIMIT),
-    )(info, in_hbm(source), in_hbm(u_rows.reshape(2 * NB, WIDTH)), in_hbm(field), *parts, targets)
+    )(info, source, u_rows, field, *parts, targets)
 
 
 def on_device(adjoint_source, u_rows, diag_inverse, forward_field, panel_coords, pair_list):
@@ -235,26 +256,33 @@
     first, second = halves(later_field, later_coords)
     fields = choose(x >= 2, swap_x(second, (3, 2, 1, 0), zs=(0,)), first)
 
+    own_head, own_factor, _ = lax.optimization_barrier((head, u_rows[0, :, 0:NB], solve0))
     known0 = choose(x == 0, solve0, at_one)
-    block1 = (head - dot(known0, u_rows[0, :, 0:NB])).astype(BF)
+    block1 = (own_head - dot(known0, own_factor)).astype(BF)
     solve1 = dot(block1, diag_inverse[1]).astype(BF)
 
     mine = choose(x == 0, solve0, solve1)
     solves = choose(x >= 2, swap_x(mine[HALF:], (3, 2, 1, 0), zs=(0,)), mine[0:HALF])
     value = jnp.concatenate([solves, fields], axis=0)
     value = spread_z(value, z)
+    source, factors, field, value = lax.optimization_barrier(
+        (adjoint_source, u_rows.reshape(2 * NB, WIDTH), forward_field, value)
+    )
+    loaded = load(source, factors, field)
     parts = [value] + gather_x(value, 2)
 
     coords = jnp.pad(panel_coords, ((0, CROWS - 3), (0, 0)))
     info = jnp.stack([row, *held(x, core, 2), ]).astype(jnp.int32)
     scale_value = 1.0 / math.sqrt(SIDES * COLS)
     solved, table = final(
-        info, adjoint_source, u_rows, forward_field, parts, coords, scale_value
+        info, *loaded, parts, coords, scale_value
     )
 
     table = table + lax.ppermute(table, "col", [(c, c ^ 1) for c in range(COLS)])
-    others = [lax.ppermute(table, "col", [(c, (c + NC * k) % COLS) for c in range(COLS)]) for k in (1, 2, 3)]
-    table = (table + others[1]) + (others[0] + others[2])
+    across = lax.ppermute(table, "col", [(c, (c + NC * 2) % COLS) for c in range(COLS)])
+    beside = lax.ppermute(table, "col", [(c, (c + (NC if c % NC == 0 else -NC)) % COLS) for c in range(COLS)])
+    beside = beside + lax.ppermute(beside, "col", [(c, c ^ 1) for c in range(COLS)])
+    table = (table + across) + beside
     slots = (pair_list[:, 0] * QB + pair_list[:, 1] - row * QB)[:, None, None]
     gradient = jnp.broadcast_to(table[:, 0, :][None], (pair_list.shape[0], 3, NB))
     for k in range(1, 2 * QB):

time: 68.9 us -> 65.1 us (0.945)
  waiting for transfers between devices: 30.4 us -> 25.2 us
  matrix products: 3.32 us -> 2.14 us
  local copies, waits for them, and re-layouts: 0.18 us -> 1.3 us
  Pallas kernels: 11.4 us -> 12.3 us
  starting transfers between devices: 21.4 us -> 22.1 us
    ppermute x12, waiting for transfers between devices: 27.7 us -> 22.1 us  [send(): return lax.ppermute(value, ('row', 'col'), sorted(out.items()))]
    pallas_call x0 -> x1, Pallas kernels: none -> 4.14 us  [load(): pl.pallas_call(load_kernel, grid=(QB,), in_specs=blocks, out_specs=blocks...]
    pallas_call x1, Pallas kernels: 9.75 us -> 6.5 us  [final(): pl.pallas_call(body, grid_spec=pltpu.PrefetchScalarGridSpec(num_scalar_pr...]
    dot_general x2, matrix products: 3.32 us -> 2.14 us  [dot(): return jnp.dot(a, b, preferred_element_type=F32)]
    ppermute x12, starting transfers between devices: 15.5 us -> 16.6 us  [send(): return lax.ppermute(value, ('row', 'col'), sorted(out.items()))]
    squeeze x0 -> x1, local copies, waits for them, and re-layouts: none -> 1.11 us  [on_device(): u_rows[0, :, 0:NB]]
    ppermute x1, starting transfers between devices: 1.59 us -> 0.5 us  [on_device(): lax.ppermute(table, 'col', [(c, c ^ 1) for c in range(COLS)])]
  transfers between devices with their start and end apart: 16 -> 16, of which waited for: 11 -> 12; matrix products, arithmetic and copies ran while one was open for 3% -> 3% of each run, Pallas kernels for 2% -> 9%
where the time goes in v4:
time: 65.1 us; the launch traced here: 64.9 us
  waiting for transfers between devices  25.2 us (39%)
  starting transfers between devices  22.1 us (34%)
  Pallas kernels  12.3 us (19%)
  matrix products  2.14 us (3%)
  local copies, waits for them, and re-layouts  1.3 us (2%)
  other arithmetic  1 us (2%)
  between operations  0.86 us (1%)
    ppermute x12, waiting for transfers between devices, send(): return lax.ppermute(value, ('row', 'col'), sorted(out.items()))  22.1 us
    ppermute x12, starting transfers between devices, send(): return lax.ppermute(value, ('row', 'col'), sorted(out.items()))  16.6 us
    pallas_call x1, Pallas kernels, final(): pl.pallas_call(body, grid_spec=pltpu.PrefetchScalarGridSpec(num_scalar_pr...  6.5 us
    pallas_call x1, Pallas kernels, load(): pl.pallas_call(load_kernel, grid=(QB,), in_specs=blocks, out_specs=blocks...  4.14 us
    ppermute x1, starting transfers between devices, on_device(): lax.ppermute(table, 'col', [(c, (c + (NC if c % NC == 0 else -NC)) % COLS...  2.41 us
    ppermute x1, starting transfers between devices, on_device(): lax.ppermute(beside, 'col', [(c, c ^ 1) for c in range(COLS)])  2.14 us
    dot_general x2, matrix products, dot(): return jnp.dot(a, b, preferred_element_type=F32)  2.14 us
    pallas_call x1, Pallas kernels, halves(): pl.pallas_call(halves_kernel, grid=(1,), in_specs=[pl.BlockSpec((SIDES, N...  1.69 us
  transfers between devices with their start and end apart: 16, of which 12 were waited for; matrix products, arithmetic and copies ran while one was open for 3% of the time, Pallas kernels for 9%

profile of v4, /device:TPU:1, one launch (start us, length us, event | category | flops | bytes accessed | tf_op | source)
XLA Modules:
  0.0 64.9 jit_solution(8513096625161284406)
XLA Ops:
  0.7 1.6 %convolution_convert_fusion.1 = bf16[256,512]{1,0:T(8,128)(2,1)S(1)} fusion(bf16[2,512,512]{2,1,0:T(8,128)(2,1)} %param.8, f32[256,2048]{1,0:T(8,128)} %refs_0_), kind=kOutput, calls=%fused_computation.3 | convolution fusion | flops 134348800 | bytes 1048576 | tf_op jit(solution)/shard_map/dot_general | solution.py:93
  2.3 2.1 %collective-permute-start = (bf16[256,512]{1,0:T(8,128)(2,1)S(1)}, bf16[256,512]{1,0:T(8,128)(2,1)S(1)}, u32[]{:S(2)}, u32[]{:S(2)}) collective-permute-start(bf16[256,512]{1,0:T(8,128)(2,1)S(1)} %convolution_convert_fusion.1), channel_id=1, source_target_pairs={{0,8},{1,9},{2,10},{3,11},{4,12},{5,13},{6,14},{7,15},{8,0},{9,1},... | collective-permute-start | bytes 786440 | tf_op jit(solution)/shard_map/ppermute | solution.py:56
  4.4 1.7 %shard_map.77 = (bf16[144,512]{1,0:T(8,128)(2,1)}, bf16[144,512]{1,0:T(8,128)(2,1)}) custom-call(bf16[256,2048]{1,0:T(8,128)(2,1)} %refs_2_, bf16[3,2048]{1,0:T(4,128)(2,1)} %coords), custom_call_target="tpu_custom_call" | custom-call | tf_op jit(solution)/shard_map/pallas_call | solution.py:109
  6.1 1.9 %collective-permute-start.2 = (bf16[144,512]{1,0:T(8,128)(2,1)}, bf16[144,512]{1,0:T(8,128)(2,1)S(1)}, u32[]{:S(2)}, u32[]{:S(2)}) collective-permute-start(bf16[144,512]{1,0:T(8,128)(2,1)} %get-tuple-element.21), channel_id=1, source_target_pairs={{0,24},{1,25},{2,26},{3,27},{4,28},{5,29},{6,30},{7,31},{8,16},{9,... | collective-permute-start | bytes 442376 | tf_op jit(solution)/shard_map/ppermute | solution.py:56
  8.0 1.1 %slice_bitcast_fusion = bf16[512,512]{1,0:T(8,128)(2,1)S(1)} fusion(bf16[2,512,2048]{2,1,0:T(8,128)(2,1)} %param.7), kind=kLoop, calls=%fused_computation.8 | loop fusion | bytes 1048576 | tf_op jit(solution)/shard_map/squeeze | solution.py:259
  9.2 0.5 fusion.1
  9.7 0.8 %collective-permute-start.1 = (bf16[128,512]{1,0:T(8,128)(2,1)S(1)}, bf16[128,512]{1,0:T(8,128)(2,1)S(1)}, u32[]{:S(2)}, u32[]{:S(2)}) collective-permute-start(bf16[128,512]{1,0:T(8,128)(2,1)S(1)} %slice.64), channel_id=1, source_target_pairs={{0,24},{1,25},{2,26},{3,27},{4,28},{5,29},{6,30},{7,31},{8,16},{9,... | collective-permute-start | bytes 393224 | tf_op jit(solution)/shard_map/ppermute | solution.py:56
  10.5 1.1 %collective-permute-done.2 = bf16[144,512]{1,0:T(8,128)(2,1)S(1)} collective-permute-done((bf16[144,512]{1,0:T(8,128)(2,1)}, bf16[144,512]{1,0:T(8,128)(2,1)S(1)}, u32[]{:S(2)}, u32[]{:S(2)}) %collective-permute-start.2) | collective-permute-done | bytes 147488 | tf_op jit(solution)/shard_map/ppermute | solution.py:56
  11.6 3.2 %collective-permute-done.1 = bf16[128,512]{1,0:T(8,128)(2,1)S(1)} collective-permute-done((bf16[128,512]{1,0:T(8,128)(2,1)S(1)}, bf16[128,512]{1,0:T(8,128)(2,1)S(1)}, u32[]{:S(2)}, u32[]{:S(2)}) %collective-permute-start.1) | collective-permute-done | bytes 131104 | tf_op jit(solution)/shard_map/ppermute | solution.py:56
  15.0 0.8 %collective-permute-start.4 = (bf16[272,512]{1,0:T(8,128)(2,1)S(1)}, bf16[272,512]{1,0:T(8,128)(2,1)S(1)}, u32[]{:S(2)}, u32[]{:S(2)}) collective-permute-start(bf16[272,512]{1,0:T(8,128)(2,1)S(1)} %pad_maximum_fusion), channel_id=1, source_target_pairs={{0,160},{1,161},{2,162},{3,163},{4,164},{5,165},{6,166},{7,167},{8... | collective-permute-start | bytes 835592 | tf_op jit(solution)/shard_map/ppermute | solution.py:56
  15.8 6.5 %collective-permute-done.3 = bf16[272,512]{1,0:T(8,128)(2,1)S(1)} collective-permute-done((bf16[272,512]{1,0:T(8,128)(2,1)S(1)}, bf16[272,512]{1,0:T(8,128)(2,1)S(1)}, u32[]{:S(2)}, u32[]{:S(2)}) %collective-permute-start.3) | collective-permute-done | bytes 278560 | tf_op jit(solution)/shard_map/ppermute | solution.py:56
  22.3 1.3 %collective-permute-done.4 = bf16[272,512]{1,0:T(8,128)(2,1)S(1)} collective-permute-done((bf16[272,512]{1,0:T(8,128)(2,1)S(1)}, bf16[272,512]{1,0:T(8,128)(2,1)S(1)}, u32[]{:S(2)}, u32[]{:S(2)}) %collective-permute-start.4) | collective-permute-done | bytes 278560 | tf_op jit(solution)/shard_map/ppermute | solution.py:56
  23.6 0.1 select_select_fusion.1
  23.7 7.7 %collective-permute-start.5 = (bf16[272,512]{1,0:T(8,128)(2,1)S(1)}, bf16[272,512]{1,0:T(8,128)(2,1)S(1)}, u32[]{:S(2)}, u32[]{:S(2)}) collective-permute-start(bf16[272,512]{1,0:T(8,128)(2,1)S(1)} %select_select_fusion.1), channel_id=1, source_target_pairs={{0,1},{1,0},{2,3},{3,2},{4,5},{5,4},{6,7},{7,6},{8,9},{9,8},{10,11... | collective-permute-start | bytes 835592 | tf_op jit(solution)/shard_map/ppermute | solution.py:56
  31.4 0.1 collective-permute-start.6
  31.5 1.1 %collective-permute-done.5 = bf16[272,512]{1,0:T(8,128)(2,1)S(1)} collective-permute-done((bf16[272,512]{1,0:T(8,128)(2,1)S(1)}, bf16[272,512]{1,0:T(8,128)(2,1)S(1)}, u32[]{:S(2)}, u32[]{:S(2)}) %collective-permute-start.5) | collective-permute-done | bytes 278560 | tf_op jit(solution)/shard_map/ppermute | solution.py:56
  32.6 0.4 collective-permute-done.6
  33.1 2.1 %collective-permute-start.11 = (bf16[272,512]{1,0:T(8,128)(2,1)S(1)}, bf16[272,512]{1,0:T(8,128)(2,1)S(1)}, u32[]{:S(2)}, u32[]{:S(2)}) collective-permute-start(bf16[272,512]{1,0:T(8,128)(2,1)S(1)} %select_select_fusion.refs_3_), channel_id=1, source_target_pairs={{0,24},{1,17},{2,26},{3,19},{4,28},{5,21},{6,30},{7,23},{8,0},{9,2... | collective-permute-start | bytes 835592 | tf_op jit(solution)/shard_map/ppermute | solution.py:56
  35.2 0.9 %collective-permute-start.9 = (bf16[272,512]{1,0:T(8,128)(2,1)S(1)}, bf16[272,512]{1,0:T(8,128)(2,1)S(1)}, u32[]{:S(2)}, u32[]{:S(2)}) collective-permute-start(bf16[272,512]{1,0:T(8,128)(2,1)S(1)} %select_select_fusion.refs_3_), channel_id=1, source_target_pairs={{0,8},{1,25},{2,10},{3,27},{4,12},{5,29},{6,14},{7,31},{8,16},{9,1... | collective-permute-start | bytes 835592 | tf_op jit(solution)/shard_map/ppermute | solution.py:56
  36.2 4.1 %shard_map.78 = (f32[256,2048]{1,0:T(8,128)S(1)}, bf16[1024,2048]{1,0:T(8,128)(2,1)S(1)}, bf16[256,2048]{1,0:T(8,128)(2,1)S(1)}) custom-call(f32[256,2048]{1,0:T(8,128)} %refs_0_, bf16[1024,2048]{1,0:T(8,128)(2,1)} %bitcast.45, bf16[256,2048]{1,0:T(8,128)(2,1)} %refs_2_), custom_call_target="tpu_custom_call" | custom-call | bytes 14680064 | tf_op jit(solution)/shard_map/pallas_call | solution.py:197
  40.4 5.8 %collective-permute-done.10.refs_5_ = bf16[272,512]{1,0:T(8,128)(2,1)S(1)} collective-permute-done((bf16[272,512]{1,0:T(8,128)(2,1)S(1)}, bf16[272,512]{1,0:T(8,128)(2,1)S(1)}, u32[]{:S(2)}, u32[]{:S(2)}) %collective-permute-start.10) | collective-permute-done | bytes 278560 | tf_op jit(solution)/shard_map/ppermute | solution.py:56
  46.2 0.2 collective-permute-done.11.refs_6_
  46.3 2.6 %collective-permute-done.9.refs_4_ = bf16[272,512]{1,0:T(8,128)(2,1)S(1)} collective-permute-done((bf16[272,512]{1,0:T(8,128)(2,1)S(1)}, bf16[272,512]{1,0:T(8,128)(2,1)S(1)}, u32[]{:S(2)}, u32[]{:S(2)}) %collective-permute-start.9) | collective-permute-done | bytes 278560 | tf_op jit(solution)/shard_map/ppermute | solution.py:56
  49.0 6.5 %shard_map.79 = (f32[256,2048]{1,0:T(8,128)}, f32[3,8,512]{2,1,0:T(8,128)S(1)}) custom-call(s32[5]{0:T(128)S(1)} %stack.23.info, f32[256,2048]{1,0:T(8,128)S(1)} %get-tuple-element.26.refs_0_, bf16[1024,2048]{1,0:T(8,128)(2,1)S(1)} %get-tuple-element.27.refs_1_, bf16[256,2048]{1,0:T(8,128)(2,1)S(1)} %get-tuple-element.28.refs_2_, ...), custom_call_target="tpu_custom_call" | custom-call | flops 3221225472 | bytes 14680064 | tf_op jit(solution)/shard_map/pallas_call | solution.py:215
  55.5 0.5 collective-permute-start.12
  56.0 0.9 %collective-permute-done.12 = f32[3,8,512]{2,1,0:T(8,128)S(1)} collective-permute-done((f32[3,8,512]{2,1,0:T(8,128)S(1)}, f32[3,8,512]{2,1,0:T(8,128)S(1)}, u32[]{:S(2)}, u32[]{:S(2)}) %collective-permute-start.12) | collective-permute-done | bytes 49184 | tf_op jit(solution)/shard_map/ppermute | solution.py:281
  56.9 2.4 %collective-permute-start.14 = (f32[3,8,512]{2,1,0:T(8,128)S(1)}, f32[3,8,512]{2,1,0:T(8,128)S(1)}, u32[]{:S(2)}, u32[]{:S(2)}) collective-permute-start(f32[3,8,512]{2,1,0:T(8,128)S(1)} %add.67), channel_id=1, source_target_pairs={{0,2},{1,7},{2,4},{3,1},{4,6},{5,3},{6,0},{7,5},{8,10},{9,15},{10,... | collective-permute-start | bytes 147464 | tf_op jit(solution)/shard_map/ppermute | solution.py:283
  59.3 0.4 collective-permute-start.13
  59.7 0.7 %collective-permute-done.14 = f32[3,8,512]{2,1,0:T(8,128)S(1)} collective-permute-done((f32[3,8,512]{2,1,0:T(8,128)S(1)}, f32[3,8,512]{2,1,0:T(8,128)S(1)}, u32[]{:S(2)}, u32[]{:S(2)}) %collective-permute-start.14) | collective-permute-done | bytes 49184 | tf_op jit(solution)/shard_map/ppermute | solution.py:283
  60.4 2.1 %collective-permute-start.15 = (f32[3,8,512]{2,1,0:T(8,128)S(1)}, f32[3,8,512]{2,1,0:T(8,128)S(1)}, u32[]{:S(2)}, u32[]{:S(2)}) collective-permute-start(f32[3,8,512]{2,1,0:T(8,128)S(1)} %collective-permute-done.14), channel_id=1, source_target_pairs={{0,1},{1,0},{2,3},{3,2},{4,5},{5,4},{6,7},{7,6},{8,9},{9,8},{10,11... | collective-permute-start | bytes 147464 | tf_op jit(solution)/shard_map/ppermute | solution.py:284
  62.6 1.4 %collective-permute-done.13 = f32[3,8,512]{2,1,0:T(8,128)S(1)} collective-permute-done((f32[3,8,512]{2,1,0:T(8,128)S(1)}, f32[3,8,512]{2,1,0:T(8,128)S(1)}, u32[]{:S(2)}, u32[]{:S(2)}) %collective-permute-start.13) | collective-permute-done | bytes 49184 | tf_op jit(solution)/shard_map/ppermute | solution.py:282
  64.1 0.7 %select_select_fusion.2 = f32[16,3,512]{2,0,1:T(8,128)} fusion(f32[3,512]{1,0:T(4,128)S(1)} %get-tuple-element.48, f32[3,512]{1,0:T(4,128)S(1)} %get-tuple-element.49, f32[3,512]{1,0:T(4,128)S(1)} %get-tuple-element.50, f32[3,512]{1,0:T(4,128)S(1)} %get-tuple-element.51, f32[3,512]{1,0:T(4,128)S(1)} %get-tuple-element.52, ...), kind=kLoop, calls=%fused_computation.18 | loop fusion | flops 172032 | bytes 147568 | tf_op jit(solution)/shard_map/jit(_where)/select_n | solution.py:289
  (34 shorter events, 0.5 us)
Async XLA Ops:
  0.6 8.5 %slice-start = ((f32[256,2048]{1,0:T(8,128)}), f32[256,512]{1,0:T(8,128)S(1)}, s32[]{:S(2)}) async-start(f32[256,2048]{1,0:T(8,128)} %refs_0_), calls=%async_computation | async-start | bytes 1048576 | tf_op jit(solution)/shard_map/slice | solution.py:250
  0.6 8.5 %copy-start = (bf16[2,512,512]{2,1,0:T(8,128)(2,1)S(1)}, bf16[2,512,512]{2,1,0:T(8,128)(2,1)}, u32[]{:S(2)}) copy-start(bf16[2,512,512]{2,1,0:T(8,128)(2,1)} %param.8) | copy-start | bytes 3145732
  2.3 6.9 %collective-permute-start = (bf16[256,512]{1,0:T(8,128)(2,1)S(1)}, bf16[256,512]{1,0:T(8,128)(2,1)S(1)}, u32[]{:S(2)}, u32[]{:S(2)}) collective-permute-start(bf16[256,512]{1,0:T(8,128)(2,1)S(1)} %convolution_convert_fusion.1), channel_id=1, source_target_pairs={{0,8},{1,9},{2,10},{3,11},{4,12},{5,13},{6,14},{7,15},{8,0},{9,1},... | collective-permute-start | bytes 786440 | tf_op jit(solution)/shard_map/ppermute | solution.py:56
  6.1 5.5 %collective-permute-start.2 = (bf16[144,512]{1,0:T(8,128)(2,1)}, bf16[144,512]{1,0:T(8,128)(2,1)S(1)}, u32[]{:S(2)}, u32[]{:S(2)}) collective-permute-start(bf16[144,512]{1,0:T(8,128)(2,1)} %get-tuple-element.21), channel_id=1, source_target_pairs={{0,24},{1,25},{2,26},{3,27},{4,28},{5,29},{6,30},{7,31},{8,16},{9,... | collective-permute-start | bytes 442376 | tf_op jit(solution)/shard_map/ppermute | solution.py:56
  8.0 3.6 %copy-start.1 = (bf16[144,512]{1,0:T(8,128)(2,1)S(1)}, bf16[144,512]{1,0:T(8,128)(2,1)}, u32[]{:S(2)}) copy-start(bf16[144,512]{1,0:T(8,128)(2,1)} %get-tuple-element.22) | copy-start | bytes 442372
  9.7 5.1 %collective-permute-start.1 = (bf16[128,512]{1,0:T(8,128)(2,1)S(1)}, bf16[128,512]{1,0:T(8,128)(2,1)S(1)}, u32[]{:S(2)}, u32[]{:S(2)}) collective-permute-start(bf16[128,512]{1,0:T(8,128)(2,1)S(1)} %slice.64), channel_id=1, source_target_pairs={{0,24},{1,25},{2,26},{3,27},{4,28},{5,29},{6,30},{7,31},{8,16},{9,... | collective-permute-start | bytes 393224 | tf_op jit(solution)/shard_map/ppermute | solution.py:56
  11.6 24.5 %copy-start.2 = (bf16[3,2048]{1,0:T(4,128)(2,1)S(1)}, bf16[3,2048]{1,0:T(4,128)(2,1)}, u32[]{:S(2)}) copy-start(bf16[3,2048]{1,0:T(4,128)(2,1)} %coords) | copy-start | bytes 36868
  14.9 7.4 %collective-permute-start.3 = (bf16[272,512]{1,0:T(8,128)(2,1)S(1)}, bf16[272,512]{1,0:T(8,128)(2,1)S(1)}, u32[]{:S(2)}, u32[]{:S(2)}) collective-permute-start(bf16[272,512]{1,0:T(8,128)(2,1)S(1)} %pad_maximum_fusion), channel_id=1, source_target_pairs={{0,96},{1,97},{2,98},{3,99},{4,100},{5,101},{6,102},{7,103},{8,104... | collective-permute-start | bytes 835592 | tf_op jit(solution)/shard_map/ppermute | solution.py:56
  15.0 8.6 %collective-permute-start.4 = (bf16[272,512]{1,0:T(8,128)(2,1)S(1)}, bf16[272,512]{1,0:T(8,128)(2,1)S(1)}, u32[]{:S(2)}, u32[]{:S(2)}) collective-permute-start(bf16[272,512]{1,0:T(8,128)(2,1)S(1)} %pad_maximum_fusion), channel_id=1, source_target_pairs={{0,160},{1,161},{2,162},{3,163},{4,164},{5,165},{6,166},{7,167},{8... | collective-permute-start | bytes 835592 | tf_op jit(solution)/shard_map/ppermute | solution.py:56
  15.8 15.7 %collective-permute-start.7 = (bf16[272,512]{1,0:T(8,128)(2,1)S(1)}, bf16[272,512]{1,0:T(8,128)(2,1)S(1)}, u32[]{:S(2)}, u32[]{:S(2)}) collective-permute-start(bf16[272,512]{1,0:T(8,128)(2,1)S(1)} %pad_maximum_fusion), channel_id=1, source_target_pairs={{0,32},{1,33},{2,34},{3,35},{4,36},{5,37},{6,38},{7,39},{8,40},{9,... | collective-permute-start | bytes 835592 | tf_op jit(solution)/shard_map/ppermute | solution.py:56
  15.8 15.7 %collective-permute-start.8 = (bf16[272,512]{1,0:T(8,128)(2,1)S(1)}, bf16[272,512]{1,0:T(8,128)(2,1)S(1)}, u32[]{:S(2)}, u32[]{:S(2)}) collective-permute-start(bf16[272,512]{1,0:T(8,128)(2,1)S(1)} %pad_maximum_fusion), channel_id=1, source_target_pairs={{0,224},{1,225},{2,226},{3,227},{4,228},{5,229},{6,230},{7,231},{8... | collective-permute-start | bytes 835592 | tf_op jit(solution)/shard_map/ppermute | solution.py:56
  23.7 8.9 %collective-permute-start.5 = (bf16[272,512]{1,0:T(8,128)(2,1)S(1)}, bf16[272,512]{1,0:T(8,128)(2,1)S(1)}, u32[]{:S(2)}, u32[]{:S(2)}) collective-permute-start(bf16[272,512]{1,0:T(8,128)(2,1)S(1)} %select_select_fusion.1), channel_id=1, source_target_pairs={{0,1},{1,0},{2,3},{3,2},{4,5},{5,4},{6,7},{7,6},{8,9},{9,8},{10,11... | collective-permute-start | bytes 835592 | tf_op jit(solution)/shard_map/ppermute | solution.py:56
  31.4 1.6 %collective-permute-start.6 = (bf16[272,512]{1,0:T(8,128)(2,1)S(1)}, bf16[272,512]{1,0:T(8,128)(2,1)S(1)}, u32[]{:S(2)}, u32[]{:S(2)}) collective-permute-start(bf16[272,512]{1,0:T(8,128)(2,1)S(1)} %select_select_fusion.1), channel_id=1, source_target_pairs={{0,1},{1,0},{2,3},{3,2},{4,5},{5,4},{6,7},{7,6},{8,9},{9,8},{10,11... | collective-permute-start | bytes 835592 | tf_op jit(solution)/shard_map/ppermute | solution.py:56
  33.0 13.1 %collective-permute-start.10 = (bf16[272,512]{1,0:T(8,128)(2,1)S(1)}, bf16[272,512]{1,0:T(8,128)(2,1)S(1)}, u32[]{:S(2)}, u32[]{:S(2)}) collective-permute-start(bf16[272,512]{1,0:T(8,128)(2,1)S(1)} %select_select_fusion.refs_3_), channel_id=1, source_target_pairs={{0,16},{1,9},{2,18},{3,11},{4,20},{5,13},{6,22},{7,15},{8,24},{9,1... | collective-permute-start | bytes 835592 | tf_op jit(solution)/shard_map/ppermute | solution.py:56
  33.1 13.2 %collective-permute-start.11 = (bf16[272,512]{1,0:T(8,128)(2,1)S(1)}, bf16[272,512]{1,0:T(8,128)(2,1)S(1)}, u32[]{:S(2)}, u32[]{:S(2)}) collective-permute-start(bf16[272,512]{1,0:T(8,128)(2,1)S(1)} %select_select_fusion.refs_3_), channel_id=1, source_target_pairs={{0,24},{1,17},{2,26},{3,19},{4,28},{5,21},{6,30},{7,23},{8,0},{9,2... | collective-permute-start | bytes 835592 | tf_op jit(solution)/shard_map/ppermute | solution.py:56
  35.2 13.8 %collective-permute-start.9 = (bf16[272,512]{1,0:T(8,128)(2,1)S(1)}, bf16[272,512]{1,0:T(8,128)(2,1)S(1)}, u32[]{:S(2)}, u32[]{:S(2)}) collective-permute-start(bf16[272,512]{1,0:T(8,128)(2,1)S(1)} %select_select_fusion.refs_3_), channel_id=1, source_target_pairs={{0,8},{1,25},{2,10},{3,27},{4,12},{5,29},{6,14},{7,31},{8,16},{9,1... | collective-permute-start | bytes 835592 | tf_op jit(solution)/shard_map/ppermute | solution.py:56
  49.0 10.3 %copy-start.3 = (s32[16,2]{0,1:T(2,128)S(1)}, s32[16,2]{0,1:T(2,128)}, u32[]{:S(2)}) copy-start(s32[16,2]{0,1:T(2,128)} %param.11) | copy-start | bytes 388
  55.5 1.4 %collective-permute-start.12 = (f32[3,8,512]{2,1,0:T(8,128)S(1)}, f32[3,8,512]{2,1,0:T(8,128)S(1)}, u32[]{:S(2)}, u32[]{:S(2)}) collective-permute-start(f32[3,8,512]{2,1,0:T(8,128)S(1)} %get-tuple-element.31), channel_id=1, source_target_pairs={{0,1},{1,0},{2,3},{3,2},{4,5},{5,4},{6,7},{7,6},{8,9},{9,8},{10,11... | collective-permute-start | bytes 147464 | tf_op jit(solution)/shard_map/ppermute | solution.py:281
  56.9 3.6 %collective-permute-start.14 = (f32[3,8,512]{2,1,0:T(8,128)S(1)}, f32[3,8,512]{2,1,0:T(8,128)S(1)}, u32[]{:S(2)}, u32[]{:S(2)}) collective-permute-start(f32[3,8,512]{2,1,0:T(8,128)S(1)} %add.67), channel_id=1, source_target_pairs={{0,2},{1,7},{2,4},{3,1},{4,6},{5,3},{6,0},{7,5},{8,10},{9,15},{10,... | collective-permute-start | bytes 147464 | tf_op jit(solution)/shard_map/ppermute | solution.py:283
  59.3 4.7 %collective-permute-start.13 = (f32[3,8,512]{2,1,0:T(8,128)S(1)}, f32[3,8,512]{2,1,0:T(8,128)S(1)}, u32[]{:S(2)}, u32[]{:S(2)}) collective-permute-start(f32[3,8,512]{2,1,0:T(8,128)S(1)} %add.67), channel_id=1, source_target_pairs={{0,4},{1,5},{2,6},{3,7},{4,0},{5,1},{6,2},{7,3},{8,12},{9,13},{10,... | collective-permute-start | bytes 147464 | tf_op jit(solution)/shard_map/ppermute | solution.py:282
  60.4 3.6 %collective-permute-start.15 = (f32[3,8,512]{2,1,0:T(8,128)S(1)}, f32[3,8,512]{2,1,0:T(8,128)S(1)}, u32[]{:S(2)}, u32[]{:S(2)}) collective-permute-start(f32[3,8,512]{2,1,0:T(8,128)S(1)} %collective-permute-done.14), channel_id=1, source_target_pairs={{0,1},{1,0},{2,3},{3,2},{4,5},{5,4},{6,7},{7,6},{8,9},{9,8},{10,11... | collective-permute-start | bytes 147464 | tf_op jit(solution)/shard_map/ppermute | solution.py:284

commit v5 on v4

--- a/solution.py
+++ b/solution.py
@@ -77,16 +77,15 @@
     return choose((z == 4) | (z == 6), near[2], choose(z == 2, near[3], held))
 
 
-def gather_x(value, twist):
-    return [send(value, shift(0, j), shift(0, (j + twist - 1) % 3 + 1)) for j in (1, 2, 3)]
-
-
-def moved(j, core, twist):
-    return j if j == 0 else jnp.where(core == 0, j, (j + twist - 1) % 3 + 1)
-
-
-def held(x, core, twist):
-    return [(x - moved(j, core, twist)) % NX for j in range(NX)]
+STEPS = ((1, 3), (3, 1), (2, 2))
+
+
+def gather_x(value):
+    return [send(value, shift(0, a), shift(0, b)) for a, b in STEPS]
+
+
+def held(x, core):
+    return [x] + [(x - jnp.where(core == 0, a, b)) % NX for a, b in STEPS]
 
 
 def dot(a, b):
@@ -269,10 +268,10 @@
         (adjoint_source, u_rows.reshape(2 * NB, WIDTH), forward_field, value)
     )
     loaded = load(source, factors, field)
-    parts = [value] + gather_x(value, 2)
+    parts = [value] + gather_x(value)
 
     coords = jnp.pad(panel_coords, ((0, CROWS - 3), (0, 0)))
-    info = jnp.stack([row, *held(x, core, 2), ]).astype(jnp.int32)
+    info = jnp.stack([row, *held(x, core)]).astype(jnp.int32)
     scale_value = 1.0 / math.sqrt(SIDES * COLS)
     solved, table = final(
         info, *loaded, parts, coords, scale_value

time: 65.1 us -> 64.8 us (level)
  waiting for transfers between devices: 25.2 us -> 24.5 us
  transfers between devices with their start and end apart: 16 -> 16, of which waited for: 12 -> 11; matrix products, arithmetic and copies ran while one was open for 3% -> 3% of each run, Pallas kernels for 9% -> 9%
where the time goes in v5:
time: 64.8 us; the launch traced here: 64.6 us
  waiting for transfers between devices  24.5 us (38%)
  starting transfers between devices  22.5 us (35%)
  Pallas kernels  12.3 us (19%)
  matrix products  2.14 us (3%)
  local copies, waits for them, and re-layouts  1.3 us (2%)
  other arithmetic  1 us (2%)
  between operations  0.85 us (1%)
    ppermute x12, waiting for transfers between devices, send(): return lax.ppermute(value, ('row', 'col'), sorted(out.items()))  21.8 us
    ppermute x12, starting transfers between devices, send(): return lax.ppermute(value, ('row', 'col'), sorted(out.items()))  16.6 us
    pallas_call x1, Pallas kernels, final(): pl.pallas_call(body, grid_spec=pltpu.PrefetchScalarGridSpec(num_scalar_pr...  6.49 us
    pallas_call x1, Pallas kernels, load(): pl.pallas_call(load_kernel, grid=(QB,), in_specs=blocks, out_specs=blocks...  4.14 us
    ppermute x1, starting transfers between devices, on_device(): lax.ppermute(beside, 'col', [(c, c ^ 1) for c in range(COLS)])  2.37 us
    ppermute x1, starting transfers between devices, on_device(): lax.ppermute(table, 'col', [(c, (c + (NC if c % NC == 0 else -NC)) % COLS...  2.19 us
    dot_general x2, matrix products, dot(): return jnp.dot(a, b, preferred_element_type=F32)  2.14 us
    pallas_call x1, Pallas kernels, halves(): pl.pallas_call(halves_kernel, grid=(1,), in_specs=[pl.BlockSpec((SIDES, N...  1.69 us
  transfers between devices with their start and end apart: 16, of which 11 were waited for; matrix products, arithmetic and copies ran while one was open for 3% of the time, Pallas kernels for 9%

profile of v5, /device:TPU:1, one launch (start us, length us, event | category | flops | bytes accessed | tf_op | source)
XLA Modules:
  0.0 64.6 jit_solution(1139958728472574613)
XLA Ops:
  0.7 1.6 %convolution_convert_fusion.1 = bf16[256,512]{1,0:T(8,128)(2,1)S(1)} fusion(bf16[2,512,512]{2,1,0:T(8,128)(2,1)} %param.8, f32[256,2048]{1,0:T(8,128)} %refs_0_), kind=kOutput, calls=%fused_computation.3 | convolution fusion | flops 134348800 | bytes 1048576 | tf_op jit(solution)/shard_map/dot_general | solution.py:92
  2.3 2.1 %collective-permute-start = (bf16[256,512]{1,0:T(8,128)(2,1)S(1)}, bf16[256,512]{1,0:T(8,128)(2,1)S(1)}, u32[]{:S(2)}, u32[]{:S(2)}) collective-permute-start(bf16[256,512]{1,0:T(8,128)(2,1)S(1)} %convolution_convert_fusion.1), channel_id=1, source_target_pairs={{0,8},{1,9},{2,10},{3,11},{4,12},{5,13},{6,14},{7,15},{8,0},{9,1},... | collective-permute-start | bytes 786440 | tf_op jit(solution)/shard_map/ppermute | solution.py:56
  4.4 1.7 %shard_map.77 = (bf16[144,512]{1,0:T(8,128)(2,1)}, bf16[144,512]{1,0:T(8,128)(2,1)}) custom-call(bf16[256,2048]{1,0:T(8,128)(2,1)} %refs_2_, bf16[3,2048]{1,0:T(4,128)(2,1)} %coords), custom_call_target="tpu_custom_call" | custom-call | tf_op jit(solution)/shard_map/pallas_call | solution.py:108
  6.1 1.9 %collective-permute-start.2 = (bf16[144,512]{1,0:T(8,128)(2,1)}, bf16[144,512]{1,0:T(8,128)(2,1)S(1)}, u32[]{:S(2)}, u32[]{:S(2)}) collective-permute-start(bf16[144,512]{1,0:T(8,128)(2,1)} %get-tuple-element.21), channel_id=1, source_target_pairs={{0,24},{1,25},{2,26},{3,27},{4,28},{5,29},{6,30},{7,31},{8,16},{9,... | collective-permute-start | bytes 442376 | tf_op jit(solution)/shard_map/ppermute | solution.py:56
  8.0 1.1 %slice_bitcast_fusion = bf16[512,512]{1,0:T(8,128)(2,1)S(1)} fusion(bf16[2,512,2048]{2,1,0:T(8,128)(2,1)} %param.7), kind=kLoop, calls=%fused_computation.8 | loop fusion | bytes 1048576 | tf_op jit(solution)/shard_map/squeeze | solution.py:258
  9.2 0.5 fusion.1
  9.7 0.8 %collective-permute-start.1 = (bf16[128,512]{1,0:T(8,128)(2,1)S(1)}, bf16[128,512]{1,0:T(8,128)(2,1)S(1)}, u32[]{:S(2)}, u32[]{:S(2)}) collective-permute-start(bf16[128,512]{1,0:T(8,128)(2,1)S(1)} %slice.64), channel_id=1, source_target_pairs={{0,24},{1,25},{2,26},{3,27},{4,28},{5,29},{6,30},{7,31},{8,16},{9,... | collective-permute-start | bytes 393224 | tf_op jit(solution)/shard_map/ppermute | solution.py:56
  10.5 1.1 %collective-permute-done.2 = bf16[144,512]{1,0:T(8,128)(2,1)S(1)} collective-permute-done((bf16[144,512]{1,0:T(8,128)(2,1)}, bf16[144,512]{1,0:T(8,128)(2,1)S(1)}, u32[]{:S(2)}, u32[]{:S(2)}) %collective-permute-start.2) | collective-permute-done | bytes 147488 | tf_op jit(solution)/shard_map/ppermute | solution.py:56
  11.6 3.2 %collective-permute-done.1 = bf16[128,512]{1,0:T(8,128)(2,1)S(1)} collective-permute-done((bf16[128,512]{1,0:T(8,128)(2,1)S(1)}, bf16[128,512]{1,0:T(8,128)(2,1)S(1)}, u32[]{:S(2)}, u32[]{:S(2)}) %collective-permute-start.1) | collective-permute-done | bytes 131104 | tf_op jit(solution)/shard_map/ppermute | solution.py:56
  14.9 0.1 collective-permute-start.3
  15.0 0.8 %collective-permute-start.4 = (bf16[272,512]{1,0:T(8,128)(2,1)S(1)}, bf16[272,512]{1,0:T(8,128)(2,1)S(1)}, u32[]{:S(2)}, u32[]{:S(2)}) collective-permute-start(bf16[272,512]{1,0:T(8,128)(2,1)S(1)} %pad_maximum_fusion), channel_id=1, source_target_pairs={{0,160},{1,161},{2,162},{3,163},{4,164},{5,165},{6,166},{7,167},{8... | collective-permute-start | bytes 835592 | tf_op jit(solution)/shard_map/ppermute | solution.py:56
  15.8 6.5 %collective-permute-done.3 = bf16[272,512]{1,0:T(8,128)(2,1)S(1)} collective-permute-done((bf16[272,512]{1,0:T(8,128)(2,1)S(1)}, bf16[272,512]{1,0:T(8,128)(2,1)S(1)}, u32[]{:S(2)}, u32[]{:S(2)}) %collective-permute-start.3) | collective-permute-done | bytes 278560 | tf_op jit(solution)/shard_map/ppermute | solution.py:56
  22.3 1.3 %collective-permute-done.4 = bf16[272,512]{1,0:T(8,128)(2,1)S(1)} collective-permute-done((bf16[272,512]{1,0:T(8,128)(2,1)S(1)}, bf16[272,512]{1,0:T(8,128)(2,1)S(1)}, u32[]{:S(2)}, u32[]{:S(2)}) %collective-permute-start.4) | collective-permute-done | bytes 278560 | tf_op jit(solution)/shard_map/ppermute | solution.py:56
  23.6 0.1 select_select_fusion.1
  23.7 7.7 %collective-permute-start.5 = (bf16[272,512]{1,0:T(8,128)(2,1)S(1)}, bf16[272,512]{1,0:T(8,128)(2,1)S(1)}, u32[]{:S(2)}, u32[]{:S(2)}) collective-permute-start(bf16[272,512]{1,0:T(8,128)(2,1)S(1)} %select_select_fusion.1), channel_id=1, source_target_pairs={{0,1},{1,0},{2,3},{3,2},{4,5},{5,4},{6,7},{7,6},{8,9},{9,8},{10,11... | collective-permute-start | bytes 835592 | tf_op jit(solution)/shard_map/ppermute | solution.py:56
  31.4 0.1 collective-permute-start.6
  31.5 1.1 %collective-permute-done.5 = bf16[272,512]{1,0:T(8,128)(2,1)S(1)} collective-permute-done((bf16[272,512]{1,0:T(8,128)(2,1)S(1)}, bf16[272,512]{1,0:T(8,128)(2,1)S(1)}, u32[]{:S(2)}, u32[]{:S(2)}) %collective-permute-start.5) | collective-permute-done | bytes 278560 | tf_op jit(solution)/shard_map/ppermute | solution.py:56
  32.6 0.4 collective-permute-done.6
  33.1 2.1 %collective-permute-start.11 = (bf16[272,512]{1,0:T(8,128)(2,1)S(1)}, bf16[272,512]{1,0:T(8,128)(2,1)S(1)}, u32[]{:S(2)}, u32[]{:S(2)}) collective-permute-start(bf16[272,512]{1,0:T(8,128)(2,1)S(1)} %select_select_fusion.refs_3_), channel_id=1, source_target_pairs={{0,16},{1,17},{2,18},{3,19},{4,20},{5,21},{6,22},{7,23},{8,24},{9,... | collective-permute-start | bytes 835592 | tf_op jit(solution)/shard_map/ppermute | solution.py:56
  35.2 0.9 %collective-permute-start.9 = (bf16[272,512]{1,0:T(8,128)(2,1)S(1)}, bf16[272,512]{1,0:T(8,128)(2,1)S(1)}, u32[]{:S(2)}, u32[]{:S(2)}) collective-permute-start(bf16[272,512]{1,0:T(8,128)(2,1)S(1)} %select_select_fusion.refs_3_), channel_id=1, source_target_pairs={{0,8},{1,25},{2,10},{3,27},{4,12},{5,29},{6,14},{7,31},{8,16},{9,1... | collective-permute-start | bytes 835592 | tf_op jit(solution)/shard_map/ppermute | solution.py:56
  36.2 4.1 %shard_map.78 = (f32[256,2048]{1,0:T(8,128)S(1)}, bf16[1024,2048]{1,0:T(8,128)(2,1)S(1)}, bf16[256,2048]{1,0:T(8,128)(2,1)S(1)}) custom-call(f32[256,2048]{1,0:T(8,128)} %refs_0_, bf16[1024,2048]{1,0:T(8,128)(2,1)} %bitcast.45, bf16[256,2048]{1,0:T(8,128)(2,1)} %refs_2_), custom_call_target="tpu_custom_call" | custom-call | bytes 14680064 | tf_op jit(solution)/shard_map/pallas_call | solution.py:196
  40.4 6.0 %collective-permute-done.10.refs_5_ = bf16[272,512]{1,0:T(8,128)(2,1)S(1)} collective-permute-done((bf16[272,512]{1,0:T(8,128)(2,1)S(1)}, bf16[272,512]{1,0:T(8,128)(2,1)S(1)}, u32[]{:S(2)}, u32[]{:S(2)}) %collective-permute-start.10) | collective-permute-done | bytes 278560 | tf_op jit(solution)/shard_map/ppermute | solution.py:56
  46.4 2.2 %collective-permute-done.9.refs_4_ = bf16[272,512]{1,0:T(8,128)(2,1)S(1)} collective-permute-done((bf16[272,512]{1,0:T(8,128)(2,1)S(1)}, bf16[272,512]{1,0:T(8,128)(2,1)S(1)}, u32[]{:S(2)}, u32[]{:S(2)}) %collective-permute-start.9) | collective-permute-done | bytes 278560 | tf_op jit(solution)/shard_map/ppermute | solution.py:56
  48.6 6.5 %shard_map.79 = (f32[256,2048]{1,0:T(8,128)}, f32[3,8,512]{2,1,0:T(8,128)S(1)}) custom-call(s32[5]{0:T(128)S(1)} %stack.23.info, f32[256,2048]{1,0:T(8,128)S(1)} %get-tuple-element.26.refs_0_, bf16[1024,2048]{1,0:T(8,128)(2,1)S(1)} %get-tuple-element.27.refs_1_, bf16[256,2048]{1,0:T(8,128)(2,1)S(1)} %get-tuple-element.28.refs_2_, ...), custom_call_target="tpu_custom_call" | custom-call | flops 3221225472 | bytes 14680064 | tf_op jit(solution)/shard_map/pallas_call | solution.py:214
  55.1 0.9 %collective-permute-start.12 = (f32[3,8,512]{2,1,0:T(8,128)S(1)}, f32[3,8,512]{2,1,0:T(8,128)S(1)}, u32[]{:S(2)}, u32[]{:S(2)}) collective-permute-start(f32[3,8,512]{2,1,0:T(8,128)S(1)} %get-tuple-element.31), channel_id=1, source_target_pairs={{0,1},{1,0},{2,3},{3,2},{4,5},{5,4},{6,7},{7,6},{8,9},{9,8},{10,11... | collective-permute-start | bytes 147464 | tf_op jit(solution)/shard_map/ppermute | solution.py:280
  56.0 0.9 %collective-permute-done.12 = f32[3,8,512]{2,1,0:T(8,128)S(1)} collective-permute-done((f32[3,8,512]{2,1,0:T(8,128)S(1)}, f32[3,8,512]{2,1,0:T(8,128)S(1)}, u32[]{:S(2)}, u32[]{:S(2)}) %collective-permute-start.12) | collective-permute-done | bytes 49184 | tf_op jit(solution)/shard_map/ppermute | solution.py:280
  56.9 2.2 %collective-permute-start.14 = (f32[3,8,512]{2,1,0:T(8,128)S(1)}, f32[3,8,512]{2,1,0:T(8,128)S(1)}, u32[]{:S(2)}, u32[]{:S(2)}) collective-permute-start(f32[3,8,512]{2,1,0:T(8,128)S(1)} %add.64), channel_id=1, source_target_pairs={{0,2},{1,7},{2,4},{3,1},{4,6},{5,3},{6,0},{7,5},{8,10},{9,15},{10,... | collective-permute-start | bytes 147464 | tf_op jit(solution)/shard_map/ppermute | solution.py:282
  59.0 0.4 collective-permute-start.13
  59.5 0.7 %collective-permute-done.14 = f32[3,8,512]{2,1,0:T(8,128)S(1)} collective-permute-done((f32[3,8,512]{2,1,0:T(8,128)S(1)}, f32[3,8,512]{2,1,0:T(8,128)S(1)}, u32[]{:S(2)}, u32[]{:S(2)}) %collective-permute-start.14) | collective-permute-done | bytes 49184 | tf_op jit(solution)/shard_map/ppermute | solution.py:282
  60.2 2.4 %collective-permute-start.15 = (f32[3,8,512]{2,1,0:T(8,128)S(1)}, f32[3,8,512]{2,1,0:T(8,128)S(1)}, u32[]{:S(2)}, u32[]{:S(2)}) collective-permute-start(f32[3,8,512]{2,1,0:T(8,128)S(1)} %collective-permute-done.14), channel_id=1, source_target_pairs={{0,1},{1,0},{2,3},{3,2},{4,5},{5,4},{6,7},{7,6},{8,9},{9,8},{10,11... | collective-permute-start | bytes 147464 | tf_op jit(solution)/shard_map/ppermute | solution.py:283
  62.6 1.2 %collective-permute-done.13 = f32[3,8,512]{2,1,0:T(8,128)S(1)} collective-permute-done((f32[3,8,512]{2,1,0:T(8,128)S(1)}, f32[3,8,512]{2,1,0:T(8,128)S(1)}, u32[]{:S(2)}, u32[]{:S(2)}) %collective-permute-start.13) | collective-permute-done | bytes 49184 | tf_op jit(solution)/shard_map/ppermute | solution.py:281
  63.9 0.7 %select_select_fusion.2 = f32[16,3,512]{2,0,1:T(8,128)} fusion(f32[3,512]{1,0:T(4,128)S(1)} %get-tuple-element.48, f32[3,512]{1,0:T(4,128)S(1)} %get-tuple-element.49, f32[3,512]{1,0:T(4,128)S(1)} %get-tuple-element.50, f32[3,512]{1,0:T(4,128)S(1)} %get-tuple-element.51, f32[3,512]{1,0:T(4,128)S(1)} %get-tuple-element.52, ...), kind=kLoop, calls=%fused_computation.18 | loop fusion | flops 172032 | bytes 147568 | tf_op jit(solution)/shard_map/jit(_where)/select_n | solution.py:288
  (34 shorter events, 0.4 us)
Async XLA Ops:
  0.6 8.5 %slice-start = ((f32[256,2048]{1,0:T(8,128)}), f32[256,512]{1,0:T(8,128)S(1)}, s32[]{:S(2)}) async-start(f32[256,2048]{1,0:T(8,128)} %refs_0_), calls=%async_computation | async-start | bytes 1048576 | tf_op jit(solution)/shard_map/slice | solution.py:249
  0.6 8.5 %copy-start = (bf16[2,512,512]{2,1,0:T(8,128)(2,1)S(1)}, bf16[2,512,512]{2,1,0:T(8,128)(2,1)}, u32[]{:S(2)}) copy-start(bf16[2,512,512]{2,1,0:T(8,128)(2,1)} %param.8) | copy-start | bytes 3145732
  2.3 6.9 %collective-permute-start = (bf16[256,512]{1,0:T(8,128)(2,1)S(1)}, bf16[256,512]{1,0:T(8,128)(2,1)S(1)}, u32[]{:S(2)}, u32[]{:S(2)}) collective-permute-start(bf16[256,512]{1,0:T(8,128)(2,1)S(1)} %convolution_convert_fusion.1), channel_id=1, source_target_pairs={{0,8},{1,9},{2,10},{3,11},{4,12},{5,13},{6,14},{7,15},{8,0},{9,1},... | collective-permute-start | bytes 786440 | tf_op jit(solution)/shard_map/ppermute | solution.py:56
  6.1 5.5 %collective-permute-start.2 = (bf16[144,512]{1,0:T(8,128)(2,1)}, bf16[144,512]{1,0:T(8,128)(2,1)S(1)}, u32[]{:S(2)}, u32[]{:S(2)}) collective-permute-start(bf16[144,512]{1,0:T(8,128)(2,1)} %get-tuple-element.21), channel_id=1, source_target_pairs={{0,24},{1,25},{2,26},{3,27},{4,28},{5,29},{6,30},{7,31},{8,16},{9,... | collective-permute-start | bytes 442376 | tf_op jit(solution)/shard_map/ppermute | solution.py:56
  8.0 3.6 %copy-start.1 = (bf16[144,512]{1,0:T(8,128)(2,1)S(1)}, bf16[144,512]{1,0:T(8,128)(2,1)}, u32[]{:S(2)}) copy-start(bf16[144,512]{1,0:T(8,128)(2,1)} %get-tuple-element.22) | copy-start | bytes 442372
  9.7 5.1 %collective-permute-start.1 = (bf16[128,512]{1,0:T(8,128)(2,1)S(1)}, bf16[128,512]{1,0:T(8,128)(2,1)S(1)}, u32[]{:S(2)}, u32[]{:S(2)}) collective-permute-start(bf16[128,512]{1,0:T(8,128)(2,1)S(1)} %slice.64), channel_id=1, source_target_pairs={{0,24},{1,25},{2,26},{3,27},{4,28},{5,29},{6,30},{7,31},{8,16},{9,... | collective-permute-start | bytes 393224 | tf_op jit(solution)/shard_map/ppermute | solution.py:56
  11.6 24.5 %copy-start.2 = (bf16[3,2048]{1,0:T(4,128)(2,1)S(1)}, bf16[3,2048]{1,0:T(4,128)(2,1)}, u32[]{:S(2)}) copy-start(bf16[3,2048]{1,0:T(4,128)(2,1)} %coords) | copy-start | bytes 36868
  14.9 7.4 %collective-permute-start.3 = (bf16[272,512]{1,0:T(8,128)(2,1)S(1)}, bf16[272,512]{1,0:T(8,128)(2,1)S(1)}, u32[]{:S(2)}, u32[]{:S(2)}) collective-permute-start(bf16[272,512]{1,0:T(8,128)(2,1)S(1)} %pad_maximum_fusion), channel_id=1, source_target_pairs={{0,96},{1,97},{2,98},{3,99},{4,100},{5,101},{6,102},{7,103},{8,104... | collective-permute-start | bytes 835592 | tf_op jit(solution)/shard_map/ppermute | solution.py:56
  15.0 8.6 %collective-permute-start.4 = (bf16[272,512]{1,0:T(8,128)(2,1)S(1)}, bf16[272,512]{1,0:T(8,128)(2,1)S(1)}, u32[]{:S(2)}, u32[]{:S(2)}) collective-permute-start(bf16[272,512]{1,0:T(8,128)(2,1)S(1)} %pad_maximum_fusion), channel_id=1, source_target_pairs={{0,160},{1,161},{2,162},{3,163},{4,164},{5,165},{6,166},{7,167},{8... | collective-permute-start | bytes 835592 | tf_op jit(solution)/shard_map/ppermute | solution.py:56
  15.8 15.7 %collective-permute-start.7 = (bf16[272,512]{1,0:T(8,128)(2,1)S(1)}, bf16[272,512]{1,0:T(8,128)(2,1)S(1)}, u32[]{:S(2)}, u32[]{:S(2)}) collective-permute-start(bf16[272,512]{1,0:T(8,128)(2,1)S(1)} %pad_maximum_fusion), channel_id=1, source_target_pairs={{0,32},{1,33},{2,34},{3,35},{4,36},{5,37},{6,38},{7,39},{8,40},{9,... | collective-permute-start | bytes 835592 | tf_op jit(solution)/shard_map/ppermute | solution.py:56
  15.8 15.7 %collective-permute-start.8 = (bf16[272,512]{1,0:T(8,128)(2,1)S(1)}, bf16[272,512]{1,0:T(8,128)(2,1)S(1)}, u32[]{:S(2)}, u32[]{:S(2)}) collective-permute-start(bf16[272,512]{1,0:T(8,128)(2,1)S(1)} %pad_maximum_fusion), channel_id=1, source_target_pairs={{0,224},{1,225},{2,226},{3,227},{4,228},{5,229},{6,230},{7,231},{8... | collective-permute-start | bytes 835592 | tf_op jit(solution)/shard_map/ppermute | solution.py:56
  23.7 8.9 %collective-permute-start.5 = (bf16[272,512]{1,0:T(8,128)(2,1)S(1)}, bf16[272,512]{1,0:T(8,128)(2,1)S(1)}, u32[]{:S(2)}, u32[]{:S(2)}) collective-permute-start(bf16[272,512]{1,0:T(8,128)(2,1)S(1)} %select_select_fusion.1), channel_id=1, source_target_pairs={{0,1},{1,0},{2,3},{3,2},{4,5},{5,4},{6,7},{7,6},{8,9},{9,8},{10,11... | collective-permute-start | bytes 835592 | tf_op jit(solution)/shard_map/ppermute | solution.py:56
  31.4 1.6 %collective-permute-start.6 = (bf16[272,512]{1,0:T(8,128)(2,1)S(1)}, bf16[272,512]{1,0:T(8,128)(2,1)S(1)}, u32[]{:S(2)}, u32[]{:S(2)}) collective-permute-start(bf16[272,512]{1,0:T(8,128)(2,1)S(1)} %select_select_fusion.1), channel_id=1, source_target_pairs={{0,1},{1,0},{2,3},{3,2},{4,5},{5,4},{6,7},{7,6},{8,9},{9,8},{10,11... | collective-permute-start | bytes 835592 | tf_op jit(solution)/shard_map/ppermute | solution.py:56
  33.0 13.4 %collective-permute-start.10 = (bf16[272,512]{1,0:T(8,128)(2,1)S(1)}, bf16[272,512]{1,0:T(8,128)(2,1)S(1)}, u32[]{:S(2)}, u32[]{:S(2)}) collective-permute-start(bf16[272,512]{1,0:T(8,128)(2,1)S(1)} %select_select_fusion.refs_3_), channel_id=1, source_target_pairs={{0,24},{1,9},{2,26},{3,11},{4,28},{5,13},{6,30},{7,15},{8,0},{9,17... | collective-permute-start | bytes 835592 | tf_op jit(solution)/shard_map/ppermute | solution.py:56
  33.1 13.3 %collective-permute-start.11 = (bf16[272,512]{1,0:T(8,128)(2,1)S(1)}, bf16[272,512]{1,0:T(8,128)(2,1)S(1)}, u32[]{:S(2)}, u32[]{:S(2)}) collective-permute-start(bf16[272,512]{1,0:T(8,128)(2,1)S(1)} %select_select_fusion.refs_3_), channel_id=1, source_target_pairs={{0,16},{1,17},{2,18},{3,19},{4,20},{5,21},{6,22},{7,23},{8,24},{9,... | collective-permute-start | bytes 835592 | tf_op jit(solution)/shard_map/ppermute | solution.py:56
  35.2 13.4 %collective-permute-start.9 = (bf16[272,512]{1,0:T(8,128)(2,1)S(1)}, bf16[272,512]{1,0:T(8,128)(2,1)S(1)}, u32[]{:S(2)}, u32[]{:S(2)}) collective-permute-start(bf16[272,512]{1,0:T(8,128)(2,1)S(1)} %select_select_fusion.refs_3_), channel_id=1, source_target_pairs={{0,8},{1,25},{2,10},{3,27},{4,12},{5,29},{6,14},{7,31},{8,16},{9,1... | collective-permute-start | bytes 835592 | tf_op jit(solution)/shard_map/ppermute | solution.py:56
  48.6 10.4 %copy-start.3 = (s32[16,2]{0,1:T(2,128)S(1)}, s32[16,2]{0,1:T(2,128)}, u32[]{:S(2)}) copy-start(s32[16,2]{0,1:T(2,128)} %param.11) | copy-start | bytes 388
  55.1 1.8 %collective-permute-start.12 = (f32[3,8,512]{2,1,0:T(8,128)S(1)}, f32[3,8,512]{2,1,0:T(8,128)S(1)}, u32[]{:S(2)}, u32[]{:S(2)}) collective-permute-start(f32[3,8,512]{2,1,0:T(8,128)S(1)} %get-tuple-element.31), channel_id=1, source_target_pairs={{0,1},{1,0},{2,3},{3,2},{4,5},{5,4},{6,7},{7,6},{8,9},{9,8},{10,11... | collective-permute-start | bytes 147464 | tf_op jit(solution)/shard_map/ppermute | solution.py:280
  56.9 3.4 %collective-permute-start.14 = (f32[3,8,512]{2,1,0:T(8,128)S(1)}, f32[3,8,512]{2,1,0:T(8,128)S(1)}, u32[]{:S(2)}, u32[]{:S(2)}) collective-permute-start(f32[3,8,512]{2,1,0:T(8,128)S(1)} %add.64), channel_id=1, source_target_pairs={{0,2},{1,7},{2,4},{3,1},{4,6},{5,3},{6,0},{7,5},{8,10},{9,15},{10,... | collective-permute-start | bytes 147464 | tf_op jit(solution)/shard_map/ppermute | solution.py:282
  59.0 4.7 %collective-permute-start.13 = (f32[3,8,512]{2,1,0:T(8,128)S(1)}, f32[3,8,512]{2,1,0:T(8,128)S(1)}, u32[]{:S(2)}, u32[]{:S(2)}) collective-permute-start(f32[3,8,512]{2,1,0:T(8,128)S(1)} %add.64), channel_id=1, source_target_pairs={{0,4},{1,5},{2,6},{3,7},{4,0},{5,1},{6,2},{7,3},{8,12},{9,13},{10,... | collective-permute-start | bytes 147464 | tf_op jit(solution)/shard_map/ppermute | solution.py:281
  60.2 3.6 %collective-permute-start.15 = (f32[3,8,512]{2,1,0:T(8,128)S(1)}, f32[3,8,512]{2,1,0:T(8,128)S(1)}, u32[]{:S(2)}, u32[]{:S(2)}) collective-permute-start(f32[3,8,512]{2,1,0:T(8,128)S(1)} %collective-permute-done.14), channel_id=1, source_target_pairs={{0,1},{1,0},{2,3},{3,2},{4,5},{5,4},{6,7},{7,6},{8,9},{9,8},{10,11... | collective-permute-start | bytes 147464 | tf_op jit(solution)/shard_map/ppermute | solution.py:283
